TPU v7x, 32 devices: a whole 2x2x4 slice. The times are simulated.
32 devices in a mesh: dp: 8 (over z, x), seq: 4 (over y, core).
Axes of the slice: x: 2, y: 2, z: 4, core: 2. Of those that a mesh axis runs over, the one named last changes fastest.
Arguments:
- tokens: bfloat16 [32, 1024, 768], P('dp', 'seq'), may hold values from -6 to 6
- doc_lengths: int32 [32, 24], P('dp'), may hold values from 1 to 1001, as said below
- teacher: bfloat16 [32, 12, 1024, 1024], P('dp', None, 'seq'), may hold values from 0.099609375 to 10
- cotangent: bfloat16 [32, 1024, 768], P('dp', 'seq'), may hold values from -6 to 6
- joint_weight: float32 [768, 2304], P(('dp', 'seq')), may hold values from -0.21650635 to 0.21650635
- output_weight: float32 [768, 768], P(('dp', 'seq')), may hold values from -0.4375 to 0.4375
- expand_weight: float32 [768, 3072], P(('dp', 'seq')), may hold values from -0.21650635 to 0.21650635
- shrink_weight: float32 [3072, 768], P(('dp', 'seq')), may hold values from -0.109375 to 0.109375
- vectors: float32 [12, 768], P(None, ('dp', 'seq')), may hold values from -2 to 3
- joint_mean: float32 [768, 2304], P(('dp', 'seq')), may hold values from -0.00061035156 to 0.00061035156
- output_mean: float32 [768, 768], P(('dp', 'seq')), may hold values from -0.00061035156 to 0.00061035156
- expand_mean: float32 [768, 3072], P(('dp', 'seq')), may hold values from -0.00061035156 to 0.00061035156
- shrink_mean: float32 [3072, 768], P(('dp', 'seq')), may hold values from -0.00061035156 to 0.00061035156
- vector_mean: float32 [12, 768], P(None, ('dp', 'seq')), may hold values from -0.00061035156 to 0.00061035156
- joint_square: float32 [768, 2304], P(('dp', 'seq')), may hold values from 1.4110135e-10 to 5.644054e-10
- output_square: float32 [768, 768], P(('dp', 'seq')), may hold values from 1.4110135e-10 to 5.644054e-10
- expand_square: float32 [768, 3072], P(('dp', 'seq')), may hold values from 1.4110135e-10 to 5.644054e-10
- shrink_square: float32 [3072, 768], P(('dp', 'seq')), may hold values from 1.4110135e-10 to 5.644054e-10
- vector_square: float32 [12, 768], P(None, ('dp', 'seq')), may hold values from 1.4110135e-10 to 5.644054e-10
Outputs:
- layer_output: bfloat16 [32, 1024, 768], P('dp', 'seq')
- token_gradient: float32 [32, 1024, 768], P('dp', 'seq')
- gradient_norm: float32 [], replicated
- joint_master: float32 [768, 2304], P(('dp', 'seq'))
- output_master: float32 [768, 768], P(('dp', 'seq'))
- expand_master: float32 [768, 3072], P(('dp', 'seq'))
- shrink_master: float32 [3072, 768], P(('dp', 'seq'))
- vector_master: float32 [12, 768], P(None, ('dp', 'seq'))
- joint_momentum: float32 [768, 2304], P(('dp', 'seq'))
- output_momentum: float32 [768, 768], P(('dp', 'seq'))
- expand_momentum: float32 [768, 3072], P(('dp', 'seq'))
- shrink_momentum: float32 [3072, 768], P(('dp', 'seq'))
- vector_momentum: float32 [12, 768], P(None, ('dp', 'seq'))
- joint_variance: float32 [768, 2304], P(('dp', 'seq'))
- output_variance: float32 [768, 768], P(('dp', 'seq'))
- expand_variance: float32 [768, 3072], P(('dp', 'seq'))
- shrink_variance: float32 [3072, 768], P(('dp', 'seq'))
- vector_variance: float32 [12, 768], P(None, ('dp', 'seq'))
Inputs may be any that keep to these rules, and one draw needn't show every extreme that they name: `doc_lengths`: each row's 24 lengths sum to 1024.
All inputs are finite; a program needn't handle non-finite values.
Results may differ from a plain program's by a relative error of at most 0.0083.
Values may be sent and summed in bfloat16 or wider, within the bound.
No kernel may reach another device: no remote copies, remote signals or barrier semaphores. Data moves between devices by JAX's collectives and lax.ppermute only.
A program may use at most 320 MiB of HBM per device.

v0:
```python
import jax
import jax.numpy as jnp
from jax import lax
from jax.sharding import PartitionSpec as P

HEADS = 12
STEP = 10


NORM_EPS = 1e-05
MASK_FILL = -1e30
DISTILL = 0.5
CLIP_LEVEL = 1.0
BETA_ONE = 0.9
BETA_TWO = 0.999
ADAM_EPS = 1e-08
DECAY = 0.01
RATE_MATRIX = 0.05
RATE_VECTOR = 0.5


def passed_along(block, axis, distance):
    devices = range(lax.axis_size(axis))
    route = [((i - distance) % len(devices), i) for i in devices]
    return lax.ppermute(block, axis, route)


def shortened(x):

    def short(part):
        return part.astype(jnp.bfloat16) if part.dtype == jnp.float32 else part

    return jax.tree.map(short, x)


def segment_ids(doc_lengths, total):
    doc_ends = jnp.cumsum(doc_lengths, axis=-1, dtype=jnp.int32)
    places = jnp.arange(total, dtype=jnp.int32)
    return jnp.sum(
        (doc_ends[:, None, :] <= places[None, :, None]).astype(jnp.int32), axis=-1, dtype=jnp.int32
    )


def norm_forward(values, norm_gain, norm_shift):
    center = jnp.mean(values, axis=-1, keepdims=True)
    spread = jnp.mean(jnp.square(values - center), axis=-1, keepdims=True)
    inverse = lax.rsqrt(spread + NORM_EPS)
    normed = (values - center) * inverse
    return (normed * norm_gain + norm_shift, normed, inverse)


def norm_backward(upstream, normed, inverse, norm_gain):
    scaled = upstream * norm_gain
    inner_mean = jnp.mean(scaled, axis=-1, keepdims=True)
    cross_mean = jnp.mean(scaled * normed, axis=-1, keepdims=True)
    return (
        inverse * (scaled - inner_mean - normed * cross_mean),
        jnp.sum(upstream * normed, axis=0),
        jnp.sum(upstream, axis=0),
    )


def adam_step(gradient, master, mean_old, square_old, rate, decay):
    momentum = BETA_ONE * mean_old + (1.0 - BETA_ONE) * gradient
    variance = BETA_TWO * square_old + (1.0 - BETA_TWO) * gradient * gradient
    update = (
        momentum / (1.0 - BETA_ONE**STEP) / (jnp.sqrt(variance / (1.0 - BETA_TWO**STEP)) + ADAM_EPS)
    )
    return (master - rate * (update + decay * master), momentum, variance)


def local(
    tokens,
    doc_lengths,
    teacher,
    cotangent,
    joint_weight,
    output_weight,
    expand_weight,
    shrink_weight,
    vectors,
    joint_mean,
    output_mean,
    expand_mean,
    shrink_mean,
    vector_mean,
    joint_square,
    output_square,
    expand_square,
    shrink_square,
    vector_square,
):
    seq_count = lax.axis_size("seq")
    seq_rank = lax.axis_index("seq")
    row_count, local_len, width = tokens.shape
    full_len = local_len * seq_count
    head_dim = width // HEADS
    score_scale = head_dim ** (-0.5)
    token_total = row_count * local_len
    joint_w, output_w, expand_w, shrink_w, vector_w = (
        lax.all_gather(joint_weight.astype(jnp.bfloat16), ("dp", "seq"), axis=0, tiled=True),
        lax.all_gather(output_weight.astype(jnp.bfloat16), ("dp", "seq"), axis=0, tiled=True),
        lax.all_gather(expand_weight.astype(jnp.bfloat16), ("dp", "seq"), axis=0, tiled=True),
        lax.all_gather(shrink_weight.astype(jnp.bfloat16), ("dp", "seq"), axis=0, tiled=True),
        lax.all_gather(vectors.astype(jnp.bfloat16), ("dp", "seq"), axis=1, tiled=True),
    )
    hidden_width = expand_w.shape[1]
    spare = hidden_width // width
    vector_f = vector_w.astype(jnp.float32)
    bias_query = vector_f[0]
    bias_value = vector_f[1]
    bias_out = vector_f[2]
    bias_expand = vector_f[3 : 3 + spare].reshape(hidden_width)
    bias_shrink = vector_f[3 + spare]
    gain_one = vector_f[4 + spare]
    shift_one = vector_f[5 + spare]
    gain_two = vector_f[6 + spare]
    shift_two = vector_f[7 + spare]
    flat_tokens = tokens.reshape(token_total, width)
    joint_bias = jnp.concatenate([bias_query, jnp.zeros((width,), jnp.float32), bias_value])
    joint_act = (
        jnp.dot(flat_tokens, joint_w, preferred_element_type=jnp.float32) + joint_bias
    ).astype(jnp.bfloat16)
    queries = joint_act[:, :width].reshape(row_count, local_len, HEADS, head_dim)
    keys_own = joint_act[:, width : 2 * width].reshape(row_count, local_len, HEADS, head_dim)
    values_own = joint_act[:, 2 * width :].reshape(row_count, local_len, HEADS, head_dim)
    segments = segment_ids(doc_lengths, full_len)
    query_segments = lax.dynamic_slice_in_dim(segments, seq_rank * local_len, local_len, 1)

    def block_mask(source):
        key_segments = lax.dynamic_slice_in_dim(segments, source * local_len, local_len, 1)
        return (query_segments[:, :, None] == key_segments[:, None, :])[:, None]

    def block_scores(key_block, pair_mask):
        raw_scores = (
            jnp.einsum("rqhd,rkhd->rhqk", queries, key_block, preferred_element_type=jnp.float32)
            * score_scale
        )
        return jnp.where(pair_mask, raw_scores, MASK_FILL)

    running_max = jnp.full((row_count, HEADS, local_len), MASK_FILL, jnp.float32)
    running_sum = jnp.zeros((row_count, HEADS, local_len), jnp.float32)
    moving_keys = keys_own
    for cycle_step in range(seq_count):
        source = (seq_rank - cycle_step) % seq_count
        pair_mask = block_mask(source)
        scores = block_scores(moving_keys, pair_mask)
        new_max = jnp.maximum(running_max, jnp.max(scores, axis=-1))
        block_sum = jnp.sum(
            jnp.where(pair_mask, jnp.exp(scores - new_max[..., None]), 0.0), axis=-1
        )
        running_sum = running_sum * jnp.exp(running_max - new_max) + block_sum
        running_max = new_max
        if cycle_step + 1 < seq_count:
            moving_keys = passed_along(moving_keys, "seq", 1)
    log_total = running_max + jnp.log(running_sum)
    attended = jnp.zeros((row_count, local_len, HEADS, head_dim), jnp.float32)
    keys_now, values_now = (keys_own, values_own)
    for cycle_step in range(seq_count):
        source = (seq_rank - cycle_step) % seq_count
        pair_mask = block_mask(source)
        scores = block_scores(keys_now, pair_mask)
        attention = jnp.where(pair_mask, jnp.exp(scores - log_total[..., None]), 0.0)
        attended = attended + jnp.einsum(
            "rhqk,rkhd->rqhd",
            attention.astype(jnp.bfloat16),
            values_now,
            preferred_element_type=jnp.float32,
        )
        if cycle_step + 1 < seq_count:
            keys_now, values_now = passed_along((keys_now, values_now), "seq", 1)
    attended_low = attended.reshape(token_total, width).astype(jnp.bfloat16)
    branch = jnp.dot(attended_low, output_w, preferred_element_type=jnp.float32) + bias_out
    hidden_one, normed_one, inverse_one = norm_forward(
        flat_tokens.astype(jnp.float32) + branch, gain_one, shift_one
    )
    hidden_low = hidden_one.astype(jnp.bfloat16)
    expanded = jnp.dot(hidden_low, expand_w, preferred_element_type=jnp.float32) + bias_expand
    activated, gelu_back = jax.vjp(
        lambda pre_act: jax.nn.gelu(pre_act, approximate=False), expanded
    )
    active_low = activated.astype(jnp.bfloat16)
    shrunk = jnp.dot(active_low, shrink_w, preferred_element_type=jnp.float32) + bias_shrink
    result, normed_two, inverse_two = norm_forward(hidden_one + shrunk, gain_two, shift_two)
    layer_output = result.astype(jnp.bfloat16).reshape(row_count, local_len, width)
    upstream = cotangent.reshape(token_total, width).astype(jnp.float32)
    d_second, grad_gain_two, grad_shift_two = norm_backward(
        upstream, normed_two, inverse_two, gain_two
    )
    shrink_low = d_second.astype(jnp.bfloat16)
    grad_bias_shrink = jnp.sum(shrink_low.astype(jnp.float32), axis=0)
    grad_shrink = jnp.einsum(
        "nf,nd->fd", active_low, shrink_low, preferred_element_type=jnp.float32
    )
    d_active = jnp.einsum("nd,fd->nf", shrink_low, shrink_w, preferred_element_type=jnp.float32)
    (d_expanded,) = gelu_back(d_active)
    expand_low = d_expanded.astype(jnp.bfloat16)
    grad_bias_expand = jnp.sum(expand_low.astype(jnp.float32), axis=0)
    grad_expand = jnp.einsum(
        "nd,nf->df", hidden_low, expand_low, preferred_element_type=jnp.float32
    )
    d_hidden = d_second + jnp.einsum(
        "nf,df->nd", expand_low, expand_w, preferred_element_type=jnp.float32
    )
    d_first, grad_gain_one, grad_shift_one = norm_backward(
        d_hidden, normed_one, inverse_one, gain_one
    )
    branch_low = d_first.astype(jnp.bfloat16)
    grad_bias_out = jnp.sum(branch_low.astype(jnp.float32), axis=0)
    grad_output = jnp.einsum(
        "nd,ne->de", attended_low, branch_low, preferred_element_type=jnp.float32
    )
    d_attended = (
        jnp.einsum("ne,de->nd", branch_low, output_w, preferred_element_type=jnp.float32)
        .astype(jnp.bfloat16)
        .reshape(row_count, local_len, HEADS, head_dim)
    )
    row_dot = jnp.einsum("rqhd,rqhd->rhq", d_attended.astype(jnp.float32), attended)
    full_mask = (query_segments[:, :, None] == segments[:, None, :])[:, None]
    teacher_total = jnp.sum(jnp.where(full_mask, teacher.astype(jnp.float32), 0.0), axis=-1)
    grad_query = jnp.zeros((row_count, local_len, HEADS, head_dim), jnp.float32)
    key_carry = jnp.zeros((row_count, local_len, HEADS, head_dim), jnp.float32)
    value_carry = jnp.zeros((row_count, local_len, HEADS, head_dim), jnp.float32)
    keys_now, values_now = (keys_own, values_own)
    for cycle_step in range(seq_count):
        source = (seq_rank - cycle_step) % seq_count
        pair_mask = block_mask(source)
        scores = block_scores(keys_now, pair_mask)
        attention = jnp.where(pair_mask, jnp.exp(scores - log_total[..., None]), 0.0)
        attention_low = attention.astype(jnp.bfloat16)
        value_here = jnp.einsum(
            "rhqk,rqhd->rkhd", attention_low, d_attended, preferred_element_type=jnp.float32
        )
        grad_attention = jnp.einsum(
            "rqhd,rkhd->rhqk", d_attended, values_now, preferred_element_type=jnp.float32
        )
        teach_block = lax.dynamic_slice_in_dim(teacher, source * local_len, local_len, 3).astype(
            jnp.float32
        )
        target = jnp.where(pair_mask, teach_block / teacher_total[..., None], 0.0)
        grad_scores = attention * (grad_attention - row_dot[..., None]) + DISTILL * (
            attention - target
        )
        scores_low = grad_scores.astype(jnp.bfloat16)
        grad_query = (
            grad_query
            + jnp.einsum(
                "rhqk,rkhd->rqhd", scores_low, keys_now, preferred_element_type=jnp.float32
            )
            * score_scale
        )
        key_here = (
            jnp.einsum("rhqk,rqhd->rkhd", scores_low, queries, preferred_element_type=jnp.float32)
            * score_scale
        )
        key_carry, value_carry = (
            passed_along(shortened(key_carry + key_here), "seq", 1),
            passed_along((value_carry + value_here).astype(jnp.bfloat16), "seq", 1).astype(
                jnp.float32
            ),
        )
        if cycle_step + 1 < seq_count:
            keys_now, values_now = passed_along((keys_now, values_now), "seq", 1)
    grad_keys, grad_values = (key_carry, value_carry)
    query_low = grad_query.reshape(token_total, width).astype(jnp.bfloat16)
    key_low = grad_keys.reshape(token_total, width).astype(jnp.bfloat16)
    value_low = grad_values.reshape(token_total, width).astype(jnp.bfloat16)
    joint_low = jnp.concatenate([query_low, key_low, value_low], axis=-1)
    grad_bias_query = jnp.sum(query_low.astype(jnp.float32), axis=0)
    grad_bias_value = jnp.sum(value_low.astype(jnp.float32), axis=0)
    grad_joint = jnp.einsum("nd,ne->de", flat_tokens, joint_low, preferred_element_type=jnp.float32)
    token_gradient = (
        d_first + jnp.einsum("ne,de->nd", joint_low, joint_w, preferred_element_type=jnp.float32)
    ).reshape(row_count, local_len, width)
    grad_vector = jnp.concatenate(
        [
            jnp.stack([grad_bias_query, grad_bias_value, grad_bias_out]),
            grad_bias_expand.reshape(spare, width),
            jnp.stack(
                [grad_bias_shrink, grad_gain_one, grad_shift_one, grad_gain_two, grad_shift_two]
            ),
        ],
        axis=0,
    )
    shard_joint, shard_output, shard_expand, shard_shrink, shard_vector = (
        lax.psum_scatter(grad_joint, ("dp", "seq"), scatter_dimension=0, tiled=True),
        lax.psum_scatter(grad_output, ("dp", "seq"), scatter_dimension=0, tiled=True),
        lax.psum_scatter(grad_expand, ("dp", "seq"), scatter_dimension=0, tiled=True),
        lax.psum_scatter(grad_shrink, ("dp", "seq"), scatter_dimension=0, tiled=True),
        lax.psum_scatter(grad_vector, ("dp", "seq"), scatter_dimension=1, tiled=True),
    )
    local_squares = (
        jnp.sum(shard_joint * shard_joint)
        + jnp.sum(shard_output * shard_output)
        + jnp.sum(shard_expand * shard_expand)
        + jnp.sum(shard_shrink * shard_shrink)
        + jnp.sum(shard_vector * shard_vector)
    )
    square_total = lax.psum(local_squares, ("dp", "seq"))
    gradient_norm = jnp.sqrt(square_total)
    clip_scale = CLIP_LEVEL / (gradient_norm + 1e-06)
    joint_master, joint_momentum, joint_variance = adam_step(
        shard_joint * clip_scale, joint_weight, joint_mean, joint_square, RATE_MATRIX, DECAY
    )
    output_master, output_momentum, output_variance = adam_step(
        shard_output * clip_scale, output_weight, output_mean, output_square, RATE_MATRIX, DECAY
    )
    expand_master, expand_momentum, expand_variance = adam_step(
        shard_expand * clip_scale, expand_weight, expand_mean, expand_square, RATE_MATRIX, DECAY
    )
    shrink_master, shrink_momentum, shrink_variance = adam_step(
        shard_shrink * clip_scale, shrink_weight, shrink_mean, shrink_square, RATE_MATRIX, DECAY
    )
    vector_master, vector_momentum, vector_variance = adam_step(
        shard_vector * clip_scale, vectors, vector_mean, vector_square, RATE_VECTOR, 0.0
    )
    return (
        layer_output,
        token_gradient,
        gradient_norm,
        joint_master,
        output_master,
        expand_master,
        shrink_master,
        vector_master,
        joint_momentum,
        output_momentum,
        expand_momentum,
        shrink_momentum,
        vector_momentum,
        joint_variance,
        output_variance,
        expand_variance,
        shrink_variance,
        vector_variance,
    )


def solution(mesh):
    return jax.shard_map(
        local,
        mesh=mesh,
        in_specs=(
            P("dp", "seq", None),
            P("dp", None),
            P("dp", None, "seq", None),
            P("dp", "seq", None),
            P(("dp", "seq"), None),
            P(("dp", "seq"), None),
            P(("dp", "seq"), None),
            P(("dp", "seq"), None),
            P(None, ("dp", "seq")),
            P(("dp", "seq"), None),
            P(("dp", "seq"), None),
            P(("dp", "seq"), None),
            P(("dp", "seq"), None),
            P(None, ("dp", "seq")),
            P(("dp", "seq"), None),
            P(("dp", "seq"), None),
            P(("dp", "seq"), None),
            P(("dp", "seq"), None),
            P(None, ("dp", "seq")),
        ),
        out_specs=(
            P("dp", "seq", None),
            P("dp", "seq", None),
            P(),
            P(("dp", "seq"), None),
            P(("dp", "seq"), None),
            P(("dp", "seq"), None),
            P(("dp", "seq"), None),
            P(None, ("dp", "seq")),
            P(("dp", "seq"), None),
            P(("dp", "seq"), None),
            P(("dp", "seq"), None),
            P(("dp", "seq"), None),
            P(None, ("dp", "seq")),
            P(("dp", "seq"), None),
            P(("dp", "seq"), None),
            P(("dp", "seq"), None),
            P(("dp", "seq"), None),
            P(None, ("dp", "seq")),
        ),
        check_vma=False,
    )
```

profile of v0, /device:TPU:0, one launch (start us, length us, event | category | flops | bytes accessed | tf_op | source)
XLA Modules:
  0.0 929.6 jit_solution(8175033701341859208)
XLA Ops:
  12.9 43.6 %all-gather = bf16[32,24,12]{1,2,0:T(8,128)(2,1)S(1)} all-gather(bf16[1,24,12]{1,2,0:T(8,128)(2,1)S(1)} %convert_bitcast_fusion), channel_id=1, replica_groups=mesh['dp'=8,'seq'=4] {'dp','seq'}, dimensions={0}, use_global_device_ids=true | all-gather | bytes 19008 | tf_op jit(solution)/shard_map/all_gather | solution.py:105
  57.6 17.0 %all-gather.6.cloned.1.call-done = bf16[768,2304]{1,0:T(8,128)(2,1)} async-done(((bf16[24,2304]{1,0:T(8,128)(2,1)}), bf16[768,2304]{1,0:T(8,128)(2,1)}) %all-gather.6.cloned.1.call-update) | async-done | bytes 3538960 | tf_op jit(solution)/shard_map/all_gather | solution.py:101
  74.6 6.3 add_convert_fusion.5
  84.5 2.9 reshape.206
  92.1 3.8 reshape.204
  100.1 9.7 %collective-permute-done = bf16[4,256,12,64]{1,3,2,0:T(8,128)(2,1)} collective-permute-done((bf16[4,256,12,64]{1,3,2,0:T(8,128)(2,1)}, bf16[4,256,12,64]{1,3,2,0:T(8,128)(2,1)}, u32[]{:S(2)}, u32[]{:S(2)}) %collective-permute-start) | collective-permute-done | bytes 1572896 | tf_op jit(solution)/shard_map/ppermute | solution.py:25
  112.3 16.4 %collective-permute-done.3 = bf16[4,256,12,64]{1,3,2,0:T(8,128)(2,1)} collective-permute-done((bf16[4,256,12,64]{1,3,2,0:T(8,128)(2,1)}, bf16[4,256,12,64]{1,3,2,0:T(8,128)(2,1)}, u32[]{:S(2)}, u32[]{:S(2)}) %collective-permute-start.3) | collective-permute-done | bytes 1572896 | tf_op jit(solution)/shard_map/ppermute | solution.py:25
  133.5 2.9 reshape.205
  136.4 9.2 collective-permute-done.1
  145.9 6.7 fusion.10
  152.6 8.3 fusion.11
  160.9 4.7 collective-permute-done.4
  165.6 3.7 fusion.12
  169.3 16.1 %collective-permute-done.2 = bf16[4,256,12,64]{1,3,2,0:T(8,128)(2,1)S(1)} collective-permute-done((bf16[4,256,12,64]{1,3,2,0:T(8,128)(2,1)}, bf16[4,256,12,64]{1,3,2,0:T(8,128)(2,1)S(1)}, u32[]{:S(2)}, u32[]{:S(2)}) %collective-permute-start.2) | collective-permute-done | bytes 1572896 | tf_op jit(solution)/shard_map/ppermute | solution.py:25
  188.0 16.2 %select_reduce_fusion.3 = (f32[4,12,256]{2,1,0:T(8,128)S(1)}, f32[4,12,256]{2,1,0:T(8,128)S(1)}) fusion(f32[4,12,256,256]{2,3,1,0:T(8,128)} %get-tuple-element.153, f32[4,12,256]{2,1,0:T(8,128)S(1)} %get-tuple-element.129, pred[4,256,256]{1,2,0:T(8,128)(4,1)S(1)} %copy-done.23, f32[4,12,256]{2,1,0:T(8,128)S(1)} %get-tuple-element.138, ...), kind=kLoop, calls=%fused_computation.28 | loop fusion | flops 31432704 | bytes 25886720 | tf_op jit(solution)/shard_map/reduce_sum | solution.py:149
  204.2 7.3 select_reduce_fusion.1
  211.7 9.9 %fusion.80 = f32[4,12,64,256]{3,2,1,0:T(8,128)} fusion(bf16[4,256,12,64]{1,3,2,0:T(8,128)(2,1)} %collective-permute-done.3, f32[4,12,256,256]{2,3,1,0:T(8,128)} %get-tuple-element.153, f32[4,12,256]{2,1,0:T(8,128)S(1)} %log_add_fusion, pred[4,256,256]{1,2,0:T(8,128)(4,1)S(1)} %copy-done.23), kind=kOutput, calls=%fused_computation.201 | convolution fusion | flops 418381824 | bytes 17612800 | tf_op jit(solution)/shard_map/rhqk,rkhd->rqhd/dot_general | solution.py:164
  221.6 9.9 %fusion.77 = f32[4,12,64,256]{3,2,1,0:T(8,128)} fusion(bf16[4,256,12,64]{1,3,2,0:T(8,128)(2,1)} %collective-permute-done.4, f32[4,12,256,256]{2,3,1,0:T(8,128)} %copy-done.3, f32[4,12,256]{2,1,0:T(8,128)S(1)} %log_add_fusion, pred[4,256,256]{1,2,0:T(8,128)(4,1)S(1)} %copy-done.22), kind=kOutput, calls=%fused_computation.200 | convolution fusion | flops 418381824 | bytes 17612800 | tf_op jit(solution)/shard_map/rhqk,rkhd->rqhd/dot_general | solution.py:164
  231.5 9.3 %fusion.69 = f32[4,12,64,256]{3,2,1,0:T(8,128)} fusion(bf16[4,256,12,64]{1,0,3,2:T(4,128)(2,1)S(1)} %copy-done.15, f32[4,12,256,256]{2,3,1,0:T(8,128)} %get-tuple-element.155, f32[4,12,256]{2,1,0:T(8,128)S(1)} %log_add_fusion, pred[4,256,256]{1,2,0:T(8,128)(4,1)S(1)} %copy-done.36), kind=kOutput, calls=%fused_computation.195 | convolution fusion | flops 418381824 | bytes 17612800 | tf_op jit(solution)/shard_map/rhqk,rkhd->rqhd/dot_general | solution.py:164
  240.9 7.8 bitcast_convert_fusion
  251.5 3.9 fusion.98
  255.9 35.9 %multiply_convert_fusion = (bf16[1024,3072]{1,0:T(8,128)(2,1)}, f32[1024,3072]{1,0:T(8,128)}, f32[1024,3072]{1,0:T(8,128)}) fusion(f32[3072]{0:T(1024)S(1)} %add.363, bf16[768,3072]{1,0:T(8,128)(2,1)} %all-gather.10.cloned.1.call-done, f32[1024,768]{1,0:T(8,128)S(1)} %get-tuple-element.159, f32[768]{0:T(1024)S(1)} %get-tuple-element.101, ...), kind=kOutput, calls=%fused_computation.9 | convolution fusion | flops 5043388416 | bytes 39348224 | tf_op jit(solution)/shard_map/dot_general | solution.py:178
  291.8 8.9 fusion.99
  303.1 3.9 convert_reduce_fusion.2
  307.0 19.3 %convert_reduce_fusion = (f32[3072]{0:T(1024)}, bf16[1024,3072]{1,0:T(8,128)(2,1)}) fusion(f32[1024,3072]{1,0:T(8,128)} %get-tuple-element.126, bf16[3072,768]{1,0:T(8,128)(2,1)} %all-gather.12.cloned.1.call-done, f32[1024,768]{1,0:T(8,128)} %get-tuple-element.122, f32[1024,3072]{1,0:T(8,128)} %get-tuple-element.160, f32[3072]{0:T(1024)S(1)} %add.363), kind=kOutput, calls=%fused_computation.3 | convolution fusion | flops 4886098944 | bytes 39346176 | tf_op jit(solution)/shard_map/nd,fd->nf/dot_general | solution.py:195
  326.3 10.6 %multiply_reduce_fusion = (f32[768]{0:T(1024)}, f32[1024]{0:T(1024)S(1)}, f32[1024]{0:T(1024)S(1)}, f32[768]{0:T(1024)}, f32[1024,768]{1,0:T(8,128)S(1)}) fusion(f32[1024,768]{1,0:T(8,128)S(1)} %get-tuple-element.159, f32[1024]{0:T(1024)S(1)} %add_rsqrt_fusion.1, f32[1024]{0:T(1024)S(1)} %broadcast_multiply_fusion.4, f32[768]{0:T(1024)S(1)} %get-tuple-element.102, ...), kind=kOutput, calls=%fused_computation.71 | convolution fusion | flops 4839698432 | bytes 20472832 | tf_op jit(solution)/shard_map/nf,df->nd/dot_general | solution.py:202
  340.2 2.8 fusion.61
  343.1 10.6 %fusion.84 = f32[768,3072]{1,0:T(8,128)} fusion(bf16[1024,3072]{1,0:T(8,128)(2,1)} %get-tuple-element.167, f32[1024,768]{1,0:T(8,128)S(1)} %get-tuple-element.159, f32[768]{0:T(1024)S(1)} %get-tuple-element.101, f32[768]{0:T(1024)S(1)} %get-tuple-element.102, f32[1024]{0:T(1024)S(1)} %add_rsqrt_fusion.1, f32[1024]{0:T(1024)S(1)} %broadcast_multiply_fusion.4), kind=kOutput, calls=%fused_computation.202 | convolution fusion | flops 4835770368 | bytes 18888704 | tf_op jit(solution)/shard_map/nd,nf->df/dot_general | solution.py:199
  353.8 19.4 %constant_dynamic-slice_fusion.2 = (bf16[4,12,256,256]{3,2,1,0:T(8,128)(2,1)}, bf16[4,12,256,256]{3,2,1,0:T(8,128)(2,1)}, bf16[4,12,256,256]{3,2,1,0:T(8,128)(2,1)}, bf16[4,12,256,256]{3,2,1,0:T(8,128)(2,1)}) fusion(bf16[4,12,256,1024]{3,2,1,0:T(8,128)(2,1)} %param.21, s32[]{:T(128)S(6)} %select_n.132, s32[]{:T(128)S(6)} %select_n.135, s32[]{:T(128)S(6)} %select_n.129, ...), kind=kLoop, calls=%fused_computation.175 | loop fusion | bytes 50331664 | tf_op jit(solution)/shard_map/dynamic_slice | solution.py:237
  373.2 8.7 copy.364
  382.0 8.6 copy.363
  390.6 8.7 copy.365
  399.3 8.6 copy.366
  408.6 12.4 %select_reduce_fusion = f32[4,12,256]{2,1,0:T(8,128)S(1)} fusion(bf16[4,12,256,1024]{3,2,1,0:T(8,128)(2,1)} %param.21, pred[4,256,1024]{2,1,0:T(8,128)(4,1)S(1)} %broadcast_compare_fusion), kind=kLoop, calls=%fused_computation | loop fusion | flops 37736448 | bytes 26263552 | tf_op jit(solution)/shard_map/reduce_sum | solution.py:220
  424.5 9.5 %fusion.29 = bf16[4,256,12,64]{1,3,2,0:T(8,128)(2,1)} fusion(bf16[4,256,12,64]{1,0,3,2:T(4,128)(2,1)S(1)} %reshape.208, f32[4,12,256,256]{2,3,1,0:T(8,128)} %get-tuple-element.155, f32[4,12,256]{2,1,0:T(8,128)S(1)} %copy-done.48, pred[4,256,256]{1,2,0:T(8,128)(4,1)S(1)} %copy-done.37), kind=kOutput, calls=%fused_computation.97 | convolution fusion | flops 419168256 | bytes 16039936 | tf_op jit(solution)/shard_map/rhqk,rqhd->rkhd/dot_general | solution.py:231
  437.5 10.6 %add_convert_fusion.3 = bf16[4,12,256,256]{2,3,1,0:T(8,128)(2,1)S(1)} fusion(bf16[4,12,256,256]{2,3,1,0:T(8,128)(2,1)} %copy.363, f32[4,12,256,256]{2,3,1,0:T(8,128)} %get-tuple-element.155, f32[4,12,256]{2,1,0:T(8,128)S(1)} %select_reduce_fusion, f32[4,12,256]{2,1,0:T(8,128)S(1)} %fusion.20, f32[4,12,256]{2,1,0:T(8,128)S(1)} %copy-done.48, ...), kind=kOutput, calls=%fused_computation.7 | convolution fusion | flops 443547648 | bytes 28721152 | tf_op jit(solution)/shard_map/rqhd,rkhd->rhqk/dot_general | solution.py:234
  448.1 3.2 fusion.30
  454.2 10.5 %fusion.64 = f32[3072,768]{1,0:T(8,128)} fusion(bf16[1024,3072]{1,0:T(8,128)(2,1)} %get-tuple-element.125, f32[1024,768]{1,0:T(8,128)S(1)} %copy-done.26), kind=kOutput, calls=%fused_computation.190 | convolution fusion | flops 4832624640 | bytes 18874368 | tf_op jit(solution)/shard_map/nf,nd->fd/dot_general | solution.py:192
  465.6 16.7 %add_convert_fusion.2 = bf16[4,12,256,256]{2,3,1,0:T(8,128)(2,1)} fusion(bf16[4,12,256,256]{2,3,1,0:T(8,128)(2,1)} %copy.364, f32[4,12,256,256]{2,3,1,0:T(8,128)} %get-tuple-element.153, f32[4,12,256]{2,1,0:T(8,128)S(1)} %select_reduce_fusion, f32[4,12,256]{2,1,0:T(8,128)} %copy-done.56, f32[4,12,256]{2,1,0:T(8,128)S(1)} %copy-done.48, ...), kind=kOutput, calls=%fused_computation.6 | convolution fusion | flops 443547648 | bytes 28721152 | tf_op jit(solution)/shard_map/rqhd,rkhd->rhqk/dot_general | solution.py:234
  482.4 16.2 %add_convert_fusion.1 = bf16[4,12,256,256]{2,3,1,0:T(8,128)(2,1)} fusion(bf16[4,12,256,256]{2,3,1,0:T(8,128)(2,1)} %copy.365, f32[4,12,256,256]{2,3,1,0:T(8,128)} %copy-done.3, f32[4,12,256]{2,1,0:T(8,128)S(1)} %select_reduce_fusion, f32[4,12,256]{2,1,0:T(8,128)S(1)} %copy-done.57, f32[4,12,256]{2,1,0:T(8,128)S(1)} %copy-done.48, ...), kind=kOutput, calls=%fused_computation.5 | convolution fusion | flops 443547648 | bytes 28721152 | tf_op jit(solution)/shard_map/rqhd,rkhd->rhqk/dot_general | solution.py:234
  498.6 13.0 %add_convert_fusion = bf16[4,12,256,256]{2,3,1,0:T(8,128)(2,1)} fusion(bf16[4,12,256,256]{2,3,1,0:T(8,128)(2,1)} %copy.366, f32[4,12,256,256]{2,3,1,0:T(8,128)S(1)} %bitcast.140, f32[4,12,256]{2,1,0:T(8,128)S(1)} %select_reduce_fusion, f32[4,12,256]{2,1,0:T(8,128)S(1)} %copy-done.57, f32[4,12,256]{2,1,0:T(8,128)S(1)} %copy-done.48, ...), kind=kOutput, calls=%fused_computation.4 | convolution fusion | flops 443547648 | bytes 28721152 | tf_op jit(solution)/shard_map/rqhd,rkhd->rhqk/dot_general | solution.py:234
  511.7 5.6 fusion.71
  517.3 9.6 %fusion.16 = bf16[4,256,12,64]{1,3,2,0:T(8,128)(2,1)} fusion(bf16[4,256,12,64]{1,3,2,0:T(8,128)(2,1)} %collective-permute-done.10, bf16[4,256,12,64]{1,0,3,2:T(4,128)(2,1)S(1)} %copy-done.18, f32[4,12,256,256]{2,3,1,0:T(8,128)} %get-tuple-element.153, f32[4,12,256]{2,1,0:T(8,128)S(1)} %copy-done.48, pred[4,256,256]{1,2,0:T(8,128)(4,1)S(1)} %copy-done.25), kind=kOutput, calls=%fused_computation.50 | convolution fusion | flops 420741120 | bytes 17612800 | tf_op jit(solution)/shard_map/rhqk,rqhd->rkhd/dot_general | solution.py:231
  527.8 6.6 fusion.19
  535.3 6.7 fusion.46
  542.0 9.4 %fusion.36 = f32[4,12,64,256]{3,2,1,0:T(8,128)} fusion(bf16[4,256,12,64]{1,0,3,2:T(4,128)(2,1)S(1)} %copy-done.19, f32[4,12,256,256]{2,3,1,0:T(8,128)} %copy-done.3, f32[4,12,256]{2,1,0:T(8,128)S(1)} %copy-done.48, pred[4,256,256]{1,2,0:T(8,128)(4,1)} %get-tuple-element.146), kind=kOutput, calls=%fused_computation.120 | convolution fusion | flops 418381824 | bytes 17612800 | tf_op jit(solution)/shard_map/rhqk,rqhd->rkhd/dot_general | solution.py:231
  551.5 4.2 fusion.15
  555.8 19.3 %collective-permute-done.7 = bf16[4,256,12,64]{1,3,2,0:T(8,128)(2,1)} collective-permute-done((bf16[4,256,12,64]{1,3,2,0:T(8,128)(2,1)}, bf16[4,256,12,64]{1,3,2,0:T(8,128)(2,1)}, u32[]{:S(2)}, u32[]{:S(2)}) %collective-permute-start.7) | collective-permute-done | bytes 1572896 | tf_op jit(solution)/shard_map/ppermute | solution.py:25
  575.1 3.2 fusion.18
  578.5 3.6 fusion.44
  582.1 4.5 fusion.34
  586.6 7.4 collective-permute-done.12
  594.1 2.9 fusion.14
  597.0 13.9 %collective-permute-done.8 = bf16[4,256,12,64]{1,3,2,0:T(8,128)(2,1)} collective-permute-done((bf16[4,256,12,64]{1,3,2,0:T(8,128)(2,1)}, bf16[4,256,12,64]{1,3,2,0:T(8,128)(2,1)}, u32[]{:S(2)}, u32[]{:S(2)}) %collective-permute-start.8) | collective-permute-done | bytes 1572896 | tf_op jit(solution)/shard_map/ppermute | solution.py:25
  613.2 5.0 fusion.100
  618.2 2.9 fusion.101
  629.2 15.3 %collective-permute-done.9 = bf16[4,256,12,64]{1,3,2,0:T(8,128)(2,1)S(1)} collective-permute-done((bf16[4,256,12,64]{1,3,2,0:T(8,128)(2,1)S(1)}, bf16[4,256,12,64]{1,3,2,0:T(8,128)(2,1)S(1)}, u32[]{:S(2)}, u32[]{:S(2)}) %collective-permute-start.9) | collective-permute-done | bytes 1572896 | tf_op jit(solution)/shard_map/ppermute | solution.py:25
  648.5 5.9 convolution_bitcast_fusion
  654.4 8.0 copy.359
  665.3 39.5 %all-reduce = f32[12,768]{1,0:T(8,128)S(1)} all-reduce(f32[12,768]{1,0:T(8,128)S(1)} %concatenate.11), channel_id=6, replica_groups=mesh['dp'=8,'seq'=4] {'dp','seq'}, use_global_device_ids=true, to_apply=%region_36.37.clone | all-reduce | flops 9216 | bytes 73728
  707.1 27.3 %reduce-scatter.12.cloned.1.call-done = f32[96,768]{1,0:T(8,128)} async-done(((f32[3072,768]{1,0:T(8,128)}), f32[96,768]{1,0:T(8,128)}) %reduce-scatter.12.cloned.1.call-update) | async-done | bytes 294928 | tf_op jit(solution)/shard_map/reduce_scatter | solution.py:289
  736.0 123.3 %reduce-scatter.14.cloned.1.call-done = f32[24,2304]{1,0:T(8,128)} async-done(((f32[768,2304]{1,0:T(8,128)}), f32[24,2304]{1,0:T(8,128)}) %reduce-scatter.14.cloned.1.call-update) | async-done | bytes 221200 | tf_op jit(solution)/shard_map/reduce_scatter | solution.py:286
  864.9 10.0 %convolution_add_fusion.1 = f32[1024,768]{1,0:T(8,128)} fusion(f32[1024,768]{1,0:T(8,128)} %copy-done.28, bf16[1024,2304]{0,1:T(8,128)(2,1)} %copy-done.40, bf16[768,2304]{1,0:T(8,128)(2,1)} %all-gather.6.cloned.1.call-done), kind=kOutput, calls=%fused_computation.93 | convolution fusion | flops 3624665088 | bytes 14548992 | tf_op jit(solution)/shard_map/ne,de->nd/dot_general | solution.py:273
  874.9 40.1 %psum.7 = f32[]{:T(128)} all-reduce(f32[]{:T(128)S(6)} %add.393), channel_id=1, replica_groups=mesh['dp'=8,'seq'=4] {'dp','seq'}, use_global_device_ids=true, to_apply=%region_38.39 | all-reduce | flops 1 | bytes 8 | tf_op jit(solution)/shard_map/psum | solution.py:299
  (290 shorter events, 80.7 us)
Async XLA Ops:
  7.2 67.4 %all-gather.6.cloned.1.call-start = ((), (), s32[]{:S(2)}) async-start(), calls=%async_computation.4 | async-start | bytes 3649536 | tf_op jit(solution)/shard_map/all_gather | solution.py:101
  8.9 242.6 %all-gather.8.cloned.1.call-start = ((), (), s32[]{:S(2)}) async-start(), calls=%async_computation.5 | async-start | bytes 1216512 | tf_op jit(solution)/shard_map/all_gather | solution.py:102
  10.4 245.4 %all-gather.10.cloned.1.call-start = ((), (), s32[]{:S(2)}) async-start(), calls=%async_computation.6 | async-start | bytes 4866048 | tf_op jit(solution)/shard_map/all_gather | solution.py:103
  12.2 279.6 %all-gather.12.cloned.1.call-start = ((), (), s32[]{:S(2)}) async-start(), calls=%async_computation.7 | async-start | bytes 4866048 | tf_op jit(solution)/shard_map/all_gather | solution.py:104
  57.6 53.4 %copy-start.54 = (f32[768]{0:T(1024)}, f32[768]{0:T(1024)S(1)}, u32[]{:S(2)}) copy-start(f32[768]{0:T(1024)S(1)} %get-tuple-element.98) | copy-start | bytes 9220
  87.4 58.6 %copy-start.9 = (bf16[4,256,12,64]{1,0,3,2:T(4,128)(2,1)}, bf16[4,256,12,64]{1,0,3,2:T(4,128)(2,1)S(1)}, u32[]{:S(2)}) copy-start(bf16[4,256,12,64]{1,0,3,2:T(4,128)(2,1)S(1)} %reshape.206) | copy-start | bytes 4718596
  89.1 20.7 %collective-permute-start = (bf16[4,256,12,64]{1,3,2,0:T(8,128)(2,1)}, bf16[4,256,12,64]{1,3,2,0:T(8,128)(2,1)}, u32[]{:S(2)}, u32[]{:S(2)}) collective-permute-start(bf16[4,256,12,64]{1,3,2,0:T(8,128)(2,1)} %copy.282), channel_id=1, source_target_pairs={{3,0},{0,1},{1,2},{2,3},{7,4},{4,5},{5,6},{6,7},{11,8},{8,9},{9,10... | collective-permute-start | bytes 4718600 | tf_op jit(solution)/shard_map/ppermute | solution.py:25
  89.3 20.4 %copy-start.31 = (f32[96,768]{1,0:T(8,128)S(1)}, f32[96,768]{1,0:T(8,128)}, u32[]{:S(2)}) copy-start(f32[96,768]{1,0:T(8,128)} %param.26) | copy-start | bytes 884740
  89.3 21.2 %copy-start.73 = (s32[4,24]{1,0:T(4,128)S(1)}, s32[4,24]{1,0:T(4,128)}, u32[]{:S(2)}) copy-start(s32[4,24]{1,0:T(4,128)} %param.20) | copy-start | bytes 1156
  89.3 21.6 %copy-start.7 = (bf16[4,256,768]{2,1,0:T(8,128)(2,1)S(1)}, bf16[4,256,768]{2,1,0:T(8,128)(2,1)}, u32[]{:S(2)}) copy-start(bf16[4,256,768]{2,1,0:T(8,128)(2,1)} %param.22) | copy-start | bytes 4718596
  98.8 30.0 %collective-permute-start.3 = (bf16[4,256,12,64]{1,3,2,0:T(8,128)(2,1)}, bf16[4,256,12,64]{1,3,2,0:T(8,128)(2,1)}, u32[]{:S(2)}, u32[]{:S(2)}) collective-permute-start(bf16[4,256,12,64]{1,3,2,0:T(8,128)(2,1)} %copy.287), channel_id=1, source_target_pairs={{3,0},{0,1},{1,2},{2,3},{7,4},{4,5},{5,6},{6,7},{11,8},{8,9},{9,10... | collective-permute-start | bytes 4718600 | tf_op jit(solution)/shard_map/ppermute | solution.py:25
  109.8 35.8 %collective-permute-start.1 = (bf16[4,256,12,64]{1,3,2,0:T(8,128)(2,1)}, bf16[4,256,12,64]{1,3,2,0:T(8,128)(2,1)}, u32[]{:S(2)}, u32[]{:S(2)}) collective-permute-start(bf16[4,256,12,64]{1,3,2,0:T(8,128)(2,1)} %collective-permute-done), channel_id=1, source_target_pairs={{3,0},{0,1},{1,2},{2,3},{7,4},{4,5},{5,6},{6,7},{11,8},{8,9},{9,10... | collective-permute-start | bytes 4718600 | tf_op jit(solution)/shard_map/ppermute | solution.py:25
  110.5 552.8 %reduce-scatter.8.cloned.1.call-start = ((), (), s32[]{:S(2)}) async-start(), calls=%async_computation.8 | async-start | bytes 2433024 | tf_op jit(solution)/shard_map/reduce_scatter | solution.py:287
  110.9 17.8 %copy-start.51 = (s32[4,1024]{1,0:T(4,128)}, s32[4,1024]{1,0:T(4,128)S(1)}, u32[]{:S(2)}) copy-start(s32[4,1024]{1,0:T(4,128)S(1)} %convert_reduce_fusion.6) | copy-start | bytes 49156
  128.7 36.9 %collective-permute-start.4 = (bf16[4,256,12,64]{1,3,2,0:T(8,128)(2,1)}, bf16[4,256,12,64]{1,3,2,0:T(8,128)(2,1)}, u32[]{:S(2)}, u32[]{:S(2)}) collective-permute-start(bf16[4,256,12,64]{1,3,2,0:T(8,128)(2,1)} %collective-permute-done.3), channel_id=1, source_target_pairs={{3,0},{0,1},{1,2},{2,3},{7,4},{4,5},{5,6},{6,7},{11,8},{8,9},{9,10... | collective-permute-start | bytes 4718600 | tf_op jit(solution)/shard_map/ppermute | solution.py:25
  128.7 23.9 %copy-start.58 = (s32[4,256]{1,0:T(4,128)}, s32[4,256]{1,0:T(4,128)S(1)}, u32[]{:S(2)}) copy-start(s32[4,256]{1,0:T(4,128)S(1)} %get-tuple-element.143) | copy-start | bytes 12292
  130.8 110.1 %copy-start.20 = (pred[4,256,256]{1,2,0:T(8,128)(4,1)}, pred[4,256,256]{1,2,0:T(8,128)(4,1)S(1)}, u32[]{:S(2)}) copy-start(pred[4,256,256]{1,2,0:T(8,128)(4,1)S(1)} %get-tuple-element.147) | copy-start | bytes 786436
  136.4 49.0 %copy-start = (bf16[4,256,12,64]{1,0,3,2:T(4,128)(2,1)}, bf16[4,256,12,64]{1,0,3,2:T(4,128)(2,1)S(1)}, u32[]{:S(2)}) copy-start(bf16[4,256,12,64]{1,0,3,2:T(4,128)(2,1)S(1)} %reshape.205) | copy-start | bytes 4718596
  145.6 39.8 %collective-permute-start.2 = (bf16[4,256,12,64]{1,3,2,0:T(8,128)(2,1)}, bf16[4,256,12,64]{1,3,2,0:T(8,128)(2,1)S(1)}, u32[]{:S(2)}, u32[]{:S(2)}) collective-permute-start(bf16[4,256,12,64]{1,3,2,0:T(8,128)(2,1)} %collective-permute-done.1), channel_id=1, source_target_pairs={{3,0},{0,1},{1,2},{2,3},{7,4},{4,5},{5,6},{6,7},{11,8},{8,9},{9,10... | collective-permute-start | bytes 4718600 | tf_op jit(solution)/shard_map/ppermute | solution.py:25
  165.6 75.3 %collective-permute-start.5 = (bf16[4,256,12,64]{1,3,2,0:T(8,128)(2,1)}, bf16[4,256,12,64]{1,3,2,0:T(8,128)(2,1)}, u32[]{:S(2)}, u32[]{:S(2)}) collective-permute-start(bf16[4,256,12,64]{1,3,2,0:T(8,128)(2,1)} %collective-permute-done.4), channel_id=1, source_target_pairs={{3,0},{0,1},{1,2},{2,3},{7,4},{4,5},{5,6},{6,7},{11,8},{8,9},{9,10... | collective-permute-start | bytes 4718600 | tf_op jit(solution)/shard_map/ppermute | solution.py:25
  169.3 34.9 %copy-start.3 = (f32[4,12,256,256]{2,3,1,0:T(8,128)}, f32[4,12,256,256]{2,3,1,0:T(8,128)S(1)}, u32[]{:S(2)}) copy-start(f32[4,12,256,256]{2,3,1,0:T(8,128)S(1)} %get-tuple-element.151) | copy-start | bytes 37748740
  188.0 52.9 %copy-start.2 = (f32[4,12,256,256]{2,3,1,0:T(8,128)}, f32[4,12,256,256]{2,3,1,0:T(8,128)S(1)}, u32[]{:S(2)}) copy-start(f32[4,12,256,256]{2,3,1,0:T(8,128)S(1)} %get-tuple-element.149) | copy-start | bytes 37748740
  211.7 29.2 %copy-start.47 = (f32[4,12,256]{2,1,0:T(8,128)}, f32[4,12,256]{2,1,0:T(8,128)S(1)}, u32[]{:S(2)}) copy-start(f32[4,12,256]{2,1,0:T(8,128)S(1)} %log_add_fusion) | copy-start | bytes 147460
  255.9 35.9 %copy-start.70 = (f32[768]{0:T(1024)S(1)}, f32[768]{0:T(1024)}, u32[]{:S(2)}) copy-start(f32[768]{0:T(1024)} %get-tuple-element.100) | copy-start | bytes 9220
  343.1 362.3 %reduce-scatter.10.cloned.1.call-start = ((), (), s32[]{:S(2)}) async-start(), calls=%async_computation.9 | async-start | bytes 9732096 | tf_op jit(solution)/shard_map/reduce_scatter | solution.py:288
  353.8 380.6 %reduce-scatter.12.cloned.1.call-start = ((), (), s32[]{:S(2)}) async-start(), calls=%async_computation.10 | async-start | bytes 9732096 | tf_op jit(solution)/shard_map/reduce_scatter | solution.py:289
  424.5 57.9 %copy-start.17 = (bf16[4,256,12,64]{1,0,3,2:T(4,128)(2,1)}, bf16[4,256,12,64]{1,0,3,2:T(4,128)(2,1)S(1)}, u32[]{:S(2)}) copy-start(bf16[4,256,12,64]{1,0,3,2:T(4,128)(2,1)S(1)} %reshape.208) | copy-start | bytes 4718596
  434.0 83.3 %collective-permute-start.10 = (bf16[4,256,12,64]{1,3,2,0:T(8,128)(2,1)}, bf16[4,256,12,64]{1,3,2,0:T(8,128)(2,1)}, u32[]{:S(2)}, u32[]{:S(2)}) collective-permute-start(bf16[4,256,12,64]{1,3,2,0:T(8,128)(2,1)} %fusion.29), channel_id=1, source_target_pairs={{3,0},{0,1},{1,2},{2,3},{7,4},{4,5},{5,6},{6,7},{11,8},{8,9},{9,10... | collective-permute-start | bytes 4718600 | tf_op jit(solution)/shard_map/ppermute | solution.py:25
  451.8 76.0 %collective-permute-start.6 = (bf16[4,256,12,64]{1,3,2,0:T(8,128)(2,1)}, bf16[4,256,12,64]{1,3,2,0:T(8,128)(2,1)}, u32[]{:S(2)}, u32[]{:S(2)}) collective-permute-start(bf16[4,256,12,64]{1,3,2,0:T(8,128)(2,1)} %fusion.30), channel_id=1, source_target_pairs={{3,0},{0,1},{1,2},{2,3},{7,4},{4,5},{5,6},{6,7},{11,8},{8,9},{9,10... | collective-permute-start | bytes 4718600 | tf_op jit(solution)/shard_map/ppermute | solution.py:25
  464.7 394.6 %reduce-scatter.14.cloned.1.call-start = ((), (), s32[]{:S(2)}) async-start(), calls=%async_computation.11 | async-start | bytes 7299072 | tf_op jit(solution)/shard_map/reduce_scatter | solution.py:286
  465.6 16.8 %copy-start.57 = (f32[4,12,256]{2,1,0:T(8,128)S(1)}, f32[4,12,256]{2,1,0:T(8,128)}, u32[]{:S(2)}) copy-start(f32[4,12,256]{2,1,0:T(8,128)} %copy-done.56) | copy-start | bytes 147460
  465.6 33.0 %slice-start = ((s8[12582912]{0:T(1024)(128)(4,1)}), s8[4194304]{0:T(1024)(128)(4,1)S(1)}, s32[]{:S(2)}) async-start(s8[12582912]{0:T(1024)(128)(4,1)} %bitcast.139), calls=%async_computation.12 | async-start | bytes 8388608
  465.6 33.0 %slice-start.1 = ((s8[12582912]{0:T(1024)(128)(4,1)}), s8[4194304]{0:T(1024)(128)(4,1)S(1)}, s32[]{:S(2)}) async-start(s8[12582912]{0:T(1024)(128)(4,1)} %bitcast.139), calls=%async_computation.13 | async-start | bytes 8388608
  482.4 16.2 %slice-start.2 = ((s8[12582912]{0:T(1024)(128)(4,1)}), s8[4194304]{0:T(1024)(128)(4,1)S(1)}, s32[]{:S(2)}) async-start(s8[12582912]{0:T(1024)(128)(4,1)} %bitcast.139), calls=%async_computation.14 | async-start | bytes 8388608
  482.4 16.2 %copy-start.21 = (pred[4,256,256]{1,2,0:T(8,128)(4,1)S(1)}, pred[4,256,256]{1,2,0:T(8,128)(4,1)}, u32[]{:S(2)}) copy-start(pred[4,256,256]{1,2,0:T(8,128)(4,1)} %copy-done.20) | copy-start | bytes 786436
  498.6 13.0 %copy-start.10 = (bf16[4,256,12,64]{1,0,3,2:T(4,128)(2,1)S(1)}, bf16[4,256,12,64]{1,0,3,2:T(4,128)(2,1)}, u32[]{:S(2)}) copy-start(bf16[4,256,12,64]{1,0,3,2:T(4,128)(2,1)} %copy-done.9) | copy-start | bytes 4718596
  526.9 24.6 %collective-permute-start.11 = (bf16[4,256,12,64]{1,3,2,0:T(8,128)(2,1)}, bf16[4,256,12,64]{1,3,2,0:T(8,128)(2,1)}, u32[]{:S(2)}, u32[]{:S(2)}) collective-permute-start(bf16[4,256,12,64]{1,3,2,0:T(8,128)(2,1)} %fusion.16), channel_id=1, source_target_pairs={{3,0},{0,1},{1,2},{2,3},{7,4},{4,5},{5,6},{6,7},{11,8},{8,9},{9,10... | collective-permute-start | bytes 4718600 | tf_op jit(solution)/shard_map/ppermute | solution.py:25
  534.4 40.7 %collective-permute-start.7 = (bf16[4,256,12,64]{1,3,2,0:T(8,128)(2,1)}, bf16[4,256,12,64]{1,3,2,0:T(8,128)(2,1)}, u32[]{:S(2)}, u32[]{:S(2)}) collective-permute-start(bf16[4,256,12,64]{1,3,2,0:T(8,128)(2,1)} %fusion.19), channel_id=1, source_target_pairs={{3,0},{0,1},{1,2},{2,3},{7,4},{4,5},{5,6},{6,7},{11,8},{8,9},{9,10... | collective-permute-start | bytes 4718600 | tf_op jit(solution)/shard_map/ppermute | solution.py:25
  535.3 43.2 %slice-start.3 = ((s8[6291456]{0:T(1024)(128)(4,1)}), s8[4194304]{0:T(1024)(128)(4,1)S(1)}, s32[]{:S(2)}) async-start(s8[6291456]{0:T(1024)(128)(4,1)} %bitcast.141), calls=%async_computation.15 | async-start | bytes 8388608
  542.0 36.5 %slice-start.4 = ((s8[6291456]{0:T(1024)(128)(4,1)}), s8[2097152]{0:T(1024)(128)(4,1)S(1)}, s32[]{:S(2)}) async-start(s8[6291456]{0:T(1024)(128)(4,1)} %bitcast.141), calls=%async_computation.16 | async-start | bytes 4194304
  551.5 23.6 %copy-start.6 = (f32[4,12,64,256]{3,2,1,0:T(8,128)S(1)}, f32[4,12,64,256]{3,2,1,0:T(8,128)}, u32[]{:S(2)}) copy-start(f32[4,12,64,256]{3,2,1,0:T(8,128)} %fusion.46) | copy-start | bytes 9437188
  555.7 38.4 %collective-permute-start.12 = (bf16[4,256,12,64]{1,3,2,0:T(8,128)(2,1)}, bf16[4,256,12,64]{1,3,2,0:T(8,128)(2,1)}, u32[]{:S(2)}, u32[]{:S(2)}) collective-permute-start(bf16[4,256,12,64]{1,3,2,0:T(8,128)(2,1)} %fusion.15), channel_id=1, source_target_pairs={{3,0},{0,1},{1,2},{2,3},{7,4},{4,5},{5,6},{6,7},{11,8},{8,9},{9,10... | collective-permute-start | bytes 4718600 | tf_op jit(solution)/shard_map/ppermute | solution.py:25
  578.3 32.6 %collective-permute-start.8 = (bf16[4,256,12,64]{1,3,2,0:T(8,128)(2,1)}, bf16[4,256,12,64]{1,3,2,0:T(8,128)(2,1)}, u32[]{:S(2)}, u32[]{:S(2)}) collective-permute-start(bf16[4,256,12,64]{1,3,2,0:T(8,128)(2,1)} %fusion.18), channel_id=1, source_target_pairs={{3,0},{0,1},{1,2},{2,3},{7,4},{4,5},{5,6},{6,7},{11,8},{8,9},{9,10... | collective-permute-start | bytes 4718600 | tf_op jit(solution)/shard_map/ppermute | solution.py:25
  586.6 24.3 %copy-start.5 = (f32[4,12,64,256]{3,2,1,0:T(8,128)S(1)}, f32[4,12,64,256]{3,2,1,0:T(8,128)}, u32[]{:S(2)}) copy-start(f32[4,12,64,256]{3,2,1,0:T(8,128)} %fusion.44) | copy-start | bytes 9437188
  596.9 30.7 %collective-permute-start.13 = (bf16[4,256,12,64]{1,3,2,0:T(8,128)(2,1)S(1)}, bf16[4,256,12,64]{1,3,2,0:T(8,128)(2,1)S(1)}, u32[]{:S(2)}, u32[]{:S(2)}) collective-permute-start(bf16[4,256,12,64]{1,3,2,0:T(8,128)(2,1)S(1)} %fusion.14), channel_id=1, source_target_pairs={{3,0},{0,1},{1,2},{2,3},{7,4},{4,5},{5,6},{6,7},{11,8},{8,9},{9,10... | collective-permute-start | bytes 4718600 | tf_op jit(solution)/shard_map/ppermute | solution.py:25
  613.1 31.4 %collective-permute-start.9 = (bf16[4,256,12,64]{1,3,2,0:T(8,128)(2,1)S(1)}, bf16[4,256,12,64]{1,3,2,0:T(8,128)(2,1)S(1)}, u32[]{:S(2)}, u32[]{:S(2)}) collective-permute-start(bf16[4,256,12,64]{1,3,2,0:T(8,128)(2,1)S(1)} %fusion.17), channel_id=1, source_target_pairs={{3,0},{0,1},{1,2},{2,3},{7,4},{4,5},{5,6},{6,7},{11,8},{8,9},{9,10... | collective-permute-start | bytes 4718600 | tf_op jit(solution)/shard_map/ppermute | solution.py:25
  864.7 51.0 %copy-start.60 = (f32[12,24]{1,0:T(8,128)S(1)}, f32[12,24]{1,0:T(8,128)}, u32[]{:S(2)}) copy-start(f32[12,24]{1,0:T(8,128)} %param.27) | copy-start | bytes 3460
  864.8 51.0 %copy-start.68 = (f32[12,24]{1,0:T(8,128)S(1)}, f32[12,24]{1,0:T(8,128)}, u32[]{:S(2)}) copy-start(f32[12,24]{1,0:T(8,128)} %param.32) | copy-start | bytes 3460
  864.8 51.0 %copy-start.69 = (f32[12,24]{1,0:T(8,128)S(1)}, f32[12,24]{1,0:T(8,128)}, u32[]{:S(2)}) copy-start(f32[12,24]{1,0:T(8,128)} %param.37) | copy-start | bytes 3460
  864.8 51.7 %copy-start.32 = (f32[96,768]{1,0:T(8,128)S(1)}, f32[96,768]{1,0:T(8,128)}, u32[]{:S(2)}) copy-start(f32[96,768]{1,0:T(8,128)} %param.26) | copy-start | bytes 884740
  864.8 51.7 %copy-start.35 = (f32[96,768]{1,0:T(8,128)S(1)}, f32[96,768]{1,0:T(8,128)}, u32[]{:S(2)}) copy-start(f32[96,768]{1,0:T(8,128)} %reduce-scatter.12.cloned.1.call-done) | copy-start | bytes 884740
  864.8 51.7 %copy-start.41 = (f32[96,768]{1,0:T(8,128)S(1)}, f32[96,768]{1,0:T(8,128)}, u32[]{:S(2)}) copy-start(f32[96,768]{1,0:T(8,128)} %param.31) | copy-start | bytes 884740
  864.8 51.7 %copy-start.42 = (f32[96,768]{1,0:T(8,128)S(1)}, f32[96,768]{1,0:T(8,128)}, u32[]{:S(2)}) copy-start(f32[96,768]{1,0:T(8,128)} %param.36) | copy-start | bytes 884740
  864.8 52.8 %copy-start.33 = (f32[24,3072]{1,0:T(8,128)S(1)}, f32[24,3072]{1,0:T(8,128)}, u32[]{:S(2)}) copy-start(f32[24,3072]{1,0:T(8,128)} %param.25) | copy-start | bytes 884740
  864.8 52.8 %copy-start.34 = (f32[24,3072]{1,0:T(8,128)S(1)}, f32[24,3072]{1,0:T(8,128)}, u32[]{:S(2)}) copy-start(f32[24,3072]{1,0:T(8,128)} %reduce-scatter.10.cloned.1.call-done) | copy-start | bytes 884740
  864.8 52.8 %copy-start.43 = (f32[24,3072]{1,0:T(8,128)S(1)}, f32[24,3072]{1,0:T(8,128)}, u32[]{:S(2)}) copy-start(f32[24,3072]{1,0:T(8,128)} %param.30) | copy-start | bytes 884740
  864.9 52.7 %copy-start.44 = (f32[24,3072]{1,0:T(8,128)S(1)}, f32[24,3072]{1,0:T(8,128)}, u32[]{:S(2)}) copy-start(f32[24,3072]{1,0:T(8,128)} %param.35) | copy-start | bytes 884740
  864.9 53.8 %copy-start.45 = (f32[24,768]{1,0:T(8,128)S(1)}, f32[24,768]{1,0:T(8,128)}, u32[]{:S(2)}) copy-start(f32[24,768]{1,0:T(8,128)} %param.24) | copy-start | bytes 221188
  864.9 53.8 %copy-start.46 = (f32[24,768]{1,0:T(8,128)S(1)}, f32[24,768]{1,0:T(8,128)}, u32[]{:S(2)}) copy-start(f32[24,768]{1,0:T(8,128)} %reduce-scatter.8.cloned.1.call-done) | copy-start | bytes 221188
  864.9 53.8 %copy-start.53 = (f32[24,768]{1,0:T(8,128)S(1)}, f32[24,768]{1,0:T(8,128)}, u32[]{:S(2)}) copy-start(f32[24,768]{1,0:T(8,128)} %param.29) | copy-start | bytes 221188
  874.9 45.4 %copy-start.38 = (f32[24,2304]{1,0:T(8,128)S(1)}, f32[24,2304]{1,0:T(8,128)}, u32[]{:S(2)}) copy-start(f32[24,2304]{1,0:T(8,128)} %param.23) | copy-start | bytes 663556
  874.9 45.4 %copy-start.39 = (f32[24,2304]{1,0:T(8,128)S(1)}, f32[24,2304]{1,0:T(8,128)}, u32[]{:S(2)}) copy-start(f32[24,2304]{1,0:T(8,128)} %reduce-scatter.14.cloned.1.call-done) | copy-start | bytes 663556
  874.9 45.4 %copy-start.49 = (f32[24,2304]{1,0:T(8,128)S(1)}, f32[24,2304]{1,0:T(8,128)}, u32[]{:S(2)}) copy-start(f32[24,2304]{1,0:T(8,128)} %param.28) | copy-start | bytes 663556
  874.9 45.4 %copy-start.50 = (f32[24,2304]{1,0:T(8,128)S(1)}, f32[24,2304]{1,0:T(8,128)}, u32[]{:S(2)}) copy-start(f32[24,2304]{1,0:T(8,128)} %param.33) | copy-start | bytes 663556
  (41 other events, 194.1 us)
Sparse Core Ops, SparseCore 0:
  11.5 63.0 all-gather.5
  78.1 54.1 all-gather.7
  135.8 66.8 all-gather.9
  206.0 62.4 all-gather.11
  343.2 98.3 reduce-scatter.7
  448.3 143.6 reduce-scatter.9
  598.0 136.3 reduce-scatter.11
  741.0 118.2 reduce-scatter.13
where the time goes:
time: 938 us; the launch traced here: 930 us
  matrix products  309 us (33%)
  waiting for transfers between devices  282 us (30%)
  blocking collectives  123 us (13%)
  local copies, waits for them, and re-layouts  105 us (11%)
  other arithmetic  80.1 us (9%)
  between operations  21 us (2%)
    reduce_scatter x1, waiting for transfers between devices, local(): lax.psum_scatter(grad_joint, ('dp', 'seq'), scatter_dimension=0, tiled=True)  123 us
    ppermute x14, waiting for transfers between devices, passed_along(): return lax.ppermute(block, axis, route)  115 us
    dot_general x4, matrix products, local(): jnp.einsum('rqhd,rkhd->rhqk', d_attended, values_now, preferred_element_t...  56.5 us
    unnamed x179, local copies, waits for them, and re-layouts  54.4 us
    all_gather x1, blocking collectives, local(): lax.all_gather(vectors.astype(jnp.bfloat16), ('dp', 'seq'), axis=1, tiled...  43.6 us
    psum x1, blocking collectives, local(): square_total = lax.psum(local_squares, ('dp', 'seq'))  40.1 us
    unnamed x1, blocking collectives  39.5 us
    dot_general x4, matrix products, local(): jnp.einsum('rhqk,rkhd->rqhd', attention.astype(jnp.bfloat16), values_now,...  37 us
  transfers between devices with their start and end apart: 22, of which 13 were waited for; matrix products, arithmetic and copies ran while one was open for 45% of the time, Pallas kernels for 0%

commit v1 on v0

v1 whole, which is shorter than its diff:
```python
import functools

import jax
import jax.numpy as jnp
import numpy as np
from jax import lax
from jax.experimental import pallas as pl
from jax.experimental.pallas import tpu as pltpu
from jax.sharding import PartitionSpec as P

HEADS = 12
STEP = 10
NORM_EPS = 1e-05
MASK_FILL = -1e30
DISTILL = 0.5
CLIP_LEVEL = 1.0
BETA_ONE = 0.9
BETA_TWO = 0.999
ADAM_EPS = 1e-08
DECAY = 0.01
RATE_MATRIX = 0.05
RATE_VECTOR = 0.5

LANES = 128
CHIPS = 16
SLAB = 48
VMEM_BYTES = 60 * 1024 * 1024
F32 = jnp.float32
BF16 = jnp.bfloat16
INV_SQRT2 = 0.7071067811865476
INV_SQRT_2PI = 0.3989422804014327
GATHER_Z = (0, 2, 1, 3)
PLACES = [(x, y, z) for x in range(2) for y in range(2) for z in GATHER_Z]


def params(rank, fuse=False):
    return pltpu.CompilerParams(
        dimension_semantics=("arbitrary",) * rank,
        vmem_limit_bytes=VMEM_BYTES,
        fuse_transposed_lhs_in_matmul=fuse,
    )


def cost(flops, nbytes, trans=0):
    return pl.CostEstimate(flops=int(flops), bytes_accessed=int(nbytes), transcendentals=int(trans))


def dot(a, b):
    return lax.dot_general(a, b, (((1,), (0,)), ((), ())), preferred_element_type=F32)


def dot_nt(a, b):
    return lax.dot_general(a, b, (((1,), (1,)), ((), ())), preferred_element_type=F32)


def dot_tn(a, b):
    return lax.dot_general(a, b, (((0,), (0,)), ((), ())), preferred_element_type=F32)


def swap(x, axis, bit):
    return lax.ppermute(x, axis, [(i, i ^ bit) for i in range(lax.axis_size(axis))])


def after(x, *deps):
    return lax.optimization_barrier((x, *deps))[0]


def stage(*parts):
    return list(lax.optimization_barrier(parts))


def split_core(mine, got):
    total = mine + got.astype(F32)
    kept = (total[0, 0], total[1, 0, 2:], total[0, 1, :2])
    over_x = jnp.stack([total[1, 1, :2], total[1, 0, :2]]).astype(BF16)
    over_y = jnp.stack([total[1, 1, 2:], total[0, 1, 2:]]).astype(BF16)
    return kept, over_x, over_y


def add_first(kept, got_x, got_y):
    near, next_x, next_y = kept
    got_x, got_y = got_x.astype(F32), got_y.astype(F32)
    near = (near[:2] + got_x[1], near[2:] + got_y[1])
    return near, (next_x + got_y[0]).astype(BF16), (next_y + got_x[0]).astype(BF16)


def add_second(near, got_x, got_y):
    front = near[0] + got_y.astype(F32)
    back = near[1] + got_x.astype(F32)
    return jnp.stack([front[0], back[0]]), jnp.stack([front[1], back[1]]).astype(BF16)


def add_z(near, got):
    return near[0] + got[0].astype(F32), (near[1] + got[1].astype(F32)).astype(BF16)


def sum_all(v):
    for axis, bit in (("seq", 1), ("dp", 1), ("dp", 2), ("dp", 4), ("seq", 2)):
        v = v + swap(v, axis, bit)
    return v


def load_slabs(meta, sources, dest, sems, row_base, rows, cols, col_base, sem_base):
    copies = []
    for which, source in enumerate(sources):
        half = jnp.bitwise_xor(meta[0], which // 4)
        for z in range(4):
            chip = meta[4 + which % 4 * 4 + z]
            copies.append(
                pltpu.make_async_copy(
                    source.at[z, pl.ds(row_base, rows), pl.ds(0, cols)],
                    dest.at[
                        pl.ds(pl.multiple_of(chip * rows, 16), rows),
                        pl.ds(pl.multiple_of(col_base(half), LANES), cols),
                    ],
                    sems.at[sem_base + len(copies)],
                )
            )
    for c in copies:
        c.start()
    return copies


def project_kernel(blocks, steps, meta, need, *refs):
    xs = refs[:blocks]
    slabs = refs[blocks : blocks + 8]
    bias, q_ref, k_ref, v_ref, w_ref, sems = refs[blocks + 8 :]
    width = q_ref.shape[-1]
    half_cols = w_ref.shape[1] // 2
    step = pl.program_id(0)
    row = step % steps * 2

    @pl.when(step == 0)
    def _():
        for c in load_slabs(
            meta, slabs, w_ref, sems, 0, SLAB, half_cols, lambda h: h * half_cols, 0
        ):
            c.wait()

    for d in range(blocks):

        @pl.when((step // steps == d) & (need[row, d] + need[row + 1, d] > 0))
        def _(d=d):
            x = xs[d][...]
            k_ref[0] = dot(x, w_ref[:, width : 2 * width]).astype(BF16)
            v_ref[0] = (dot(x, w_ref[:, 2 * width :]) + bias[1:2, :]).astype(BF16)
            if d == 0:
                q = dot(x, w_ref[:, :width]) + bias[0:1, :]
                q_ref[...] = q.astype(BF16) * jnp.asarray((width // HEADS) ** -0.5, BF16)


def project(meta, need, xs, slabs, vec, deps):
    blocks = len(xs)
    tokens, width = xs[0].shape
    steps = need.shape[0] // 2
    size = tokens // steps

    def x_spec(d):
        return pl.BlockSpec((size, width), lambda i, *_: (jnp.clip(i - d * steps, 0, steps - 1), 0))

    hbm = pl.BlockSpec(memory_space=pl.ANY)
    kv_spec = pl.BlockSpec((1, size, width), lambda i, *_: (i // steps, i % steps, 0))
    kv_shape = jax.ShapeDtypeStruct((blocks, tokens, width), BF16)
    return pl.pallas_call(
        skipping(
            functools.partial(project_kernel, blocks, steps), blocks + len(slabs) + 3, len(deps)
        ),
        grid_spec=pltpu.PrefetchScalarGridSpec(
            num_scalar_prefetch=2,
            grid=(blocks * steps,),
            in_specs=[x_spec(d) for d in range(blocks)]
            + [hbm] * len(slabs)
            + [pl.BlockSpec(vec.shape, lambda i, *_: (0, 0))]
            + [hbm] * len(deps),
            out_specs=[
                pl.BlockSpec((size, width), lambda i, *_: (jnp.minimum(i, steps - 1), 0)),
                kv_spec,
                kv_spec,
                pl.BlockSpec((width, 3 * width), lambda i, *_: (0, 0)),
            ],
            scratch_shapes=[pltpu.SemaphoreType.DMA((2 * CHIPS,))],
        ),
        out_shape=[
            jax.ShapeDtypeStruct((tokens, width), BF16),
            kv_shape,
            kv_shape,
            jax.ShapeDtypeStruct((width, 3 * width), BF16),
        ],
        compiler_params=params(1),
        cost_estimate=cost(
            2 * tokens * width * width * (2 * blocks + 1), 4 * blocks * tokens * width
        ),
        name="project",
    )(meta, need, *xs, *slabs, vec, *deps)


def share_kernel(start, teach_ref, segq_ref, segk_ref, out_ref, mask_scr):
    length, keys = mask_scr.shape

    @pl.when(pl.program_id(1) == 0)
    def _():
        same = spread(segq_ref[0], keys) == segk_ref[0, 0:1, :]
        mask_scr[...] = jnp.where(same, 1.0, 0.0).astype(BF16)

    ones = jnp.ones((keys, LANES), BF16)
    sums = [dot(teach_ref[0, h] * mask_scr[...], ones) for h in range(2)]
    out_ref[0, 0] = DISTILL / pick_lanes(sums[0], sums[1])


def share(teacher, segq, seg_row, start, count, deps):
    _, heads, length, keys = teacher.shape
    return pl.pallas_call(
        skipping(functools.partial(share_kernel, start), 3, len(deps)),
        grid=(count, heads // 2),
        in_specs=[
            pl.BlockSpec((1, 2, length, keys), lambda r, p: (r + start, p, 0, 0)),
            pl.BlockSpec((1, length, LANES), lambda r, p: (r + start, 0, 0)),
            pl.BlockSpec((1, 8, keys), lambda r, p: (r + start, 0, 0)),
        ]
        + [pl.BlockSpec(memory_space=pl.ANY)] * len(deps),
        out_specs=pl.BlockSpec((1, 1, length, LANES), lambda r, p: (r, p, 0, 0)),
        scratch_shapes=[pltpu.VMEM((length, keys), BF16)],
        out_shape=jax.ShapeDtypeStruct((count, heads // 2, length, LANES), F32),
        compiler_params=params(2),
        cost_estimate=cost(4 * count * heads * length * keys, 2 * count * heads * length * keys),
        name="share",
    )(teacher, segq, seg_row, *deps)


def head_parts(x):
    lane = lax.broadcasted_iota(jnp.int32, x.shape, 1)
    zero = jnp.zeros_like(x)
    first = lane < LANES // 2
    return (jnp.where(first, x, zero), jnp.where(first, zero, x))


def pick_lanes(a, b):
    lane = lax.broadcasted_iota(jnp.int32, (a.shape[0], LANES), 1)
    return jnp.where(lane < LANES // 2, a, b)


def spread(x, length):
    return x if length == LANES else jnp.concatenate([x] * (length // LANES), axis=1)


def fold(x, op):
    out = x[:, :LANES]
    for i in range(1, x.shape[1] // LANES):
        out = op(out, x[:, i * LANES : (i + 1) * LANES])
    return out


def fill_bias(plan, r, blocks, length, segq_ref, segk_ref, bias_scr, mask_scr):
    seg_q = spread(segq_ref[0], length)
    for j in range(blocks):

        @pl.when(plan[r, 0] > j)
        def _(j=j):
            d = plan[r, 1 + j]
            same = seg_q == segk_ref[d, 0, 0:1, :]
            bias_scr[d] = jnp.where(same, 0.0, MASK_FILL)
            if mask_scr is not None:
                mask_scr[d] = jnp.where(same, 1.0, 0.0).astype(BF16)


def skipping(kernel, first, count):
    def run(*refs):
        kernel(*refs[:first], *refs[first + count :])

    return run


def attend_kernel(
    blocks, start, plan, q_ref, k_ref, v_ref, segq_ref, segk_ref, o_ref, lse_ref, bias_scr
):
    r = pl.program_id(0) + start
    length = q_ref.shape[1]

    @pl.when(pl.program_id(1) == 0)
    def _():
        fill_bias(plan, r, blocks, length, segq_ref, segk_ref, bias_scr, None)

    for count in range(1, blocks + 1):

        @pl.when(plan[r, 0] == count)
        def _(count=count):
            for pair in range(q_ref.shape[2] // LANES):
                lanes = slice(pair * LANES, (pair + 1) * LANES)
                q_heads = head_parts(q_ref[0, :, lanes])
                outs, logs = [], []
                for h in range(2):
                    scores = []
                    for j in range(count):
                        d = plan[r, 1 + j]
                        scores.append(dot_nt(q_heads[h], k_ref[d, 0, :, lanes]) + bias_scr[d])
                    top = fold(functools.reduce(jnp.maximum, scores), jnp.maximum)
                    top = jnp.max(top, axis=1, keepdims=True)
                    total = acc = None
                    for j in range(count):
                        d = plan[r, 1 + j]
                        e = jnp.exp(scores[j] - top)
                        part = fold(e, jnp.add)
                        out = dot(e.astype(BF16), v_ref[d, 0, :, lanes])
                        total = part if j == 0 else total + part
                        acc = out if j == 0 else acc + out
                    total = jnp.sum(total, axis=1, keepdims=True)
                    outs.append(acc * (1.0 / total))
                    logs.append(jnp.broadcast_to(top + jnp.log(total), (length, LANES)))
                o_ref[0, :, lanes] = pick_lanes(outs[0], outs[1]).astype(BF16)
                lse_ref[0, pair] = pick_lanes(logs[0], logs[1])


def attend(plan, q, k, v, segq, segk, start, count, before, deps):
    blocks, rows, length, width = k.shape
    pairs = width // LANES
    group = 2
    lanes = group * LANES
    extra = (*before, *deps)
    kv_spec = pl.BlockSpec((blocks, 1, length, lanes), lambda r, p, *_: (0, r + start, 0, p))
    tok_spec = pl.BlockSpec((1, length, lanes), lambda r, p, *_: (r + start, 0, p))
    return pl.pallas_call(
        skipping(functools.partial(attend_kernel, blocks, start), 6, len(extra)),
        grid_spec=pltpu.PrefetchScalarGridSpec(
            num_scalar_prefetch=1,
            grid=(count, pairs // group),
            in_specs=[
                tok_spec,
                kv_spec,
                kv_spec,
                pl.BlockSpec((1, length, LANES), lambda r, p, *_: (r + start, 0, 0)),
                pl.BlockSpec((blocks, 1, 8, length), lambda r, p, *_: (0, r + start, 0, 0)),
            ]
            + [pl.BlockSpec(memory_space=pl.ANY)] * len(extra),
            out_specs=[
                tok_spec,
                pl.BlockSpec((1, group, length, LANES), lambda r, p, *_: (r + start, p, 0, 0)),
            ],
            scratch_shapes=[pltpu.VMEM((blocks, length, length), F32)],
        ),
        out_shape=[
            jax.ShapeDtypeStruct((rows, length, width), BF16),
            jax.ShapeDtypeStruct((rows, pairs, length, LANES), F32),
        ],
        input_output_aliases={6 + i: i for i in range(len(before))},
        compiler_params=params(2),
        cost_estimate=cost(16 * count * length * length * blocks * width, k.size),
        name="attend",
    )(plan, q, k, v, segq, segk, *extra)


def attend_back_kernel(
    blocks, start, meta, plan, q_ref, k_ref, v_ref, do_ref, o_ref, lse_ref, share_ref, teach_ref,
    segq_ref, segk_ref, dq_ref, dk_ref, dv_ref, bias_scr, mask_scr
):
    r = pl.program_id(0) + start
    length = q_ref.shape[1]
    head_dim = LANES // 2
    seq_rank = meta[3]

    @pl.when(pl.program_id(1) == 0)
    def _():
        fill_bias(plan, r, blocks, length, segq_ref, segk_ref, bias_scr, mask_scr)

    def body(count):
        q = q_ref[0]
        do = do_ref[0]
        q_heads = head_parts(q)
        do_heads = head_parts(do)
        q_turned = q.T
        do_turned = do.T
        o = o_ref[0].astype(F32)
        dk = [[], []]
        dv = [[], []]
        dq = []
        for h in range(2):
            rows = slice(h * head_dim, (h + 1) * head_dim)
            shift = DISTILL - jnp.sum(do_heads[h].astype(F32) * o, axis=1, keepdims=True)
            lse = lse_ref[0, 0][:, h * head_dim : h * head_dim + 1]
            share_h = share_ref[0, 0][:, h * head_dim : h * head_dim + 1]
            for j in range(count):
                d = plan[r, 1 + j]
                k = k_ref[d, 0]
                p = jnp.exp(dot_nt(q_heads[h], k) + bias_scr[d] - lse)
                dp = dot_nt(do_heads[h], v_ref[d, 0])
                place = pl.multiple_of(jnp.bitwise_xor(seq_rank, d) * length, LANES)
                t = (teach_ref[0, h, :, pl.ds(place, length)] * mask_scr[d]).astype(F32)
                ds = (p * (dp + shift) - t * share_h).astype(BF16)
                dv[h].append(dot(do_turned[rows], p.astype(BF16)))
                dk[h].append(dot(q_turned[rows], ds))
                part = dot(ds, k)
                if j == 0:
                    dq.append(part)
                else:
                    dq[h] = dq[h] + part
        for j in range(count):
            d = plan[r, 1 + j]
            dk_ref[d, 0] = jnp.concatenate([dk[0][j], dk[1][j]]).T.astype(BF16)
            dv_ref[d, 0] = jnp.concatenate([dv[0][j], dv[1][j]]).T.astype(BF16)
        dq_ref[0] = (pick_lanes(dq[0], dq[1]) * head_dim**-0.5).astype(BF16)

    for count in range(1, blocks + 1):
        pl.when(plan[r, 0] == count)(functools.partial(body, count))
    for j in range(1, blocks):

        @pl.when(plan[r, 0] <= j)
        def _(j=j):
            d = plan[r, 1 + j]
            dk_ref[d, 0] = jnp.zeros((length, LANES), BF16)
            dv_ref[d, 0] = jnp.zeros((length, LANES), BF16)


def attend_back(
    meta, plan, q, k, v, d_out, out, lse, shares, teacher, segq, segk, start, before, deps
):
    blocks, rows, length, width = k.shape
    pairs = width // LANES
    extra = (*before, *deps)
    per = shares[0].shape[0]
    kv_spec = pl.BlockSpec((blocks, 1, length, LANES), lambda r, p, *_: (0, r + start, 0, p))
    tok_spec = pl.BlockSpec((1, length, LANES), lambda r, p, *_: (r + start, 0, p))
    kv_shape = jax.ShapeDtypeStruct(k.shape, BF16)
    return pl.pallas_call(
        skipping(functools.partial(attend_back_kernel, blocks, start), 12, len(extra)),
        grid_spec=pltpu.PrefetchScalarGridSpec(
            num_scalar_prefetch=2,
            grid=(1, pairs),
            in_specs=[
                tok_spec,
                kv_spec,
                kv_spec,
                tok_spec,
                tok_spec,
                pl.BlockSpec((1, 1, length, LANES), lambda r, p, *_: (r + start, p, 0, 0)),
                pl.BlockSpec((1, 1, length, LANES), lambda r, p, *_: (start % per, p, 0, 0)),
                pl.BlockSpec(
                    (1, 2, length, teacher.shape[3]), lambda r, p, *_: (r + start, p, 0, 0)
                ),
                pl.BlockSpec((1, length, LANES), lambda r, p, *_: (r + start, 0, 0)),
                pl.BlockSpec((blocks, 1, 8, length), lambda r, p, *_: (0, r + start, 0, 0)),
            ]
            + [pl.BlockSpec(memory_space=pl.ANY)] * len(extra),
            out_specs=[tok_spec, kv_spec, kv_spec],
            scratch_shapes=[
                pltpu.VMEM((blocks, length, length), F32),
                pltpu.VMEM((blocks, length, length), BF16),
            ],
        ),
        out_shape=[jax.ShapeDtypeStruct(q.shape, BF16), kv_shape, kv_shape],
        input_output_aliases={12 + i: i for i in range(len(before))},
        compiler_params=params(2),
        cost_estimate=cost(40 * length * length * blocks * width, 2 * k.size),
        name="attend_back",
    )(
        meta, plan, q, k, v, d_out, out, lse, shares[start // per], teacher, segq, segk, *extra
    )


def norm(values):
    centered = values - jnp.mean(values, axis=1, keepdims=True)
    inverse = lax.rsqrt(jnp.mean(centered * centered, axis=1, keepdims=True) + NORM_EPS)
    return centered * inverse, inverse


def norm_back(upstream, normed, inverse, gain):
    scaled = upstream * gain
    inner = jnp.mean(scaled, axis=1, keepdims=True)
    cross = jnp.mean(scaled * normed, axis=1, keepdims=True)
    return inverse * (scaled - inner - normed * cross)


def colsum(x):
    return jnp.sum(x, axis=0, keepdims=True)


def feed_kernel(
    meta, x_ref, o_ref, cot_ref, vec, fbias, *refs
):
    sources = refs[: 8]
    (out_ref, df1_ref, do_ref, gl_ref, du_ref, h1_ref, dz_ref, da_ref, gvec_ref, gbias_ref,
     wo, we, ws, gp_scr, sems) = refs[8 :]
    step = pl.program_id(0)
    half_d = wo.shape[1] // 2
    half_f = we.shape[1] // 2

    @pl.when(step == 0)
    def _():
        copies = []
        for k in range(half_f // half_d):
            copies += load_slabs(
                meta, sources, we, sems, k * SLAB, SLAB, half_d,
                lambda h, k=k: h * half_f + k * half_d, len(copies)
            )
        base = half_f // half_d * SLAB
        copies += load_slabs(
            meta, sources, wo, sems, base, SLAB, half_d, lambda h: h * half_d, len(copies)
        )
        base += SLAB
        copies += load_slabs(
            meta, sources, ws, sems, base, ws.shape[0] // CHIPS, half_d,
            lambda h: h * half_d, len(copies)
        )
        gvec_ref[...] = jnp.zeros(gvec_ref.shape, F32)
        gbias_ref[...] = jnp.zeros(gbias_ref.shape, F32)
        for c in copies:
            c.wait()

    base = 3 + ws.shape[0] // wo.shape[0]
    bias_out = vec[2:3]
    bias_shrink, gain1, shift1, gain2, shift2 = (vec[base + i : base + i + 1] for i in range(5))
    chunk = wo.shape[0] // 2
    chunks = ws.shape[0] // chunk

    branch = dot(o_ref[...], wo[...]) + bias_out
    normed1, inverse1 = norm(x_ref[...].astype(F32) + branch)
    hidden = normed1 * gain1 + shift1
    hidden_low = hidden.astype(BF16)
    h1_ref[...] = hidden_low
    z = None
    spans = [slice(c * chunk, (c + 1) * chunk) for c in range(chunks)]
    ahead = dot(hidden_low, we[:, spans[0]])
    for c, cols in enumerate(spans):
        u = ahead + fbias[0:1, cols]
        if c + 1 < chunks:
            ahead = dot(hidden_low, we[:, spans[c + 1]])
        phi = 0.5 + 0.5 * lax.erf(u * INV_SQRT2)
        gp_scr[:, cols] = phi + u * (jnp.exp(-0.5 * u * u) * INV_SQRT_2PI)
        gl = (u * phi).astype(BF16)
        gl_ref[:, cols] = gl
        part = dot(gl, ws[cols, :])
        z = part if c == 0 else z + part
    normed2, inverse2 = norm(hidden + z + bias_shrink)
    out_ref[...] = (normed2 * gain2 + shift2).astype(BF16)
    cot = cot_ref[...].astype(F32)
    gvec_ref[6:7] += colsum(cot * normed2)
    gvec_ref[7:8] += colsum(cot)
    df2 = norm_back(cot, normed2, inverse2, gain2)
    dz = df2.astype(BF16)
    dz_ref[...] = dz
    gvec_ref[3:4] += colsum(dz.astype(F32))
    dh = df2
    ahead = dot_nt(dz, ws[spans[0], :])
    for c, cols in enumerate(spans):
        du = (ahead * gp_scr[:, cols]).astype(BF16)
        if c + 1 < chunks:
            ahead = dot_nt(dz, ws[spans[c + 1], :])
        du_ref[:, cols] = du
        gbias_ref[0:1, cols] += colsum(du.astype(F32))
        dh = dh + dot_nt(du, we[:, cols])
    gvec_ref[4:5] += colsum(dh * normed1)
    gvec_ref[5:6] += colsum(dh)
    df1 = norm_back(dh, normed1, inverse1, gain1)
    df1_ref[...] = df1
    da = df1.astype(BF16)
    da_ref[...] = da
    gvec_ref[2:3] += colsum(da.astype(F32))
    do_ref[...] = dot_nt(da, wo[...]).astype(BF16)


def feed(meta, x, o, cot, vec, fbias, slabs):
    tokens, width = x.shape
    hidden = fbias.shape[1]
    size = tokens // 4
    tok = pl.BlockSpec((size, width), lambda i, *_: (i, 0))
    wide = pl.BlockSpec((size, hidden), lambda i, *_: (i, 0))
    full = lambda shape: pl.BlockSpec(shape, lambda i, *_: (0, 0))
    hbm = pl.BlockSpec(memory_space=pl.ANY)
    low = jax.ShapeDtypeStruct(x.shape, BF16)
    wide_low = jax.ShapeDtypeStruct((tokens, hidden), BF16)
    return pl.pallas_call(
        feed_kernel,
        grid_spec=pltpu.PrefetchScalarGridSpec(
            num_scalar_prefetch=1,
            grid=(tokens // size,),
            in_specs=[tok, tok, tok, full(vec.shape), full(fbias.shape)] + [hbm] * len(slabs),
            out_specs=[tok, tok, tok, wide, wide, tok, tok, tok, full((8, width)), full((8, hidden))],
            scratch_shapes=[
                pltpu.VMEM((width, width), BF16),
                pltpu.VMEM((width, hidden), BF16),
                pltpu.VMEM((hidden, width), BF16),
                pltpu.VMEM((size, hidden), F32),
                pltpu.SemaphoreType.DMA((32 * (hidden // width + 2),)),
            ],
        ),
        out_shape=[
            low,
            jax.ShapeDtypeStruct(x.shape, F32),
            low,
            wide_low,
            wide_low,
            low,
            low,
            low,
            jax.ShapeDtypeStruct((8, width), F32),
            jax.ShapeDtypeStruct((8, hidden), F32),
        ],
        compiler_params=params(1),
        cost_estimate=cost(
            4 * tokens * width * (width + 2 * hidden), 4 * tokens * (5 * width + hidden)
        ),
        name="feed",
    )(meta, x, o, cot, vec, fbias, *slabs)


def chip_of(meta, x, y, z):
    far_z, far_x, far_y = (jnp.bitwise_xor(meta[20 + i], v) for i, v in enumerate((z, x, y)))
    return (far_z * 2 + far_x) * 2 + far_y


def feed_grad_kernel(added, meta, h1_ref, du_ref, gl_ref, dz_ref, ol_ref, da_ref, *refs):
    got_ref = refs[0] if added else None
    scr = refs[-1]
    step = pl.program_id(0)
    half = dz_ref.shape[1]
    width = 2 * half
    we_rows = 4 * SLAB

    def put(x, y, z, at, rows, part):
        at = pl.ds(at, rows)
        if not added:
            refs[0][x, y, z, at] = part.astype(BF16)
            return
        near, next_x, next_y, over_x, over_y = refs[1:6]
        total = part + got_ref[x, y, z, at].astype(F32)

        def first_half():
            if x == 1:
                over_x[1 - y, z % 2, at] = total.astype(BF16)
            elif y == 1:
                next_y[z % 2, at] = total

        def last_half():
            if y == 1:
                over_y[1 - x, z % 2, at] = total.astype(BF16)
            elif x == 1:
                next_x[z % 2, at] = total

        if x == 0 and y == 0:
            near[z, at] = total
        elif isinstance(z, int):
            first_half() if z < 2 else last_half()
        else:
            pl.when(z < 2)(first_half)
            pl.when(z >= 2)(last_half)

    def put_all(at, cols):
        for x in range(2):
            for y in range(2):
                for z in range(4):
                    first = pl.multiple_of(chip_of(meta, x, y, z) * SLAB, 8)
                    put(x, y, z, at, SLAB, scr[pl.ds(first, SLAB), cols])

    @pl.when(step == 0)
    def _():
        scr[:, :half] = dot_tn(ol_ref[...], da_ref[...])
        put_all(we_rows, slice(0, half))

    for u in range(2):

        @pl.when(step == u)
        def _(u=u):
            scr[...] = dot_tn(h1_ref[...], du_ref[...])
            for k in range(width // half):
                put_all((2 * u + k) * SLAB, slice(k * half, (k + 1) * half))

    @pl.when(step >= 2)
    def _():
        scr[:, :half] = dot_tn(gl_ref[...], dz_ref[...])
        z = jnp.bitwise_xor(meta[20], step - 2)
        for x in range(2):
            for y in range(2):
                chip = jnp.bitwise_xor(meta[21], x) * 2 + jnp.bitwise_xor(meta[22], y)
                first = pl.multiple_of(chip * 4 * SLAB, 8)
                put(x, y, z, we_rows + SLAB, 4 * SLAB, scr[pl.ds(first, 4 * SLAB), :half])


def feed_grad(meta, h1, du, gl, dz, ol, da, got):
    tokens, width = h1.shape
    half = width // 2
    wide = lambda index: pl.BlockSpec((tokens, width), index)
    added = got is not None
    slab = (9 * SLAB, half)
    every = (2, 2, 4)
    if added:
        outs = [((4,), F32), ((2,), F32), ((2,), F32), ((2, 2), BF16), ((2, 2), BF16)]
    else:
        outs = [(every, BF16)]
    slab_spec = lambda lead: pl.BlockSpec(lead + slab, lambda u, m: (0,) * (len(lead) + 2))
    return pl.pallas_call(
        functools.partial(feed_grad_kernel, added),
        grid_spec=pltpu.PrefetchScalarGridSpec(
            num_scalar_prefetch=1,
            grid=(6,),
            in_specs=[
                wide(lambda u, m: (0, 0)),
                wide(lambda u, m: (0, 2 * m[0] + jnp.minimum(u, 1))),
                wide(lambda u, m: (0, jnp.clip(u - 2, 0, 3))),
                pl.BlockSpec((tokens, half), lambda u, m: (0, m[0])),
                wide(lambda u, m: (0, 0)),
                pl.BlockSpec((tokens, half), lambda u, m: (0, m[0])),
            ]
            + [slab_spec(every)] * added,
            out_specs=[slab_spec(lead) for lead, _ in outs],
            scratch_shapes=[pltpu.VMEM((width, width), F32)],
        ),
        out_shape=[jax.ShapeDtypeStruct(lead + slab, dtype) for lead, dtype in outs],
        compiler_params=params(1, True),
        cost_estimate=cost(9 * tokens * width * width, 16 * tokens * width),
        name="feed_grad",
    )(meta, h1, du, gl, dz, ol, da, *((got,) if added else ()))


def token_grad_kernel(steps, sent, kept, meta, need, dk_ref, dv_ref, w_ref, *refs):
    step = pl.program_id(0)
    row = step % steps * 2
    width = w_ref.shape[0]
    blocks = sent + kept
    for i, d in enumerate(blocks):
        out_ref = refs[-2] if i < len(sent) and kept else refs[-1]
        wanted = need[row, d] + need[row + 1, d]

        @pl.when((step // steps == i) & (wanted > 0))
        def _(d=d, out_ref=out_ref):
            out = dot_nt(dk_ref[0], w_ref[:, width : 2 * width])
            out = out + dot_nt(dv_ref[0], w_ref[:, 2 * width :])
            if d == 0:
                dq_ref, df1_ref = refs[:2]
                out = out + dot_nt(dq_ref[...], w_ref[:, :width]) + df1_ref[...]
            out_ref[0] = out.astype(out_ref.dtype)

        if d > 0:

            @pl.when((step // steps == i) & (wanted == 0))
            def _(out_ref=out_ref):
                out_ref[0] = jnp.zeros(out_ref.shape[1:], out_ref.dtype)


def token_grad(meta, need, dk, dv, w, sent, kept, extra, dtype, deps=()):
    _, tokens, width = dk.shape
    steps = need.shape[0] // 2
    size = tokens // steps
    blocks = sent + kept

    def block_of(i):
        d = jnp.int32(blocks[0])
        for at, b in enumerate(blocks):
            d = jnp.where(i // steps == at, b, d)
        return d

    kv_spec = pl.BlockSpec((1, size, width), lambda i, *_: (block_of(i), i % steps, 0))

    def out_spec(first, count):
        def index(i, *_):
            at = jnp.clip(i - first * steps, 0, count * steps - 1)
            return (at // steps, at % steps, 0)

        return pl.BlockSpec((1, size, width), index)

    groups = [(0, len(sent))] + ([(len(sent), len(kept))] if kept else [])
    return pl.pallas_call(
        skipping(
            functools.partial(token_grad_kernel, steps, sent, kept), 5 + len(extra), len(deps)
        ),
        grid_spec=pltpu.PrefetchScalarGridSpec(
            num_scalar_prefetch=2,
            grid=(len(blocks) * steps,),
            in_specs=[kv_spec, kv_spec, pl.BlockSpec(w.shape, lambda i, *_: (0, 0))]
            + [pl.BlockSpec((size, width), lambda i, *_: (i, 0)) for _ in extra]
            + [pl.BlockSpec(memory_space=pl.ANY)] * len(deps),
            out_specs=[out_spec(*g) for g in groups],
        ),
        out_shape=[jax.ShapeDtypeStruct((n, tokens, width), dtype) for _, n in groups],
        compiler_params=params(1),
        cost_estimate=cost(
            4 * len(blocks) * tokens * width * width, 6 * len(blocks) * tokens * width
        ),
        name="token_grad",
    )(meta, need, dk, dv, w, *extra, *deps)


def joint_grad_kernel(blocks, meta, *refs):
    xs = refs[:blocks]
    dq_ref, dk_ref, dv_ref, mine_ref, theirs_ref, sum_ref, acc = refs[blocks:]
    step = pl.program_id(0)
    width = acc.shape[0]
    half = acc.shape[1] // 2

    for d in range(blocks):

        @pl.when(step == d)
        def _(d=d):
            x = xs[d][...].T
            k_part = dot(x, dk_ref[0])
            v_part = dot(x, dv_ref[0])
            v_sum = colsum(dv_ref[0].astype(F32))
            if d == 0:
                acc[:, :width] = dot(x, dq_ref[...])
                acc[:, width : 2 * width] = k_part
                acc[:, 2 * width :] = v_part
                sum_ref[0:1] = colsum(dq_ref[...].astype(F32))
                sum_ref[1:2] = v_sum
            else:
                acc[:, width : 2 * width] += k_part
                acc[:, 2 * width :] += v_part
                sum_ref[1:2] += v_sum

    @pl.when(step == blocks - 1)
    def _():
        mine = pl.ds(pl.multiple_of(meta[0] * half, LANES), half)
        theirs = pl.ds(pl.multiple_of((1 - meta[0]) * half, LANES), half)
        for x in range(2):
            for y in range(2):
                for z in range(4):
                    part = pl.ds(pl.multiple_of(chip_of(meta, x, y, z) * SLAB, 8), SLAB)
                    mine_ref[x, y, z] = acc[part, mine]
                    theirs_ref[x, y, z] = acc[part, theirs].astype(BF16)


def joint_grad(meta, xs, dq, dk, dv, deps):
    blocks = len(xs)
    tokens, width = dq.shape
    half = 3 * width // 2
    full = pl.BlockSpec((tokens, width), lambda i, *_: (0, 0))
    kv_spec = pl.BlockSpec((1, tokens, width), lambda i, *_: (i, 0, 0))
    shape = (2, 2, 4, SLAB, half)
    slab_spec = pl.BlockSpec(shape, lambda i, *_: (0, 0, 0, 0, 0))
    return pl.pallas_call(
        skipping(functools.partial(joint_grad_kernel, blocks), blocks + 4, len(deps)),
        grid_spec=pltpu.PrefetchScalarGridSpec(
            num_scalar_prefetch=1,
            grid=(blocks,),
            in_specs=[full] * blocks
            + [full, kv_spec, kv_spec]
            + [pl.BlockSpec(memory_space=pl.ANY)] * len(deps),
            out_specs=[slab_spec, slab_spec, pl.BlockSpec((8, width), lambda i, *_: (0, 0))],
            scratch_shapes=[pltpu.VMEM((width, 3 * width), F32)],
        ),
        out_shape=[
            jax.ShapeDtypeStruct(shape, F32),
            jax.ShapeDtypeStruct(shape, BF16),
            jax.ShapeDtypeStruct((8, width), F32),
        ],
        compiler_params=params(1),
        cost_estimate=cost(
            2 * tokens * width * width * (2 * blocks + 1), 8 * blocks * tokens * width
        ),
        name="joint_grad",
    )(meta, *xs, dq, dk, dv, *deps)


def segment_ids(doc_lengths, total):
    doc_ends = jnp.cumsum(doc_lengths, axis=-1, dtype=jnp.int32)
    places = jnp.arange(total, dtype=jnp.int32)
    return jnp.sum(
        (doc_ends[:, None, :] <= places[None, :, None]).astype(jnp.int32), axis=-1, dtype=jnp.int32
    )


def adam_step(gradient, master, mean_old, square_old, rate, decay):
    momentum = BETA_ONE * mean_old + (1.0 - BETA_ONE) * gradient
    variance = BETA_TWO * square_old + (1.0 - BETA_TWO) * gradient * gradient
    update = (
        momentum / (1.0 - BETA_ONE**STEP) / (jnp.sqrt(variance / (1.0 - BETA_TWO**STEP)) + ADAM_EPS)
    )
    return (master - rate * (update + decay * master), momentum, variance)


def own_part(x, index, axis):
    return lax.dynamic_index_in_dim(x, index, axis, keepdims=False)


def both_halves(own, other, core, axis=-1):
    first = jnp.where(core == 0, own, other)
    second = jnp.where(core == 0, other, own)
    return jnp.concatenate([first, second], axis=axis)


def full_slabs(w, row_groups):
    rows, cols = w.shape
    half = cols // 2
    out = []
    for h in range(2):
        s = w[:, h * half : (h + 1) * half].reshape(4, 2, 2, rows // CHIPS, half)
        s = s.transpose(1, 2, 0, 3, 4)
        if row_groups > 1:
            s = s.reshape(2, 2, 4, rows // CHIPS, row_groups, half // row_groups)
            s = s.transpose(0, 1, 2, 4, 3, 5).reshape(2, 2, 4, -1, half // row_groups)
        out.append(s)
    return out


def slab_list(halves):
    order = np.asarray(GATHER_Z)
    out = []
    for h in halves:
        out += [h[x, y][order] for x in range(2) for y in range(2)]
    return out


def full_weight(halves, row_groups):
    out = []
    for s in halves:
        _, _, _, rows, cols = s.shape
        s = s.reshape(2, 2, 4, row_groups, rows // row_groups, cols)
        s = s.transpose(2, 0, 1, 4, 3, 5)
        out.append(s.reshape(CHIPS * rows // row_groups, row_groups * cols))
    return jnp.concatenate(out, axis=1)


def local(
    tokens,
    doc_lengths,
    teacher,
    cotangent,
    joint_weight,
    output_weight,
    expand_weight,
    shrink_weight,
    vectors,
    joint_mean,
    output_mean,
    expand_mean,
    shrink_mean,
    vector_mean,
    joint_square,
    output_square,
    expand_square,
    shrink_square,
    vector_square,
):
    seq_count = lax.axis_size("seq")
    dp_count = lax.axis_size("dp")
    seq_rank = lax.axis_index("seq")
    dp_rank = lax.axis_index("dp")
    rows, length, width = tokens.shape
    hidden = expand_weight.shape[1]
    spare = hidden // width
    token_total = rows * length
    shard_rows = joint_weight.shape[0]
    half = width // 2
    by_slabs = dp_count == 8 and seq_count == 4 and 2 * shard_rows == SLAB
    core = seq_rank % 2

    segments = segment_ids(doc_lengths, length * seq_count).reshape(rows, seq_count, length)
    seg_rel = jnp.take(segments, jnp.arange(seq_count) ^ seq_rank, axis=1)
    need = (
        (seg_rel[:, :, 0] <= seg_rel[:, :1, -1]) & (seg_rel[:, :, -1] >= seg_rel[:, :1, 0])
    ).astype(jnp.int32)
    segq = jnp.broadcast_to(seg_rel[:, 0, :, None], (rows, length, LANES))
    segk = jnp.broadcast_to(
        seg_rel.transpose(1, 0, 2)[:, :, None, :], (seq_count, rows, 8, length)
    )
    seg_row = jnp.broadcast_to(segments.reshape(rows, 1, -1), (rows, 8, length * seq_count))
    rank_in = jnp.cumsum(need, axis=1)
    slots = jnp.where(need > 0, rank_in - 1, rank_in[:, -1:] + jnp.cumsum(1 - need, axis=1) - 1)
    spots = slots[:, None, :] == jnp.arange(seq_count)[None, :, None]
    order = jnp.sum(spots * jnp.arange(seq_count)[None, None, :], axis=2)
    plan = jnp.concatenate([rank_in[:, -1:], order], axis=1).astype(jnp.int32)

    if by_slabs:
        me_z, me_x, me_y, my_half = dp_rank // 2, dp_rank % 2, seq_rank // 2, core
    else:
        me_z = me_x = me_y = my_half = jnp.zeros((), jnp.int32)
    places = [
        ((me_z ^ z) * 2 + (me_x ^ x)) * 2 + (me_y ^ y) for (x, y, z) in PLACES
    ]
    zero = jnp.zeros((), jnp.int32)
    meta = jnp.stack(
        [my_half, zero, zero, seq_rank, *places, me_z, me_x, me_y]
    ).astype(jnp.int32)
    meta_other = meta.at[0].set(1 - my_half)
    if by_slabs:
        low = joint_weight.astype(BF16)
        vec_low = jnp.pad(vectors.astype(BF16).T, ((0, 0), (0, LANES - vectors.shape[0])))
        joint_halves = low.reshape(shard_rows, 2, -1).transpose(1, 0, 2)
        joint_own = jnp.concatenate([own_part(joint_halves, core, 0), vec_low], axis=1)
        joint_send = jnp.concatenate([own_part(joint_halves, 1 - core, 0), vec_low], axis=1)
        joint_got = swap(joint_send, "seq", 1)
        joint_piece = jnp.where(
            core == 0,
            jnp.concatenate([joint_own, joint_got]),
            jnp.concatenate([joint_got, joint_own]),
        )
        lot = rows - 1
        tokens_y = swap(tokens[:lot], "seq", 2)
        joint_pair = jnp.stack([joint_piece, swap(joint_piece, "dp", 4)])
        rest_weights = after((expand_weight, output_weight, shrink_weight), joint_piece)
        expand_low, output_low, shrink_low = (w.astype(BF16) for w in rest_weights)
        expand_halves = expand_low.reshape(shard_rows, 2, spare, half)
        expand_halves = expand_halves.transpose(1, 2, 0, 3).reshape(2, spare * shard_rows, half)
        output_halves = output_low.reshape(shard_rows, 2, half).transpose(1, 0, 2)
        shrink_halves = shrink_low.reshape(-1, 2, half).transpose(1, 0, 2)
        rest = jnp.concatenate([expand_halves, output_halves, shrink_halves], axis=1)
        rest_own = own_part(rest, core, 0)
        rest_got = swap(own_part(rest, 1 - core, 0), "seq", 1)
        pair = jnp.where(
            core == 0, jnp.stack([rest_own, rest_got]), jnp.stack([rest_got, rest_own])
        )
        cut = spare * shard_rows
        expand_piece = pair[:, :cut].reshape(2, spare, shard_rows, half)
        rest_piece = jnp.concatenate(
            [
                expand_piece.transpose(1, 0, 2, 3).reshape(-1, half),
                pair[:, cut : cut + shard_rows].reshape(-1, half),
                pair[:, cut + shard_rows :].reshape(-1, half),
            ]
        )
        joint_z = jnp.concatenate([joint_pair, swap(joint_pair, "dp", 2)])
        joint_z, rest_piece = stage(joint_z, rest_piece)
        shares = [share(teacher, segq, seg_row, 0, 2, (joint_z,))]
        joint_y, joint_x, rest_got, tokens_y, shares[0] = stage(
            swap(joint_z, "seq", 2),
            swap(joint_z, "dp", 1),
            swap(rest_piece, "dp", 4),
            tokens_y,
            shares[0],
        )
        rest_pair = jnp.stack([rest_piece, rest_got])
        shares.append(share(teacher, segq, seg_row, 2, 2, (joint_x, joint_y, shares[0])))
        joint_xy, rest_got, tokens_last, tokens_core, core_z, core_y, core_x, shares[1] = stage(
            swap(joint_y, "dp", 1),
            swap(rest_pair, "dp", 2),
            swap(after(tokens[lot:], joint_y), "seq", 2),
            swap(tokens, "seq", 1),
            swap(joint_z, "seq", 1),
            swap(joint_y, "seq", 1),
            swap(joint_x, "seq", 1),
            shares[1],
        )
        tokens_y = jnp.concatenate([tokens_y, tokens_last])
        core_xy, tokens_far = stage(swap(joint_xy, "seq", 1), swap(tokens_y, "seq", 1))
        got = {0: tokens, 1: tokens_core, 2: tokens_y, 3: tokens_far}
        joint_slabs = [joint_z, joint_y, joint_x, joint_xy, core_z, core_y, core_x, core_xy]
        rest_z = jnp.concatenate([rest_pair, rest_got])
        rest_y = swap(rest_z, "seq", 2)
        rest_x = swap(rest_z, "dp", 1)
        vec_slabs = jnp.stack([t[..., -LANES:] for t in joint_slabs[:4]])
        vec_slabs = vec_slabs.reshape(CHIPS, SLAB, LANES)
        spots = np.argsort([(z * 2 + x) * 2 + y for (x, y, z) in PLACES])
        me_chip = (me_z * 2 + me_x) * 2 + me_y
        order = jnp.asarray(spots, jnp.int32)[jnp.arange(CHIPS, dtype=jnp.int32) ^ me_chip]
        vec_f = jnp.take(vec_slabs, order, axis=0).reshape(width, LANES).T[: vectors.shape[0]]
    else:
        joint_full, output_full, expand_full, shrink_full = (
            lax.all_gather(w.astype(BF16), ("dp", "seq"), axis=0, tiled=True)
            for w in (joint_weight, output_weight, expand_weight, shrink_weight)
        )
        vec_f = lax.all_gather(vectors.astype(BF16), ("dp", "seq"), axis=1, tiled=True)
        joint_parts = full_slabs(joint_full, 1)
        joint_slabs = slab_list(joint_parts)
        rest_parts = [
            jnp.concatenate(p, axis=3)
            for p in zip(
                full_slabs(expand_full, spare), full_slabs(output_full, 1), full_slabs(shrink_full, 1)
            )
        ]
        rest_slabs = slab_list(rest_parts)
    vec_f = vec_f.astype(F32)
    vec_pad = jnp.pad(vec_f, ((0, -vec_f.shape[0] % 8), (0, 0)))
    fbias = jnp.broadcast_to(vec_f[3 : 3 + spare].reshape(1, hidden), (8, hidden))

    bits = [1 << i for i in range(seq_count.bit_length() - 1)]
    if not by_slabs:
        got = {0: tokens}
        for bit in reversed(bits):
            for d, block in list(got.items()):
                got[d | bit] = swap(block, "seq", bit)
    xs = [got[d] for d in range(seq_count)]

    bias_qv = jnp.pad(vec_f[:2], ((0, 6), (0, 0)))
    flat = lambda t: t.reshape(token_total, t.shape[-1])
    by_rows = lambda t: t.reshape(*t.shape[:-2], rows, length, width)
    if not by_slabs:
        shares = [share(teacher, segq, seg_row, r, 1, ()) for r in range(rows)]
    q_flat, k_flat, v_flat, joint_w = project(
        meta, need, [flat(x) for x in xs], joint_slabs, bias_qv, tuple(shares[-1:])
    )
    q, k, v = by_rows(q_flat), by_rows(k_flat), by_rows(v_flat)
    if by_slabs:
        rest_y, rest_x = after(rest_y, q_flat), after(rest_x, q_flat)
        rest_xya = swap(rest_y[:2], "dp", 1)
        rest_xyb = swap(rest_x[2:], "seq", 2)
        rest_slabs = [rest_z, rest_y, rest_x]
        rest_other = [swap(t, "seq", 1) for t in rest_slabs]
    cut = rows // 2
    front = attend(plan, q, k, v, segq, segk, 0, cut, (), ())
    if by_slabs:
        rest_xya, rest_xyb = after(rest_xya, front[0]), after(rest_xyb, front[0])
        rest_xy = jnp.concatenate([rest_xya, rest_xyb])
        rest_slabs = rest_slabs + [rest_xy] + rest_other + [swap(rest_xy, "seq", 1)]
    attended, lse = attend(
        plan, q, k, v, segq, segk, cut, rows - cut, front, (rest_slabs[3],)
    )
    layer_output, d_first, d_att, gl, du, h1, dz, da, gvec, gbias = feed(
        meta, flat(tokens), flat(attended), flat(cotangent), vec_pad, fbias, rest_slabs
    )
    layer_output = by_rows(layer_output)
    grad_args = (h1, du, gl, dz, flat(attended), da)
    rest_theirs = feed_grad(meta_other, *grad_args, None)[0]
    back_args = (
        meta, plan, q, k, v, by_rows(d_att), attended, lse, shares, teacher, segq, segk
    )
    deps = (rest_theirs,)
    if by_slabs:
        rest_got = swap(rest_theirs, "seq", 1)
    grads = ()
    for r in range(rows):
        grads = tuple(attend_back(*back_args, r, grads, deps))
        deps = ()
        if not by_slabs:
            continue
        if r == 0:
            near, next_x, next_y, over_x, over_y = feed_grad(
                meta, *grad_args, after(rest_got, grads[0])
            )
            rest_kept = (near, next_x, next_y)
            got_x, got_y = swap(over_x, "dp", 1), swap(over_y, "seq", 2)
            deps = (over_x, over_y)
        if r == rows - 2:
            got_x, got_y, _ = stage(got_x, got_y, grads[0])
            rest_near, over_x, over_y = add_first(rest_kept, got_x, got_y)
            got_x, got_y = swap(over_x, "dp", 1), swap(over_y, "seq", 2)
            deps = (over_x, over_y)
    dq, dk, dv = grads
    if not by_slabs:
        nothing = jnp.zeros(rest_theirs.shape, BF16)
        near, next_x, next_y, over_x, over_y = feed_grad(meta, *grad_args, nothing)
        over_x, over_y = over_x.astype(F32), over_y.astype(F32)
        rest_mine = jnp.stack(
            [
                jnp.stack([near, jnp.concatenate([next_y, over_y[1]])]),
                jnp.stack(
                    [jnp.concatenate([over_x[1], next_x]), jnp.concatenate([over_x[0], over_y[0]])]
                ),
            ]
        )
    deps = ()
    if by_slabs:
        got_x, got_y, _ = stage(got_x, got_y, dq)
        rest_near, rest_far = add_second(rest_near, got_x, got_y)
        rest_got = swap(rest_far, "dp", 2)
        deps = (rest_far,)
    flat_kv = lambda t: t.reshape(seq_count, token_total, width)
    dq, dk, dv = flat(dq), flat_kv(dk), flat_kv(dv)
    joint_mine, joint_theirs, sums = joint_grad(meta, [flat(x) for x in xs], dq, dk, dv, deps)
    grad_vector = jnp.concatenate(
        [sums[:2], gvec[2:3], gbias[0:1].reshape(spare, width), gvec[3:8]], axis=0
    )
    if by_slabs:
        joint_got = swap(joint_theirs, "seq", 1)
        vector_got = swap(grad_vector, "seq", 1)
    odd = tuple(range(1, seq_count, 2))
    even = tuple(range(2, seq_count, 2))
    sent, kept = token_grad(meta, need, dk, dv, joint_w, odd, even, (), BF16)
    deps = ()
    if by_slabs:
        rest_got, joint_got, vector_got, _ = stage(rest_got, joint_got, vector_got, sent)
        joint_kept, over_x, over_y = split_core(joint_mine, joint_got)
        got_x, got_y = swap(over_x, "dp", 1), swap(over_y, "seq", 2)
        grad_vector = grad_vector + vector_got
        vector_got = swap(grad_vector, "dp", 1)
        rest_near, rest_far = add_z(rest_near, rest_got)
        rest_got = swap(rest_far, "dp", 4)
        deps = (over_x, over_y)
    arrived = swap(sent, "seq", 1)
    own_grad = token_grad(meta, need, dk, dv, joint_w, (0,), (), (dq, d_first), F32, deps)[0]
    if by_slabs:
        arrived, got_x, got_y, _ = stage(arrived, got_x, got_y, own_grad)
    held = {0: own_grad[0] + arrived[0].astype(F32)}
    for i, d in enumerate(even):
        held[d] = (kept[i].astype(F32) + arrived[i + 1].astype(F32)).astype(BF16)
    if by_slabs:
        joint_near, over_x, over_y = add_first(joint_kept, got_x, got_y)
        got_x, got_y, rest_got = stage(swap(over_x, "dp", 1), swap(over_y, "seq", 2), rest_got)
        joint_near, joint_far = add_second(joint_near, got_x, got_y)
        joint_got = swap(joint_far, "dp", 2)
        rest_sum = rest_near + rest_got.astype(F32)
        grad_vector = grad_vector + after(vector_got, joint_far)
        vector_got = swap(grad_vector, "seq", 2)
        held[2] = after(held[2], joint_far, vector_got)
    for bit in bits[1:]:
        for d in [d for d in held if d & bit]:
            arrived = swap(held.pop(d).astype(BF16), "seq", bit).astype(F32)
            held[d ^ bit] = held[d ^ bit].astype(F32) + arrived
    token_gradient = held[0].reshape(rows, length, width)
    if by_slabs:
        joint_near, joint_far = add_z(joint_near, joint_got)
        joint_got = swap(joint_far, "dp", 4)
        grad_vector = grad_vector + after(vector_got, joint_far)
        grad_vector = grad_vector + swap(grad_vector, "dp", 2)
        joint_sum = joint_near + joint_got.astype(F32)
        vector_sum = grad_vector + swap(after(grad_vector, joint_sum), "dp", 4)

    cut = spare * SLAB
    if by_slabs:
        rank = dp_rank * seq_count + seq_rank
        shard_cols = vectors.shape[1]
        shard_vector = lax.dynamic_slice_in_dim(vector_sum, rank * shard_cols, shard_cols, 1)
        local_squares = (
            jnp.sum(rest_sum * rest_sum)
            + jnp.sum(joint_sum * joint_sum)
            + jnp.sum(shard_vector * shard_vector)
        )
        expand_sum = rest_sum[:cut].reshape(spare, 2, shard_rows, half).transpose(1, 0, 2, 3)
        rest_cores = jnp.concatenate(
            [
                expand_sum.reshape(2, spare * shard_rows, half),
                rest_sum[cut : cut + SLAB].reshape(2, shard_rows, half),
                rest_sum[cut + SLAB :].reshape(2, -1, half),
            ],
            axis=1,
        )
        joint_cores = joint_sum.reshape(2, shard_rows, -1)
        rest_two = both_halves(
            own_part(rest_cores, core, 0)[None],
            swap(own_part(rest_cores, 1 - core, 0), "seq", 1)[None],
            core,
            axis=0,
        )
        shard_joint = both_halves(
            own_part(joint_cores, core, 0),
            swap(own_part(joint_cores, 1 - core, 0), "seq", 1),
            core,
        )
        cut = spare * shard_rows
        shard_expand = rest_two[:, :cut].reshape(2, spare, shard_rows, half)
        shard_expand = shard_expand.transpose(2, 0, 1, 3).reshape(shard_rows, hidden)
        shard_output = rest_two[:, cut : cut + shard_rows].transpose(1, 0, 2)
        shard_output = shard_output.reshape(shard_rows, width)
        shard_shrink = rest_two[:, cut + shard_rows :].transpose(1, 0, 2).reshape(-1, width)
        square_total = sum_all(local_squares.reshape(1, 1))[0, 0]
    else:
        rest_other = rest_theirs.astype(F32)
        grads = (
            full_weight((joint_mine, joint_theirs.astype(F32)), 1),
            full_weight((rest_mine[..., cut : cut + SLAB, :], rest_other[..., cut : cut + SLAB, :]), 1),
            full_weight((rest_mine[..., :cut, :], rest_other[..., :cut, :]), spare),
            full_weight((rest_mine[..., cut + SLAB :, :], rest_other[..., cut + SLAB :, :]), 1),
        )
        shard_joint, shard_output, shard_expand, shard_shrink = (
            lax.psum_scatter(g, ("dp", "seq"), scatter_dimension=0, tiled=True) for g in grads
        )
        shard_vector = lax.psum_scatter(
            grad_vector, ("dp", "seq"), scatter_dimension=1, tiled=True
        )
        local_squares = sum(
            jnp.sum(g * g)
            for g in (shard_joint, shard_output, shard_expand, shard_shrink, shard_vector)
        )
        square_total = lax.psum(local_squares, ("dp", "seq"))
    gradient_norm = jnp.sqrt(square_total)
    clip_scale = CLIP_LEVEL / (gradient_norm + 1e-06)
    joint_master, joint_momentum, joint_variance = adam_step(
        shard_joint * clip_scale, joint_weight, joint_mean, joint_square, RATE_MATRIX, DECAY
    )
    output_master, output_momentum, output_variance = adam_step(
        shard_output * clip_scale, output_weight, output_mean, output_square, RATE_MATRIX, DECAY
    )
    expand_master, expand_momentum, expand_variance = adam_step(
        shard_expand * clip_scale, expand_weight, expand_mean, expand_square, RATE_MATRIX, DECAY
    )
    shrink_master, shrink_momentum, shrink_variance = adam_step(
        shard_shrink * clip_scale, shrink_weight, shrink_mean, shrink_square, RATE_MATRIX, DECAY
    )
    vector_master, vector_momentum, vector_variance = adam_step(
        shard_vector * clip_scale, vectors, vector_mean, vector_square, RATE_VECTOR, 0.0
    )
    return (
        layer_output,
        token_gradient,
        gradient_norm,
        joint_master,
        output_master,
        expand_master,
        shrink_master,
        vector_master,
        joint_momentum,
        output_momentum,
        expand_momentum,
        shrink_momentum,
        vector_momentum,
        joint_variance,
        output_variance,
        expand_variance,
        shrink_variance,
        vector_variance,
    )


def solution(mesh):
    rows = P(("dp", "seq"), None)
    cols = P(None, ("dp", "seq"))
    state = (rows, rows, rows, rows, cols)
    tokens = P("dp", "seq", None)
    return jax.shard_map(
        local,
        mesh=mesh,
        in_specs=(tokens, P("dp", None), P("dp", None, "seq", None), tokens) + state * 3,
        out_specs=(tokens, tokens, P()) + state * 3,
        check_vma=False,
    )
```

time: 938 us -> 476 us (0.51)
  matrix products: 309 us -> 0 us
  Pallas kernels: 0 us -> 272 us
  waiting for transfers between devices: 282 us -> 52.7 us
  blocking collectives: 123 us -> 0 us
  local copies, waits for them, and re-layouts: 105 us -> 30.8 us
  starting transfers between devices: 8.29 us -> 69.8 us
  other arithmetic: 80.1 us -> 33.3 us
  between operations: 21 us -> 8.48 us
    dot_general x36 -> x0, matrix products: 309 us -> none  [the longest x4 56.5 us: local(): jnp.einsum('rqhd,rkhd->rhqk', d_attended, values_now, preferred_element_t...]
    pallas_call x0 -> x15, Pallas kernels: none -> 272 us  [the longest x4 62.7 us: attend_back(): pl.pallas_call(skipping(functools.partial(attend_back_kernel, blocks, sta...]
    reduce_scatter x4 -> x0, waiting for transfers between devices: 151 us -> none  [the longest x1 123 us: local(): lax.psum_scatter(grad_joint, ('dp', 'seq'), scatter_dimension=0, tiled=True)]
    ppermute x14 -> x53, waiting for transfers between devices: 115 us -> 52.7 us  [swap(): lax.ppermute(x, axis, [(i, i ^ bit) for i in range(lax.axis_size(axis))])]
    ppermute x14 -> x53, starting transfers between devices: 7.96 us -> 69.8 us  [swap(): lax.ppermute(x, axis, [(i, i ^ bit) for i in range(lax.axis_size(axis))])]
    reduce_sum x14 -> x3, other arithmetic: 51.6 us -> 2.58 us  [the longest x1 1.77 us: local(): jnp.sum(rest_sum * rest_sum) + jnp.sum(joint_sum * joint_sum)]
    unnamed x179 -> x103, local copies, waits for them, and re-layouts: 54.4 us -> 10.2 us
    all_gather x1 -> x0, blocking collectives: 43.6 us -> none  [local(): lax.all_gather(vectors.astype(jnp.bfloat16), ('dp', 'seq'), axis=1, tiled...]
  transfers between devices with their start and end apart: 22 -> 53, of which waited for: 13 -> 20; matrix products, arithmetic and copies ran while one was open for 45% -> 9% of each run, Pallas kernels for 0% -> 34%
where the time goes in v1:
time: 476 us; the launch traced here: 467 us
  Pallas kernels  272 us (57%)
  starting transfers between devices  69.8 us (15%)
  waiting for transfers between devices  52.7 us (11%)
  other arithmetic  33.3 us (7%)
  local copies, waits for them, and re-layouts  30.8 us (6%)
  between operations  8.48 us (2%)
    ppermute x53, starting transfers between devices, swap(): lax.ppermute(x, axis, [(i, i ^ bit) for i in range(lax.axis_size(axis))])  69.8 us
    pallas_call x4, Pallas kernels, attend_back(): pl.pallas_call(skipping(functools.partial(attend_back_kernel, blocks, sta...  62.7 us
    ppermute x53, waiting for transfers between devices, swap(): lax.ppermute(x, axis, [(i, i ^ bit) for i in range(lax.axis_size(axis))])  52.7 us
    pallas_call x1, Pallas kernels, feed(): pl.pallas_call(feed_kernel, grid_spec=pltpu.PrefetchScalarGridSpec(num_sc...  48.1 us
    pallas_call x2, Pallas kernels, feed_grad(): pl.pallas_call(functools.partial(feed_grad_kernel, added), grid_spec=pltp...  44 us
    pallas_call x2, Pallas kernels, attend(): pl.pallas_call(skipping(functools.partial(attend_kernel, blocks, start),...  28.4 us
    pallas_call x2, Pallas kernels, share(): pl.pallas_call(skipping(functools.partial(share_kernel, start), 3, len(de...  24.2 us
    pallas_call x2, Pallas kernels, token_grad(): pl.pallas_call(skipping(functools.partial(token_grad_kernel, steps, sent,...  23.6 us
  transfers between devices with their start and end apart: 53, of which 20 were waited for; matrix products, arithmetic and copies ran while one was open for 9% of the time, Pallas kernels for 34%

profile of v1, /device:TPU:0, one launch (start us, length us, event | category | flops | bytes accessed | tf_op | source)
XLA Modules:
  0.0 466.7 jit_solution(1551793856054587856)
XLA Ops:
  4.7 2.9 collective-permute-start.7
  9.9 2.7 collective-permute-start.1
  13.0 5.5 %collective-permute-done.1 = bf16[48,1280]{1,0:T(8,128)(2,1)S(1)} collective-permute-done((bf16[48,1280]{1,0:T(8,128)(2,1)S(1)}, bf16[48,1280]{1,0:T(8,128)(2,1)S(1)}, u32[]{:S(2)}, u32[]{:S(2)}) %collective-permute-start.1) | collective-permute-done | bytes 122912 | tf_op jit(solution)/shard_map/ppermute | solution.py:61
  19.5 5.9 %collective-permute-done.2 = bf16[2,48,1280]{2,1,0:T(8,128)(2,1)S(1)} collective-permute-done((bf16[2,48,1280]{2,1,0:T(8,128)(2,1)S(1)}, bf16[2,48,1280]{2,1,0:T(8,128)(2,1)S(1)}, u32[]{:S(2)}, u32[]{:S(2)}) %collective-permute-start.2) | collective-permute-done | bytes 245792 | tf_op jit(solution)/shard_map/ppermute | solution.py:61
  25.5 1.6 collective-permute-start.5
  27.8 3.3 collective-permute-start.6
  34.0 12.1 %share.2.refs_5_.refs_8_ = f32[2,6,256,128]{3,2,1,0:T(8,128)} custom-call(bf16[4,12,256,1024]{3,2,1,0:T(8,128)(2,1)} %refs_9_.7, s32[4,256,128]{2,1,0:T(8,128)} %broadcast_in_dim.62.refs_1_.refs_4_.refs_10_, s32[4,8,1024]{2,1,0:T(8,128)} %broadcast_in_dim.63.refs_2_, bf16[4,48,1280]{2,1,0:T(8,128)(2,1)} %copy-done.9), custom_call_target="tpu_custom_call" | custom-call | flops 25165824 | bytes 12582912 | tf_op jit(solution)/shard_map/share/pallas_call | solution.py:212
  46.2 1.6 collective-permute-start.10
  48.9 8.9 %collective-permute-done.10 = bf16[1,256,768]{2,1,0:T(8,128)(2,1)S(1)} collective-permute-done((bf16[1,256,768]{2,1,0:T(8,128)(2,1)S(1)}, bf16[1,256,768]{2,1,0:T(8,128)(2,1)S(1)}, u32[]{:S(2)}, u32[]{:S(2)}) %collective-permute-start.10) | collective-permute-done | bytes 393248 | tf_op jit(solution)/shard_map/ppermute | solution.py:61
  57.8 1.8 collective-permute-start.9
  61.4 12.1 %share.3.refs_15_.refs_8_ = f32[2,6,256,128]{3,2,1,0:T(8,128)} custom-call(bf16[4,12,256,1024]{3,2,1,0:T(8,128)(2,1)} %refs_9_.7, s32[4,256,128]{2,1,0:T(8,128)} %broadcast_in_dim.62.refs_1_.refs_4_.refs_10_, s32[4,8,1024]{2,1,0:T(8,128)} %broadcast_in_dim.63.refs_2_, bf16[4,48,1280]{2,1,0:T(8,128)(2,1)} %copy-done.28, ...), custom_call_target="tpu_custom_call" | custom-call | flops 25165824 | bytes 12582912 | tf_op jit(solution)/shard_map/share/pallas_call | solution.py:212
  73.5 2.4 constant_dynamic-update-slice_fusion.1
  78.3 1.3 pad_maximum_fusion.refs_0_
  80.1 1.5 collective-permute-start.17
  84.7 20.9 %project.1 = (bf16[1024,768]{1,0:T(8,128)(2,1)}, bf16[4,1024,768]{2,1,0:T(8,128)(2,1)}, bf16[4,1024,768]{2,1,0:T(8,128)(2,1)}, bf16[768,2304]{1,0:T(8,128)(2,1)}) custom-call(s32[23]{0:T(128)} %stack.146.refs_0_.meta, s32[4,4]{1,0:T(4,128)} %copy-done.38, bf16[1024,768]{1,0:T(8,128)(2,1)} %bitcast.267, bf16[1024,768]{1,0:T(8,128)(2,1)} %bitcast.47.refs_3_.refs_2_, ...), custom_call_target="tpu_custom_call" | custom-call | flops 10871635968 | bytes 12582912 | tf_op jit(solution)/shard_map/project/pallas_call | solution.py:164
  105.7 5.6 %collective-permute-done.19.refs_2_ = bf16[4,432,384]{2,1,0:T(8,128)(2,1)} collective-permute-done((bf16[4,432,384]{2,1,0:T(8,128)(2,1)S(1)}, bf16[4,432,384]{2,1,0:T(8,128)(2,1)}, u32[]{:S(2)}, u32[]{:S(2)}) %collective-permute-start.19) | collective-permute-done | bytes 1327136 | tf_op jit(solution)/shard_map/ppermute | solution.py:61
  111.5 1.2 slice.232
  112.7 2.0 slice.233
  114.7 1.5 collective-permute-start.20
  116.2 1.5 collective-permute-start.18
  119.5 14.4 %attend.2 = (bf16[4,256,768]{2,1,0:T(8,128)(2,1)}, f32[4,6,256,128]{3,2,1,0:T(8,128)}) custom-call(s32[4,5]{1,0:T(4,128)} %pad_add_fusion.refs_0_.refs_1_, bf16[4,256,768]{2,1,0:T(8,128)(2,1)} %bitcast.252, bf16[4,4,256,768]{3,2,1,0:T(8,128)(2,1)} %bitcast.237, bf16[4,4,256,768]{3,2,1,0:T(8,128)(2,1)} %bitcast.243, ...), custom_call_target="tpu_custom_call" | custom-call | flops 6442450944 | bytes 3145728 | tf_op jit(solution)/shard_map/attend/pallas_call | solution.py:321
  135.8 2.6 collective-permute-start.24
  139.1 14.0 %attend.3 = (bf16[4,256,768]{2,1,0:T(8,128)(2,1)}, f32[4,6,256,128]{3,2,1,0:T(8,128)}) custom-call(s32[4,5]{1,0:T(4,128)} %pad_add_fusion.refs_0_.refs_1_, bf16[4,256,768]{2,1,0:T(8,128)(2,1)} %bitcast.253, bf16[4,4,256,768]{3,2,1,0:T(8,128)(2,1)} %bitcast.238, bf16[4,4,256,768]{3,2,1,0:T(8,128)(2,1)} %bitcast.244, ...), custom_call_target="tpu_custom_call", output_to_operand_aliasing={{0}: (6, {}), {1}: (7, {})} | custom-call | flops 6442450944 | bytes 3145728 | tf_op jit(solution)/shard_map/attend/pallas_call | solution.py:321
  154.2 48.1 %feed.1 = (bf16[1024,768]{1,0:T(8,128)(2,1)}, f32[1024,768]{1,0:T(8,128)}, bf16[1024,768]{1,0:T(8,128)(2,1)}, bf16[1024,3072]{1,0:T(8,128)(2,1)}, bf16[1024,3072...) custom-call(s32[23]{0:T(128)} %stack.146.refs_0_.meta, ...), custom_call_target="tpu_custom_call" | custom-call | flops 21743271936 | bytes 28311552 | tf_op jit(solution)/shard_map/feed/pallas_call | solution.py:569
  202.3 20.3 %feed_grad.2.refs_12_ = bf16[2,2,4,432,384]{4,3,2,1,0:T(8,128)(2,1)} custom-call(s32[23]{0:T(128)} %copy-done.46, bf16[1024,768]{1,0:T(8,128)(2,1)} %get-tuple-element.147.h1_ref, bf16[1024,3072]{1,0:T(8,128)(2,1)} %get-tuple-element.148.du_ref, bf16[1024,3072]{1,0:T(8,128)(2,1)} %get-tuple-element.149.gl_ref, bf16[1024,768]{1,0:T(8,128)(2,1)} %get-tuple-element.150.dz_ref, ...), custom_call_target="tpu_custom_call" | custom-call | flops 5435817984 | bytes 12582912 | tf_op jit(solution)/shard_map/feed_grad/pallas_call | solution.py:688
  222.6 2.1 collective-permute-start.25
  224.7 18.4 %attend_back.4 = (bf16[4,256,768]{2,1,0:T(8,128)(2,1)}, bf16[4,4,256,768]{3,2,1,0:T(8,128)(2,1)}, bf16[4,4,256,768]{3,2,1,0:T(8,128)(2,1)}) custom-call(s32[23]{0:T(128)} %stack.146.refs_0_.meta, s32[4,5]{1,0:T(4,128)} %pad_add_fusion.refs_0_.refs_1_, bf16[4,256,768]{2,1,0:T(8,128)(2,1)} %bitcast.254, bf16[4,4,256,768]{3,2,1,0:T(8,128)(2,1)} %bitcast.239, ...), custom_call_target="tpu_custom_call" | custom-call | flops 8053063680 | bytes 6291456 | tf_op jit(solution)/shard_map/attend_back/pallas_call | solution.py:422
  243.1 23.7 %feed_grad.3 = (f32[4,432,384]{2,1,0:T(8,128)}, f32[2,432,384]{2,1,0:T(8,128)}, f32[2,432,384]{2,1,0:T(8,128)}, bf16[2,2,432,384]{3,2,1,0:T(8,128)(2,1)}, bf16[2,2,432,384]{3,2,1,0:T(8,128)(2,1)}) custom-call(s32[23]{0:T(128)} %stack.146.refs_0_.meta, bf16[1024,768]{1,0:T(8,128)(2,1)} %get-tuple-element.147.h1_ref, ...), custom_call_target="tpu_custom_call" | custom-call | flops 5435817984 | bytes 12582912 | tf_op jit(solution)/shard_map/feed_grad/pallas_call | solution.py:688
  266.8 12.8 %attend_back.5 = (bf16[4,256,768]{2,1,0:T(8,128)(2,1)}, bf16[4,4,256,768]{3,2,1,0:T(8,128)(2,1)}, bf16[4,4,256,768]{3,2,1,0:T(8,128)(2,1)}) custom-call(s32[23]{0:T(128)} %stack.146.refs_0_.meta, s32[4,5]{1,0:T(4,128)} %pad_add_fusion.refs_0_.refs_1_, bf16[4,256,768]{2,1,0:T(8,128)(2,1)} %bitcast.255, ...), custom_call_target="tpu_custom_call", output_to_operand_aliasing={{0}: (12, {}), {1}: (13, {}), {2}: (14, {})} | custom-call | flops 8053063680 | bytes 6291456 | tf_op jit(solution)/shard_map/attend_back/pallas_call | solution.py:422
  279.7 13.0 %attend_back.6 = (bf16[4,256,768]{2,1,0:T(8,128)(2,1)}, bf16[4,4,256,768]{3,2,1,0:T(8,128)(2,1)}, bf16[4,4,256,768]{3,2,1,0:T(8,128)(2,1)}) custom-call(s32[23]{0:T(128)} %stack.146.refs_0_.meta, s32[4,5]{1,0:T(4,128)} %pad_add_fusion.refs_0_.refs_1_, bf16[4,256,768]{2,1,0:T(8,128)(2,1)} %bitcast.256, ...), custom_call_target="tpu_custom_call", output_to_operand_aliasing={{0}: (12, {}), {1}: (13, {}), {2}: (14, {})} | custom-call | flops 8053063680 | bytes 6291456 | tf_op jit(solution)/shard_map/attend_back/pallas_call | solution.py:422
  292.6 5.5 %collective-permute-done.26 = bf16[2,2,432,384]{3,2,1,0:T(8,128)(2,1)S(1)} collective-permute-done((bf16[2,2,432,384]{3,2,1,0:T(8,128)(2,1)}, bf16[2,2,432,384]{3,2,1,0:T(8,128)(2,1)S(1)}, u32[]{:S(2)}, u32[]{:S(2)}) %collective-permute-start.26) | collective-permute-done | bytes 1327136 | tf_op jit(solution)/shard_map/ppermute | solution.py:61
  300.7 1.8 collective-permute-start.28
  302.9 1.3 copy-done.2
  304.2 8.1 %collective-permute-start.29 = (bf16[2,432,384]{2,1,0:T(8,128)(2,1)S(1)}, bf16[2,432,384]{2,1,0:T(8,128)(2,1)}, u32[]{:S(2)}, u32[]{:S(2)}) collective-permute-start(bf16[2,432,384]{2,1,0:T(8,128)(2,1)S(1)} %fusion.6.refs_16_), channel_id=1, source_target_pairs={{0,2},{1,3},{2,0},{3,1},{4,6},{5,7},{6,4},{7,5},{8,10},{9,11},{10,... | collective-permute-start | bytes 1990664 | tf_op jit(solution)/shard_map/ppermute | solution.py:61
  312.3 18.6 %attend_back.7 = (bf16[4,256,768]{2,1,0:T(8,128)(2,1)}, bf16[4,4,256,768]{3,2,1,0:T(8,128)(2,1)}, bf16[4,4,256,768]{3,2,1,0:T(8,128)(2,1)}) custom-call(s32[23]{0:T(128)} %stack.146.refs_0_.meta, s32[4,5]{1,0:T(4,128)} %pad_add_fusion.refs_0_.refs_1_, bf16[4,256,768]{2,1,0:T(8,128)(2,1)} %bitcast.257, ...), custom_call_target="tpu_custom_call", output_to_operand_aliasing={{0}: (12, {}), {1}: (13, {}), {2}: (14, {})} | custom-call | flops 8053063680 | bytes 6291456 | tf_op jit(solution)/shard_map/attend_back/pallas_call | solution.py:422
  330.9 2.8 fusion.4
  336.2 19.7 %joint_grad.1 = (f32[2,2,4,48,1152]{4,3,2,1,0:T(8,128)}, bf16[2,2,4,48,1152]{4,3,2,1,0:T(8,128)(2,1)}, f32[8,768]{1,0:T(8,128)}) custom-call(s32[23]{0:T(128)} %stack.146.refs_0_.meta, bf16[1024,768]{1,0:T(8,128)(2,1)} %bitcast.269, bf16[1024,768]{1,0:T(8,128)(2,1)} %bitcast.47.refs_3_.refs_2_, bf16[1024,768]{1,0:T(8,128)(2,1)} %bitcast.48.refs_4_.refs_3_, ...), custom_call_target="tpu_custom_call" | custom-call | flops 10871635968 | bytes 25165824 | tf_op jit(solution)/shard_map/joint_grad/pallas_call | solution.py:826
  356.0 14.0 %token_grad.2 = (bf16[2,1024,768]{2,1,0:T(8,128)(2,1)}, bf16[1,1024,768]{2,1,0:T(8,128)(2,1)}) custom-call(s32[23]{0:T(128)} %stack.146.refs_0_.meta, s32[4,4]{1,0:T(4,128)} %copy-done.38, bf16[4,1024,768]{2,1,0:T(8,128)(2,1)} %bitcast.232, bf16[4,1024,768]{2,1,0:T(8,128)(2,1)} %bitcast.235, bf16[768,2304]{1,0:T(8,128)(2,1)} %get-tuple-element.170.refs_4_), custom_call_target="tpu_custom_call" | custom-call | flops 7247757312 | bytes 14155776 | tf_op jit(solution)/shard_map/token_grad/pallas_call | solution.py:759
  372.3 3.5 collective-permute-done.32
  375.8 1.6 collective-permute-start.39
  377.4 3.0 fusion.47
  380.5 1.4 collective-permute-start.34
  384.5 9.6 %token_grad.3 = f32[1,1024,768]{2,1,0:T(8,128)} custom-call(s32[23]{0:T(128)} %stack.146.refs_0_.meta, s32[4,4]{1,0:T(4,128)} %copy-done.38, bf16[4,1024,768]{2,1,0:T(8,128)(2,1)} %bitcast.233, bf16[4,1024,768]{2,1,0:T(8,128)(2,1)} %bitcast.236, bf16[768,2304]{1,0:T(8,128)(2,1)} %get-tuple-element.170.refs_4_, bf16[1024,768]{1,0:T(8,128)(2,1)} %bitcast.263, ...), custom_call_target="tpu_custom_call" | custom-call | flops 2415919104 | bytes 4718592 | tf_op jit(solution)/shard_map/token_grad/pallas_call | solution.py:759
  396.1 1.2 convert_element_type.150
  397.4 1.2 collective-permute-start.37
  399.1 3.2 fusion
  402.3 1.6 collective-permute-done.37
  404.9 1.8 multiply_reduce_fusion
  406.9 1.3 collective-permute-start.42
  408.3 1.2 collective-permute-start.40
  409.6 3.3 collective-permute-done.42
  413.0 2.4 collective-permute-start.43
  415.4 1.6 collective-permute-start.44
  417.9 2.1 collective-permute-done.44
  423.8 1.9 collective-permute-done.45
  428.8 1.5 collective-permute-start.47
  430.4 2.0 collective-permute-done.47
  433.0 2.4 collective-permute-start.48
  437.2 3.0 collective-permute-start.49
  440.2 1.4 collective-permute-done.49
  442.2 10.3 %collective-permute-start.50 = (f32[1,1]{1,0:T(1,128)}, f32[1,1]{1,0:T(1,128)}, u32[]{:S(2)}, u32[]{:S(2)}) collective-permute-start(f32[1,1]{1,0:T(1,128)} %add.449), channel_id=1, source_target_pairs={{0,2},{1,3},{2,0},{3,1},{4,6},{5,7},{6,4},{7,5},{8,10},{9,11},{10,... | collective-permute-start | bytes 20 | tf_op jit(solution)/shard_map/ppermute | solution.py:61
  452.5 1.6 collective-permute-done.50
  455.8 2.1 multiply_subtract_fusion.1
  461.5 3.6 bitcast_add_fusion
  (296 shorter events, 51.1 us)
Async XLA Ops:
  2.9 9.6 %copy-start.30 = (f32[24,768]{1,0:T(8,128)S(1)}, f32[24,768]{1,0:T(8,128)}, u32[]{:S(2)}) copy-start(f32[24,768]{1,0:T(8,128)} %param.27) | copy-start | bytes 221188
  2.9 9.6 %copy-start.19 = (f32[24,3072]{1,0:T(8,128)S(1)}, f32[24,3072]{1,0:T(8,128)}, u32[]{:S(2)}) copy-start(f32[24,3072]{1,0:T(8,128)} %param.28) | copy-start | bytes 884740
  3.0 6.9 %collective-permute-start = (bf16[24,1280]{1,0:T(8,128)(2,1)S(1)}, bf16[24,1280]{1,0:T(8,128)(2,1)S(1)}, u32[]{:S(2)}, u32[]{:S(2)}) collective-permute-start(bf16[24,1280]{1,0:T(8,128)(2,1)S(1)} %get-tuple-element.250), channel_id=1, source_target_pairs={{0,1},{1,0},{2,3},{3,2},{4,5},{5,4},{6,7},{7,6},{8,9},{9,8},{10,11... | collective-permute-start | bytes 184328 | tf_op jit(solution)/shard_map/ppermute | solution.py:61
  3.5 72.4 %collective-permute-start.11 = (bf16[4,256,768]{2,1,0:T(8,128)(2,1)S(1)}, bf16[4,256,768]{2,1,0:T(8,128)(2,1)}, u32[]{:S(2)}, u32[]{:S(2)}) collective-permute-start(bf16[4,256,768]{2,1,0:T(8,128)(2,1)S(1)} %copy-done.12), channel_id=1, source_target_pairs={{0,1},{1,0},{2,3},{3,2},{4,5},{5,4},{6,7},{7,6},{8,9},{9,8},{10,11... | collective-permute-start | bytes 4718600 | tf_op jit(solution)/shard_map/ppermute | solution.py:61
  4.7 41.5 %collective-permute-start.7 = (bf16[3,256,768]{2,1,0:T(8,128)(2,1)}, bf16[3,256,768]{2,1,0:T(8,128)(2,1)}, u32[]{:S(2)}, u32[]{:S(2)}) collective-permute-start(bf16[3,256,768]{2,1,0:T(8,128)(2,1)} %slice.223), channel_id=1, source_target_pairs={{0,2},{1,3},{2,0},{3,1},{4,6},{5,7},{6,4},{7,5},{8,10},{9,11},{10,... | collective-permute-start | bytes 3538952 | tf_op jit(solution)/shard_map/ppermute | solution.py:61
  9.9 8.6 %collective-permute-start.1 = (bf16[48,1280]{1,0:T(8,128)(2,1)S(1)}, bf16[48,1280]{1,0:T(8,128)(2,1)S(1)}, u32[]{:S(2)}, u32[]{:S(2)}) collective-permute-start(bf16[48,1280]{1,0:T(8,128)(2,1)S(1)} %maximum_select_fusion.2), channel_id=1, source_target_pairs={{0,16},{4,20},{8,24},{12,28},{16,0},{20,4},{24,8},{28,12},{1,17},{... | collective-permute-start | bytes 368648 | tf_op jit(solution)/shard_map/ppermute | solution.py:61
  12.9 6.4 %collective-permute-start.3 = (bf16[216,384]{1,0:T(8,128)(2,1)S(1)}, bf16[216,384]{1,0:T(8,128)(2,1)S(1)}, u32[]{:S(2)}, u32[]{:S(2)}) collective-permute-start(bf16[216,384]{1,0:T(8,128)(2,1)S(1)} %get-tuple-element.244), channel_id=1, source_target_pairs={{0,1},{1,0},{2,3},{3,2},{4,5},{5,4},{6,7},{7,6},{8,9},{9,8},{10,11... | collective-permute-start | bytes 497672 | tf_op jit(solution)/shard_map/ppermute | solution.py:61
  18.5 6.9 %collective-permute-start.2 = (bf16[2,48,1280]{2,1,0:T(8,128)(2,1)S(1)}, bf16[2,48,1280]{2,1,0:T(8,128)(2,1)S(1)}, u32[]{:S(2)}, u32[]{:S(2)}) collective-permute-start(bf16[2,48,1280]{2,1,0:T(8,128)(2,1)S(1)} %pad_maximum_fusion.10), channel_id=1, source_target_pairs={{0,8},{4,12},{8,0},{12,4},{16,24},{20,28},{24,16},{28,20},{1,9},{5... | collective-permute-start | bytes 737288 | tf_op jit(solution)/shard_map/ppermute | solution.py:61
  25.5 8.5 %copy-start.9 = (bf16[4,48,1280]{2,1,0:T(8,128)(2,1)}, bf16[4,48,1280]{2,1,0:T(8,128)(2,1)S(1)}, u32[]{:S(2)}) copy-start(bf16[4,48,1280]{2,1,0:T(8,128)(2,1)S(1)} %pad_maximum_fusion.4.refs_3_.refs_6_) | copy-start | bytes 1474564
  25.5 20.6 %collective-permute-start.5 = (bf16[4,48,1280]{2,1,0:T(8,128)(2,1)S(1)}, bf16[4,48,1280]{2,1,0:T(8,128)(2,1)S(1)}, u32[]{:S(2)}, u32[]{:S(2)}) collective-permute-start(bf16[4,48,1280]{2,1,0:T(8,128)(2,1)S(1)} %pad_maximum_fusion.4.refs_3_.refs_6_), channel_id=1, source_target_pairs={{0,4},{4,0},{8,12},{12,8},{16,20},{20,16},{24,28},{28,24},{1,5},{5... | collective-permute-start | bytes 1474568 | tf_op jit(solution)/shard_map/ppermute | solution.py:61
  27.1 19.1 %collective-permute-start.4 = (bf16[4,48,1280]{2,1,0:T(8,128)(2,1)S(1)}, bf16[4,48,1280]{2,1,0:T(8,128)(2,1)}, u32[]{:S(2)}, u32[]{:S(2)}) collective-permute-start(bf16[4,48,1280]{2,1,0:T(8,128)(2,1)S(1)} %pad_maximum_fusion.4.refs_3_.refs_6_), channel_id=1, source_target_pairs={{0,2},{1,3},{2,0},{3,1},{4,6},{5,7},{6,4},{7,5},{8,10},{9,11},{10,... | collective-permute-start | bytes 1474568 | tf_op jit(solution)/shard_map/ppermute | solution.py:61
  27.6 20.1 %copy-start.38 = (s32[4,4]{1,0:T(4,128)}, s32[4,4]{1,0:T(4,128)S(1)}, u32[]{:S(2)}) copy-start(s32[4,4]{1,0:T(4,128)S(1)} %get-tuple-element.222.refs_1_) | copy-start | bytes 196
  27.8 18.3 %collective-permute-start.6 = (bf16[432,384]{1,0:T(8,128)(2,1)S(1)}, bf16[432,384]{1,0:T(8,128)(2,1)S(1)}, u32[]{:S(2)}, u32[]{:S(2)}) collective-permute-start(bf16[432,384]{1,0:T(8,128)(2,1)S(1)} %pad_maximum_fusion.8), channel_id=1, source_target_pairs={{0,16},{4,20},{8,24},{12,28},{16,0},{20,4},{24,8},{28,12},{1,17},{... | collective-permute-start | bytes 995336 | tf_op jit(solution)/shard_map/ppermute | solution.py:61
  34.0 12.2 %copy-start.29 = (bf16[1,256,768]{2,1,0:T(8,128)(2,1)S(1)}, bf16[1,256,768]{2,1,0:T(8,128)(2,1)}, u32[]{:S(2)}) copy-start(bf16[1,256,768]{2,1,0:T(8,128)(2,1)} %slice.225) | copy-start | bytes 1179652
  46.1 2.6 collective-permute-start.12
  46.2 11.6 %collective-permute-start.10 = (bf16[1,256,768]{2,1,0:T(8,128)(2,1)S(1)}, bf16[1,256,768]{2,1,0:T(8,128)(2,1)S(1)}, u32[]{:S(2)}, u32[]{:S(2)}) collective-permute-start(bf16[1,256,768]{2,1,0:T(8,128)(2,1)S(1)} %copy-done.29), channel_id=1, source_target_pairs={{0,2},{1,3},{2,0},{3,1},{4,6},{5,7},{6,4},{7,5},{8,10},{9,11},{10,... | collective-permute-start | bytes 1179656 | tf_op jit(solution)/shard_map/ppermute | solution.py:61
  47.9 27.9 %collective-permute-start.13 = (bf16[4,48,1280]{2,1,0:T(8,128)(2,1)}, bf16[4,48,1280]{2,1,0:T(8,128)(2,1)}, u32[]{:S(2)}, u32[]{:S(2)}) collective-permute-start(bf16[4,48,1280]{2,1,0:T(8,128)(2,1)} %collective-permute-done.4.refs_4_.refs_7_), channel_id=1, source_target_pairs={{0,1},{1,0},{2,3},{3,2},{4,5},{5,4},{6,7},{7,6},{8,9},{9,8},{10,11... | collective-permute-start | bytes 1474568 | tf_op jit(solution)/shard_map/ppermute | solution.py:61
  48.1 27.7 %collective-permute-start.8 = (bf16[4,48,1280]{2,1,0:T(8,128)(2,1)}, bf16[4,48,1280]{2,1,0:T(8,128)(2,1)}, u32[]{:S(2)}, u32[]{:S(2)}) collective-permute-start(bf16[4,48,1280]{2,1,0:T(8,128)(2,1)} %collective-permute-done.4.refs_4_.refs_7_), channel_id=1, source_target_pairs={{0,4},{4,0},{8,12},{12,8},{16,20},{20,16},{24,28},{28,24},{1,5},{5... | collective-permute-start | bytes 1474568 | tf_op jit(solution)/shard_map/ppermute | solution.py:61
  48.8 10.8 %copy-start.48 = (bf16[4,48,1280]{2,1,0:T(8,128)(2,1)}, bf16[4,48,1280]{2,1,0:T(8,128)(2,1)S(1)}, u32[]{:S(2)}) copy-start(bf16[4,48,1280]{2,1,0:T(8,128)(2,1)S(1)} %collective-permute-done.12.refs_10_) | copy-start | bytes 1474564
  48.8 27.1 %collective-permute-start.14 = (bf16[4,48,1280]{2,1,0:T(8,128)(2,1)}, bf16[4,48,1280]{2,1,0:T(8,128)(2,1)}, u32[]{:S(2)}, u32[]{:S(2)}) collective-permute-start(bf16[4,48,1280]{2,1,0:T(8,128)(2,1)} %copy-done.28), channel_id=1, source_target_pairs={{0,1},{1,0},{2,3},{3,2},{4,5},{5,4},{6,7},{7,6},{8,9},{9,8},{10,11... | collective-permute-start | bytes 1474568 | tf_op jit(solution)/shard_map/ppermute | solution.py:61
  57.8 18.1 %collective-permute-start.9 = (bf16[2,432,384]{2,1,0:T(8,128)(2,1)S(1)}, bf16[2,432,384]{2,1,0:T(8,128)(2,1)}, u32[]{:S(2)}, u32[]{:S(2)}) collective-permute-start(bf16[2,432,384]{2,1,0:T(8,128)(2,1)S(1)} %pad_maximum_fusion.1), channel_id=1, source_target_pairs={{0,8},{4,12},{8,0},{12,4},{16,24},{20,28},{24,16},{28,20},{1,9},{5... | collective-permute-start | bytes 1990664 | tf_op jit(solution)/shard_map/ppermute | solution.py:61
  76.7 7.3 %collective-permute-start.16 = (bf16[4,256,768]{2,1,0:T(8,128)(2,1)}, bf16[4,256,768]{2,1,0:T(8,128)(2,1)}, u32[]{:S(2)}, u32[]{:S(2)}) collective-permute-start(bf16[4,256,768]{2,1,0:T(8,128)(2,1)} %constant_dynamic-update-slice_fusion), channel_id=1, source_target_pairs={{0,1},{1,0},{2,3},{3,2},{4,5},{5,4},{6,7},{7,6},{8,9},{9,8},{10,11... | collective-permute-start | bytes 4718600 | tf_op jit(solution)/shard_map/ppermute | solution.py:61
  79.6 38.8 %copy-start.16 = (bf16[4,432,384]{2,1,0:T(8,128)(2,1)}, bf16[4,432,384]{2,1,0:T(8,128)(2,1)S(1)}, u32[]{:S(2)}) copy-start(bf16[4,432,384]{2,1,0:T(8,128)(2,1)S(1)} %pad_maximum_fusion.refs_0_) | copy-start | bytes 3981316
  79.6 31.7 %collective-permute-start.19 = (bf16[4,432,384]{2,1,0:T(8,128)(2,1)S(1)}, bf16[4,432,384]{2,1,0:T(8,128)(2,1)}, u32[]{:S(2)}, u32[]{:S(2)}) collective-permute-start(bf16[4,432,384]{2,1,0:T(8,128)(2,1)S(1)} %pad_maximum_fusion.refs_0_), channel_id=1, source_target_pairs={{0,4},{4,0},{8,12},{12,8},{16,20},{20,16},{24,28},{28,24},{1,5},{5... | collective-permute-start | bytes 3981320 | tf_op jit(solution)/shard_map/ppermute | solution.py:61
  80.1 31.4 %collective-permute-start.17 = (bf16[4,432,384]{2,1,0:T(8,128)(2,1)S(1)}, bf16[4,432,384]{2,1,0:T(8,128)(2,1)}, u32[]{:S(2)}, u32[]{:S(2)}) collective-permute-start(bf16[4,432,384]{2,1,0:T(8,128)(2,1)S(1)} %pad_maximum_fusion.refs_0_), channel_id=1, source_target_pairs={{0,2},{1,3},{2,0},{3,1},{4,6},{5,7},{6,4},{7,5},{8,10},{9,11},{10,... | collective-permute-start | bytes 3981320 | tf_op jit(solution)/shard_map/ppermute | solution.py:61
  81.7 2.3 collective-permute-start.15
  114.7 19.3 %collective-permute-start.20 = (bf16[2,432,384]{2,1,0:T(8,128)(2,1)}, bf16[2,432,384]{2,1,0:T(8,128)(2,1)S(1)}, u32[]{:S(2)}, u32[]{:S(2)}) collective-permute-start(bf16[2,432,384]{2,1,0:T(8,128)(2,1)} %slice.233), channel_id=1, source_target_pairs={{0,2},{1,3},{2,0},{3,1},{4,6},{5,7},{6,4},{7,5},{8,10},{9,11},{10,... | collective-permute-start | bytes 1990664 | tf_op jit(solution)/shard_map/ppermute | solution.py:61
  116.2 17.7 %collective-permute-start.18 = (bf16[2,432,384]{2,1,0:T(8,128)(2,1)S(1)}, bf16[2,432,384]{2,1,0:T(8,128)(2,1)S(1)}, u32[]{:S(2)}, u32[]{:S(2)}) collective-permute-start(bf16[2,432,384]{2,1,0:T(8,128)(2,1)S(1)} %slice.232), channel_id=1, source_target_pairs={{0,4},{4,0},{8,12},{12,8},{16,20},{20,16},{24,28},{28,24},{1,5},{5... | collective-permute-start | bytes 1990664 | tf_op jit(solution)/shard_map/ppermute | solution.py:61
  118.3 34.7 %collective-permute-start.21 = (bf16[4,432,384]{2,1,0:T(8,128)(2,1)S(1)}, bf16[4,432,384]{2,1,0:T(8,128)(2,1)}, u32[]{:S(2)}, u32[]{:S(2)}) collective-permute-start(bf16[4,432,384]{2,1,0:T(8,128)(2,1)S(1)} %pad_maximum_fusion.refs_0_), channel_id=1, source_target_pairs={{0,1},{1,0},{2,3},{3,2},{4,5},{5,4},{6,7},{7,6},{8,9},{9,8},{10,11... | collective-permute-start | bytes 3981320 | tf_op jit(solution)/shard_map/ppermute | solution.py:61
  118.3 34.8 %collective-permute-start.22 = (bf16[4,432,384]{2,1,0:T(8,128)(2,1)}, bf16[4,432,384]{2,1,0:T(8,128)(2,1)}, u32[]{:S(2)}, u32[]{:S(2)}) collective-permute-start(bf16[4,432,384]{2,1,0:T(8,128)(2,1)} %collective-permute-done.17.refs_1_), channel_id=1, source_target_pairs={{0,1},{1,0},{2,3},{3,2},{4,5},{5,4},{6,7},{7,6},{8,9},{9,8},{10,11... | collective-permute-start | bytes 3981320 | tf_op jit(solution)/shard_map/ppermute | solution.py:61
  118.8 34.3 %collective-permute-start.23 = (bf16[4,432,384]{2,1,0:T(8,128)(2,1)}, bf16[4,432,384]{2,1,0:T(8,128)(2,1)}, u32[]{:S(2)}, u32[]{:S(2)}) collective-permute-start(bf16[4,432,384]{2,1,0:T(8,128)(2,1)} %collective-permute-done.19.refs_2_), channel_id=1, source_target_pairs={{0,1},{1,0},{2,3},{3,2},{4,5},{5,4},{6,7},{7,6},{8,9},{9,8},{10,11... | collective-permute-start | bytes 3981320 | tf_op jit(solution)/shard_map/ppermute | solution.py:61
  135.8 17.3 %collective-permute-start.24 = (bf16[4,432,384]{2,1,0:T(8,128)(2,1)}, bf16[4,432,384]{2,1,0:T(8,128)(2,1)S(1)}, u32[]{:S(2)}, u32[]{:S(2)}) collective-permute-start(bf16[4,432,384]{2,1,0:T(8,128)(2,1)} %constant_dynamic-update-slice_fusion.2.refs_8_.refs_3_), channel_id=1, source_target_pairs={{0,1},{1,0},{2,3},{3,2},{4,5},{5,4},{6,7},{7,6},{8,9},{9,8},{10,11... | collective-permute-start | bytes 3981320 | tf_op jit(solution)/shard_map/ppermute | solution.py:61
  138.4 14.6 %copy-start.46 = (s32[23]{0:T(128)}, s32[23]{0:T(128)S(1)}, u32[]{:S(2)}) copy-start(s32[23]{0:T(128)S(1)} %constant_dynamic-update-slice_fusion.4.meta) | copy-start | bytes 280
  222.6 20.5 %collective-permute-start.25 = (bf16[2,2,4,432,384]{4,3,2,1,0:T(8,128)(2,1)}, bf16[2,2,4,432,384]{4,3,2,1,0:T(8,128)(2,1)}, u32[]{:S(2)}, u32[]{:S(2)}) collective-permute-start(bf16[2,2,4,432,384]{4,3,2,1,0:T(8,128)(2,1)} %feed_grad.2.refs_12_), channel_id=1, source_target_pairs={{0,1},{1,0},{2,3},{3,2},{4,5},{5,4},{6,7},{7,6},{8,9},{9,8},{10,11... | collective-permute-start | bytes 15925256 | tf_op jit(solution)/shard_map/ppermute | solution.py:61
  266.8 31.3 %collective-permute-start.26 = (bf16[2,2,432,384]{3,2,1,0:T(8,128)(2,1)}, bf16[2,2,432,384]{3,2,1,0:T(8,128)(2,1)S(1)}, u32[]{:S(2)}, u32[]{:S(2)}) collective-permute-start(bf16[2,2,432,384]{3,2,1,0:T(8,128)(2,1)} %get-tuple-element.156.refs_15_), channel_id=1, source_target_pairs={{0,4},{4,0},{8,12},{12,8},{16,20},{20,16},{24,28},{28,24},{1,5},{5... | collective-permute-start | bytes 3981320 | tf_op jit(solution)/shard_map/ppermute | solution.py:61
  266.8 31.4 %collective-permute-start.27 = (bf16[2,2,432,384]{3,2,1,0:T(8,128)(2,1)}, bf16[2,2,432,384]{3,2,1,0:T(8,128)(2,1)S(1)}, u32[]{:S(2)}, u32[]{:S(2)}) collective-permute-start(bf16[2,2,432,384]{3,2,1,0:T(8,128)(2,1)} %get-tuple-element.157.refs_16_), channel_id=1, source_target_pairs={{0,2},{1,3},{2,0},{3,1},{4,6},{5,7},{6,4},{7,5},{8,10},{9,11},{10,... | collective-permute-start | bytes 3981320 | tf_op jit(solution)/shard_map/ppermute | solution.py:61
  300.7 30.1 %collective-permute-start.28 = (bf16[2,432,384]{2,1,0:T(8,128)(2,1)S(1)}, bf16[2,432,384]{2,1,0:T(8,128)(2,1)}, u32[]{:S(2)}, u32[]{:S(2)}) collective-permute-start(bf16[2,432,384]{2,1,0:T(8,128)(2,1)S(1)} %fusion.8.refs_15_), channel_id=1, source_target_pairs={{0,4},{4,0},{8,12},{12,8},{16,20},{20,16},{24,28},{28,24},{1,5},{5... | collective-permute-start | bytes 1990664 | tf_op jit(solution)/shard_map/ppermute | solution.py:61
  304.2 8.1 %copy-start.8 = (bf16[2,432,384]{2,1,0:T(8,128)(2,1)}, bf16[2,432,384]{2,1,0:T(8,128)(2,1)S(1)}, u32[]{:S(2)}) copy-start(bf16[2,432,384]{2,1,0:T(8,128)(2,1)S(1)} %fusion.6.refs_16_) | copy-start | bytes 1990660
  304.2 26.7 %collective-permute-start.29 = (bf16[2,432,384]{2,1,0:T(8,128)(2,1)S(1)}, bf16[2,432,384]{2,1,0:T(8,128)(2,1)}, u32[]{:S(2)}, u32[]{:S(2)}) collective-permute-start(bf16[2,432,384]{2,1,0:T(8,128)(2,1)S(1)} %fusion.6.refs_16_), channel_id=1, source_target_pairs={{0,2},{1,3},{2,0},{3,1},{4,6},{5,7},{6,4},{7,5},{8,10},{9,11},{10,... | collective-permute-start | bytes 1990664 | tf_op jit(solution)/shard_map/ppermute | solution.py:61
  336.2 19.7 %copy-start.27 = (bf16[2,432,384]{2,1,0:T(8,128)(2,1)S(1)}, bf16[2,432,384]{2,1,0:T(8,128)(2,1)}, u32[]{:S(2)}) copy-start(bf16[2,432,384]{2,1,0:T(8,128)(2,1)} %pad_maximum_fusion.2.refs_8_) | copy-start | bytes 1990660
  355.9 19.9 %collective-permute-start.31 = (bf16[2,2,4,48,1152]{4,3,2,1,0:T(8,128)(2,1)}, bf16[2,2,4,48,1152]{4,3,2,1,0:T(8,128)(2,1)S(1)}, u32[]{:S(2)}, u32[]{:S(2)}) collective-permute-start(bf16[2,2,4,48,1152]{4,3,2,1,0:T(8,128)(2,1)} %get-tuple-element.177), channel_id=1, source_target_pairs={{0,1},{1,0},{2,3},{3,2},{4,5},{5,4},{6,7},{7,6},{8,9},{9,8},{10,11... | collective-permute-start | bytes 5308424 | tf_op jit(solution)/shard_map/ppermute | solution.py:61
  355.9 19.9 %collective-permute-start.30 = (bf16[2,432,384]{2,1,0:T(8,128)(2,1)S(1)}, bf16[2,432,384]{2,1,0:T(8,128)(2,1)S(1)}, u32[]{:S(2)}, u32[]{:S(2)}) collective-permute-start(bf16[2,432,384]{2,1,0:T(8,128)(2,1)S(1)} %copy-done.27), channel_id=1, source_target_pairs={{0,8},{4,12},{8,0},{12,4},{16,24},{20,28},{24,16},{28,20},{1,9},{5... | collective-permute-start | bytes 1990664 | tf_op jit(solution)/shard_map/ppermute | solution.py:61
  356.0 14.5 %copy-start.40 = (f32[8,768]{1,0:T(8,128)S(1)}, f32[8,768]{1,0:T(8,128)}, u32[]{:S(2)}) copy-start(f32[8,768]{1,0:T(8,128)} %get-tuple-element.179) | copy-start | bytes 73732
  370.0 25.0 %collective-permute-start.33 = (bf16[2,1024,768]{2,1,0:T(8,128)(2,1)}, bf16[2,1024,768]{2,1,0:T(8,128)(2,1)}, u32[]{:S(2)}, u32[]{:S(2)}) collective-permute-start(bf16[2,1024,768]{2,1,0:T(8,128)(2,1)} %get-tuple-element.181), channel_id=1, source_target_pairs={{0,1},{1,0},{2,3},{3,2},{4,5},{5,4},{6,7},{7,6},{8,9},{9,8},{10,11... | collective-permute-start | bytes 9437192 | tf_op jit(solution)/shard_map/ppermute | solution.py:61
  372.2 3.6 collective-permute-start.32
  375.8 32.5 %collective-permute-start.39 = (f32[12,768]{1,0:T(8,128)S(1)}, f32[12,768]{1,0:T(8,128)S(1)}, u32[]{:S(2)}, u32[]{:S(2)}) collective-permute-start(f32[12,768]{1,0:T(8,128)S(1)} %fusion.39), channel_id=1, source_target_pairs={{0,4},{4,0},{8,12},{12,8},{16,20},{20,16},{24,28},{28,24},{1,5},{5... | collective-permute-start | bytes 110600 | tf_op jit(solution)/shard_map/ppermute | solution.py:61
  380.5 13.6 %collective-permute-start.34 = (bf16[2,2,48,1152]{3,2,1,0:T(8,128)(2,1)S(1)}, bf16[2,2,48,1152]{3,2,1,0:T(8,128)(2,1)}, u32[]{:S(2)}, u32[]{:S(2)}) collective-permute-start(bf16[2,2,48,1152]{3,2,1,0:T(8,128)(2,1)S(1)} %pad_maximum_fusion.5.refs_7_), channel_id=1, source_target_pairs={{0,4},{4,0},{8,12},{12,8},{16,20},{20,16},{24,28},{28,24},{1,5},{5... | collective-permute-start | bytes 1327112 | tf_op jit(solution)/shard_map/ppermute | solution.py:61
  382.7 12.3 %collective-permute-start.35 = (bf16[2,2,48,1152]{3,2,1,0:T(8,128)(2,1)}, bf16[2,2,48,1152]{3,2,1,0:T(8,128)(2,1)}, u32[]{:S(2)}, u32[]{:S(2)}) collective-permute-start(bf16[2,2,48,1152]{3,2,1,0:T(8,128)(2,1)} %pad_maximum_fusion.6.refs_8_), channel_id=1, source_target_pairs={{0,2},{1,3},{2,0},{3,1},{4,6},{5,7},{6,4},{7,5},{8,10},{9,11},{10,... | collective-permute-start | bytes 1327112 | tf_op jit(solution)/shard_map/ppermute | solution.py:61
  384.5 17.8 %collective-permute-start.38 = (bf16[432,384]{1,0:T(8,128)(2,1)}, bf16[432,384]{1,0:T(8,128)(2,1)}, u32[]{:S(2)}, u32[]{:S(2)}) collective-permute-start(bf16[432,384]{1,0:T(8,128)(2,1)} %fusion.20), channel_id=1, source_target_pairs={{0,16},{4,20},{8,24},{12,28},{16,0},{20,4},{24,8},{28,12},{1,17},{... | collective-permute-start | bytes 995336 | tf_op jit(solution)/shard_map/ppermute | solution.py:61
  397.4 6.4 %collective-permute-start.37 = (bf16[2,48,1152]{2,1,0:T(8,128)(2,1)S(1)}, bf16[2,48,1152]{2,1,0:T(8,128)(2,1)S(1)}, u32[]{:S(2)}, u32[]{:S(2)}) collective-permute-start(bf16[2,48,1152]{2,1,0:T(8,128)(2,1)S(1)} %get-tuple-element.225), channel_id=1, source_target_pairs={{0,2},{1,3},{2,0},{3,1},{4,6},{5,7},{6,4},{7,5},{8,10},{9,11},{10,... | collective-permute-start | bytes 663560 | tf_op jit(solution)/shard_map/ppermute | solution.py:61
  398.6 6.3 %collective-permute-start.36 = (bf16[2,48,1152]{2,1,0:T(8,128)(2,1)S(1)}, bf16[2,48,1152]{2,1,0:T(8,128)(2,1)S(1)}, u32[]{:S(2)}, u32[]{:S(2)}) collective-permute-start(bf16[2,48,1152]{2,1,0:T(8,128)(2,1)S(1)} %get-tuple-element.226), channel_id=1, source_target_pairs={{0,4},{4,0},{8,12},{12,8},{16,20},{20,16},{24,28},{28,24},{1,5},{5... | collective-permute-start | bytes 663560 | tf_op jit(solution)/shard_map/ppermute | solution.py:61
  406.9 6.0 %collective-permute-start.42 = (bf16[2,48,1152]{2,1,0:T(8,128)(2,1)S(1)}, bf16[2,48,1152]{2,1,0:T(8,128)(2,1)S(1)}, u32[]{:S(2)}, u32[]{:S(2)}) collective-permute-start(bf16[2,48,1152]{2,1,0:T(8,128)(2,1)S(1)} %pad_maximum_fusion.11), channel_id=1, source_target_pairs={{0,8},{4,12},{8,0},{12,4},{16,24},{20,28},{24,16},{28,20},{1,9},{5... | collective-permute-start | bytes 663560 | tf_op jit(solution)/shard_map/ppermute | solution.py:61
  408.3 7.1 %collective-permute-start.40 = (f32[12,768]{1,0:T(8,128)S(1)}, f32[12,768]{1,0:T(8,128)S(1)}, u32[]{:S(2)}, u32[]{:S(2)}) collective-permute-start(f32[12,768]{1,0:T(8,128)S(1)} %add.430), channel_id=1, source_target_pairs={{0,2},{1,3},{2,0},{3,1},{4,6},{5,7},{6,4},{7,5},{8,10},{9,11},{10,... | collective-permute-start | bytes 110600 | tf_op jit(solution)/shard_map/ppermute | solution.py:61
  413.0 7.1 %collective-permute-start.43 = (bf16[48,1152]{1,0:T(8,128)(2,1)S(1)}, bf16[48,1152]{1,0:T(8,128)(2,1)S(1)}, u32[]{:S(2)}, u32[]{:S(2)}) collective-permute-start(bf16[48,1152]{1,0:T(8,128)(2,1)S(1)} %fusion.29), channel_id=1, source_target_pairs={{0,16},{4,20},{8,24},{12,28},{16,0},{20,4},{24,8},{28,12},{1,17},{... | collective-permute-start | bytes 331784 | tf_op jit(solution)/shard_map/ppermute | solution.py:61
  415.4 4.6 collective-permute-start.44
  417.0 5.4 %collective-permute-start.52 = (f32[216,384]{1,0:T(8,128)S(1)}, f32[216,384]{1,0:T(8,128)S(1)}, u32[]{:S(2)}, u32[]{:S(2)}) collective-permute-start(f32[216,384]{1,0:T(8,128)S(1)} %dynamic-slice_bitcast_fusion), channel_id=1, source_target_pairs={{0,1},{1,0},{2,3},{3,2},{4,5},{5,4},{6,7},{7,6},{8,9},{9,8},{10,11... | collective-permute-start | bytes 995336 | tf_op jit(solution)/shard_map/ppermute | solution.py:61
  417.1 44.4 %collective-permute-start.41 = (bf16[1024,768]{1,0:T(8,128)(2,1)}, bf16[1024,768]{1,0:T(8,128)(2,1)S(1)}, u32[]{:S(2)}, u32[]{:S(2)}) collective-permute-start(bf16[1024,768]{1,0:T(8,128)(2,1)} %fusion), channel_id=1, source_target_pairs={{0,2},{1,3},{2,0},{3,1},{4,6},{5,7},{6,4},{7,5},{8,10},{9,11},{10,... | collective-permute-start | bytes 4718600 | tf_op jit(solution)/shard_map/ppermute | solution.py:61
  420.7 5.0 %collective-permute-start.45 = (f32[12,768]{1,0:T(8,128)S(1)}, f32[12,768]{1,0:T(8,128)S(1)}, u32[]{:S(2)}, u32[]{:S(2)}) collective-permute-start(f32[12,768]{1,0:T(8,128)S(1)} %add.441), channel_id=1, source_target_pairs={{0,16},{4,20},{8,24},{12,28},{16,0},{20,4},{24,8},{28,12},{1,17},{... | collective-permute-start | bytes 110600 | tf_op jit(solution)/shard_map/ppermute | solution.py:61
  422.5 38.0 %collective-permute-start.51 = (f32[24,1152]{1,0:T(8,128)}, f32[24,1152]{1,0:T(8,128)S(1)}, u32[]{:S(2)}, u32[]{:S(2)}) collective-permute-start(f32[24,1152]{1,0:T(8,128)} %dynamic-slice_bitcast_fusion.2), channel_id=1, source_target_pairs={{0,1},{1,0},{2,3},{3,2},{4,5},{5,4},{6,7},{7,6},{8,9},{9,8},{10,11... | collective-permute-start | bytes 331784 | tf_op jit(solution)/shard_map/ppermute | solution.py:61
  427.0 1.2 collective-permute-start.46
  428.8 3.6 collective-permute-start.47
  433.0 3.6 collective-permute-start.48
  437.2 4.5 collective-permute-start.49
  442.2 11.9 %collective-permute-start.50 = (f32[1,1]{1,0:T(1,128)}, f32[1,1]{1,0:T(1,128)}, u32[]{:S(2)}, u32[]{:S(2)}) collective-permute-start(f32[1,1]{1,0:T(1,128)} %add.449), channel_id=1, source_target_pairs={{0,2},{1,3},{2,0},{3,1},{4,6},{5,7},{6,4},{7,5},{8,10},{9,11},{10,... | collective-permute-start | bytes 20 | tf_op jit(solution)/shard_map/ppermute | solution.py:61
  (39 other events, 111.8 us)

commit v2 on v1

--- a/solution.py
+++ b/solution.py
@@ -33,11 +33,10 @@
 PLACES = [(x, y, z) for x in range(2) for y in range(2) for z in GATHER_Z]
 
 
-def params(rank, fuse=False):
+def params(rank):
     return pltpu.CompilerParams(
         dimension_semantics=("arbitrary",) * rank,
         vmem_limit_bytes=VMEM_BYTES,
-        fuse_transposed_lhs_in_matmul=fuse,
     )
 
 
@@ -94,13 +93,7 @@
     return near[0] + got[0].astype(F32), (near[1] + got[1].astype(F32)).astype(BF16)
 
 
-def sum_all(v):
-    for axis, bit in (("seq", 1), ("dp", 1), ("dp", 2), ("dp", 4), ("seq", 2)):
-        v = v + swap(v, axis, bit)
-    return v
-
-
-def load_slabs(meta, sources, dest, sems, row_base, rows, cols, col_base, sem_base):
+def slab_copies(meta, sources, dest, sems, row_base, rows, cols, col_base, sem_base):
     copies = []
     for which, source in enumerate(sources):
         half = jnp.bitwise_xor(meta[0], which // 4)
@@ -116,9 +109,17 @@
                     sems.at[sem_base + len(copies)],
                 )
             )
+    return copies
+
+
+def start_all(copies):
     for c in copies:
         c.start()
-    return copies
+
+
+def wait_all(copies):
+    for c in copies:
+        c.wait()
 
 
 def project_kernel(blocks, steps, meta, need, *refs):
@@ -132,10 +133,11 @@
 
     @pl.when(step == 0)
     def _():
-        for c in load_slabs(
+        copies = slab_copies(
             meta, slabs, w_ref, sems, 0, SLAB, half_cols, lambda h: h * half_cols, 0
-        ):
-            c.wait()
+        )
+        start_all(copies)
+        wait_all(copies)
 
     for d in range(blocks):
 
@@ -203,22 +205,23 @@
         mask_scr[...] = jnp.where(same, 1.0, 0.0).astype(BF16)
 
     ones = jnp.ones((keys, LANES), BF16)
-    sums = [dot(teach_ref[0, h] * mask_scr[...], ones) for h in range(2)]
-    out_ref[0, 0] = DISTILL / pick_lanes(sums[0], sums[1])
+    for pair in range(out_ref.shape[1]):
+        sums = [dot(teach_ref[0, 2 * pair + h] * mask_scr[...], ones) for h in range(2)]
+        out_ref[0, pair] = DISTILL / pick_lanes(sums[0], sums[1])
 
 
 def share(teacher, segq, seg_row, start, count, deps):
     _, heads, length, keys = teacher.shape
     return pl.pallas_call(
         skipping(functools.partial(share_kernel, start), 3, len(deps)),
-        grid=(count, heads // 2),
+        grid=(count, 2),
         in_specs=[
-            pl.BlockSpec((1, 2, length, keys), lambda r, p: (r + start, p, 0, 0)),
+            pl.BlockSpec((1, heads // 2, length, keys), lambda r, p: (r + start, p, 0, 0)),
             pl.BlockSpec((1, length, LANES), lambda r, p: (r + start, 0, 0)),
             pl.BlockSpec((1, 8, keys), lambda r, p: (r + start, 0, 0)),
         ]
         + [pl.BlockSpec(memory_space=pl.ANY)] * len(deps),
-        out_specs=pl.BlockSpec((1, 1, length, LANES), lambda r, p: (r, p, 0, 0)),
+        out_specs=pl.BlockSpec((1, heads // 4, length, LANES), lambda r, p: (r, p, 0, 0)),
         scratch_shapes=[pltpu.VMEM((length, keys), BF16)],
         out_shape=jax.ShapeDtypeStruct((count, heads // 2, length, LANES), F32),
         compiler_params=params(2),
@@ -455,6 +458,32 @@
     )
 
 
+ERF_TOP = (
+    -2.72614225801306e-10,
+    2.77068142495902e-08,
+    -2.10102402082508e-06,
+    -5.69250639462346e-05,
+    -7.34990630326855e-04,
+    -2.95459980854025e-03,
+    -1.60960333262415e-02,
+)
+ERF_LOW = (
+    -1.45660718464996e-05,
+    -2.13374055278905e-04,
+    -1.68282697438203e-03,
+    -7.37332916720468e-03,
+    -1.42647390514189e-02,
+)
+
+
+def erf(x):
+    x = jnp.clip(x, -4.0, 4.0)
+    square = x * x
+    top = functools.reduce(lambda acc, c: acc * square + c, ERF_TOP)
+    low = functools.reduce(lambda acc, c: acc * square + c, ERF_LOW)
+    return x * top / low
+
+
 def norm(values):
     centered = values - jnp.mean(values, axis=1, keepdims=True)
     inverse = lax.rsqrt(jnp.mean(centered * centered, axis=1, keepdims=True) + NORM_EPS)
@@ -482,32 +511,37 @@
     half_d = wo.shape[1] // 2
     half_f = we.shape[1] // 2
 
+    we_rows = half_f // half_d * SLAB
+
+    def copies_wo():
+        return slab_copies(meta, sources, wo, sems, we_rows, SLAB, half_d, lambda h: h * half_d, 0)
+
+    def copies_we():
+        copies = []
+        for k in range(half_f // half_d):
+            copies += slab_copies(
+                meta, sources, we, sems, k * SLAB, SLAB, half_d,
+                lambda h, k=k: h * half_f + k * half_d, 2 * CHIPS + len(copies)
+            )
+        return copies
+
+    def copies_ws():
+        return slab_copies(
+            meta, sources, ws, sems, we_rows + SLAB, ws.shape[0] // CHIPS, half_d,
+            lambda h: h * half_d, 2 * CHIPS * (1 + half_f // half_d)
+        )
+
     @pl.when(step == 0)
     def _():
-        copies = []
-        for k in range(half_f // half_d):
-            copies += load_slabs(
-                meta, sources, we, sems, k * SLAB, SLAB, half_d,
-                lambda h, k=k: h * half_f + k * half_d, len(copies)
-            )
-        base = half_f // half_d * SLAB
-        copies += load_slabs(
-            meta, sources, wo, sems, base, SLAB, half_d, lambda h: h * half_d, len(copies)
-        )
-        base += SLAB
-        copies += load_slabs(
-            meta, sources, ws, sems, base, ws.shape[0] // CHIPS, half_d,
-            lambda h: h * half_d, len(copies)
-        )
+        start_all(copies_wo() + copies_we() + copies_ws())
         gvec_ref[...] = jnp.zeros(gvec_ref.shape, F32)
         gbias_ref[...] = jnp.zeros(gbias_ref.shape, F32)
-        for c in copies:
-            c.wait()
+        wait_all(copies_wo())
 
     base = 3 + ws.shape[0] // wo.shape[0]
     bias_out = vec[2:3]
     bias_shrink, gain1, shift1, gain2, shift2 = (vec[base + i : base + i + 1] for i in range(5))
-    chunk = wo.shape[0] // 2
+    chunk = wo.shape[0]
     chunks = ws.shape[0] // chunk
 
     branch = dot(o_ref[...], wo[...]) + bias_out
@@ -515,19 +549,25 @@
     hidden = normed1 * gain1 + shift1
     hidden_low = hidden.astype(BF16)
     h1_ref[...] = hidden_low
+    pl.when(step == 0)(lambda: wait_all(copies_we()))
     z = None
     spans = [slice(c * chunk, (c + 1) * chunk) for c in range(chunks)]
     ahead = dot(hidden_low, we[:, spans[0]])
     for c, cols in enumerate(spans):
+        if c == 1:
+            pl.when(step == 0)(lambda: wait_all(copies_ws()))
         u = ahead + fbias[0:1, cols]
         if c + 1 < chunks:
             ahead = dot(hidden_low, we[:, spans[c + 1]])
-        phi = 0.5 + 0.5 * lax.erf(u * INV_SQRT2)
+        phi = 0.5 + 0.5 * erf(u * INV_SQRT2)
         gp_scr[:, cols] = phi + u * (jnp.exp(-0.5 * u * u) * INV_SQRT_2PI)
         gl = (u * phi).astype(BF16)
         gl_ref[:, cols] = gl
-        part = dot(gl, ws[cols, :])
-        z = part if c == 0 else z + part
+        if c == 0:
+            first = gl
+            continue
+        z = dot(first, ws[spans[0], :]) if c == 1 else z
+        z = z + dot(gl, ws[cols, :])
     normed2, inverse2 = norm(hidden + z + bias_shrink)
     out_ref[...] = (normed2 * gain2 + shift2).astype(BF16)
     cot = cot_ref[...].astype(F32)
@@ -536,15 +576,16 @@
     df2 = norm_back(cot, normed2, inverse2, gain2)
     dz = df2.astype(BF16)
     dz_ref[...] = dz
-    gvec_ref[3:4] += colsum(dz.astype(F32))
+    gvec_ref[3:4] += colsum(df2)
     dh = df2
     ahead = dot_nt(dz, ws[spans[0], :])
     for c, cols in enumerate(spans):
-        du = (ahead * gp_scr[:, cols]).astype(BF16)
+        du_wide = ahead * gp_scr[:, cols]
+        du = du_wide.astype(BF16)
         if c + 1 < chunks:
             ahead = dot_nt(dz, ws[spans[c + 1], :])
         du_ref[:, cols] = du
-        gbias_ref[0:1, cols] += colsum(du.astype(F32))
+        gbias_ref[0:1, cols] += colsum(du_wide)
         dh = dh + dot_nt(du, we[:, cols])
     gvec_ref[4:5] += colsum(dh * normed1)
     gvec_ref[5:6] += colsum(dh)
@@ -552,7 +593,7 @@
     df1_ref[...] = df1
     da = df1.astype(BF16)
     da_ref[...] = da
-    gvec_ref[2:3] += colsum(da.astype(F32))
+    gvec_ref[2:3] += colsum(df1)
     do_ref[...] = dot_nt(da, wo[...]).astype(BF16)
 
 
@@ -703,7 +744,7 @@
             scratch_shapes=[pltpu.VMEM((width, width), F32)],
         ),
         out_shape=[jax.ShapeDtypeStruct(lead + slab, dtype) for lead, dtype in outs],
-        compiler_params=params(1, True),
+        compiler_params=params(1),
         cost_estimate=cost(9 * tokens * width * width, 16 * tokens * width),
         name="feed_grad",
     )(meta, h1, du, gl, dz, ol, da, *((got,) if added else ()))
@@ -1007,27 +1048,28 @@
         joint_z = jnp.concatenate([joint_pair, swap(joint_pair, "dp", 2)])
         joint_z, rest_piece = stage(joint_z, rest_piece)
         shares = [share(teacher, segq, seg_row, 0, 2, (joint_z,))]
-        joint_y, joint_x, rest_got, tokens_y, shares[0] = stage(
+        joint_y, joint_x, rest_got, tokens_y, tokens_last, shares[0] = stage(
             swap(joint_z, "seq", 2),
             swap(joint_z, "dp", 1),
             swap(rest_piece, "dp", 4),
             tokens_y,
+            swap(after(tokens[lot:], joint_z), "seq", 2),
             shares[0],
         )
+        tokens_y = jnp.concatenate([tokens_y, tokens_last])
         rest_pair = jnp.stack([rest_piece, rest_got])
         shares.append(share(teacher, segq, seg_row, 2, 2, (joint_x, joint_y, shares[0])))
-        joint_xy, rest_got, tokens_last, tokens_core, core_z, core_y, core_x, shares[1] = stage(
+        joint_xy, rest_got, tokens_core, tokens_far, core_z, core_y, core_x, shares[1] = stage(
             swap(joint_y, "dp", 1),
             swap(rest_pair, "dp", 2),
-            swap(after(tokens[lot:], joint_y), "seq", 2),
             swap(tokens, "seq", 1),
+            swap(tokens_y, "seq", 1),
             swap(joint_z, "seq", 1),
             swap(joint_y, "seq", 1),
             swap(joint_x, "seq", 1),
             shares[1],
         )
-        tokens_y = jnp.concatenate([tokens_y, tokens_last])
-        core_xy, tokens_far = stage(swap(joint_xy, "seq", 1), swap(tokens_y, "seq", 1))
+        core_xy = swap(joint_xy, "seq", 1)
         got = {0: tokens, 1: tokens_core, 2: tokens_y, 3: tokens_far}
         joint_slabs = [joint_z, joint_y, joint_x, joint_xy, core_z, core_y, core_x, core_xy]
         rest_z = jnp.concatenate([rest_pair, rest_got])
@@ -1164,31 +1206,31 @@
     arrived = swap(sent, "seq", 1)
     own_grad = token_grad(meta, need, dk, dv, joint_w, (0,), (), (dq, d_first), F32, deps)[0]
     if by_slabs:
-        arrived, got_x, got_y, _ = stage(arrived, got_x, got_y, own_grad)
+        arrived, got_x, got_y, vector_got, _ = stage(arrived, got_x, got_y, vector_got, own_grad)
+        grad_vector = grad_vector + vector_got
     held = {0: own_grad[0] + arrived[0].astype(F32)}
     for i, d in enumerate(even):
         held[d] = (kept[i].astype(F32) + arrived[i + 1].astype(F32)).astype(BF16)
     if by_slabs:
         joint_near, over_x, over_y = add_first(joint_kept, got_x, got_y)
-        got_x, got_y, rest_got = stage(swap(over_x, "dp", 1), swap(over_y, "seq", 2), rest_got)
+        got_x, got_y, rest_got, vector_got, held[2] = stage(
+            swap(over_x, "dp", 1), swap(over_y, "seq", 2), rest_got, swap(grad_vector, "seq", 2),
+            held[2],
+        )
         joint_near, joint_far = add_second(joint_near, got_x, got_y)
-        joint_got = swap(joint_far, "dp", 2)
         rest_sum = rest_near + rest_got.astype(F32)
-        grad_vector = grad_vector + after(vector_got, joint_far)
-        vector_got = swap(grad_vector, "seq", 2)
-        held[2] = after(held[2], joint_far, vector_got)
+        grad_vector = grad_vector + vector_got
+        tokens_got = swap(held.pop(2), "seq", 2)
+        joint_got, vector_got = stage(swap(joint_far, "dp", 2), swap(grad_vector, "dp", 2))
+        joint_near, joint_far = add_z(joint_near, joint_got)
+        grad_vector = grad_vector + vector_got
+        joint_got, vector_got = stage(swap(joint_far, "dp", 4), swap(grad_vector, "dp", 4))
+        joint_sum = joint_near + joint_got.astype(F32)
+        vector_sum = grad_vector + vector_got
     for bit in bits[1:]:
         for d in [d for d in held if d & bit]:
             arrived = swap(held.pop(d).astype(BF16), "seq", bit).astype(F32)
             held[d ^ bit] = held[d ^ bit].astype(F32) + arrived
-    token_gradient = held[0].reshape(rows, length, width)
-    if by_slabs:
-        joint_near, joint_far = add_z(joint_near, joint_got)
-        joint_got = swap(joint_far, "dp", 4)
-        grad_vector = grad_vector + after(vector_got, joint_far)
-        grad_vector = grad_vector + swap(grad_vector, "dp", 2)
-        joint_sum = joint_near + joint_got.astype(F32)
-        vector_sum = grad_vector + swap(after(grad_vector, joint_sum), "dp", 4)
 
     cut = spare * SLAB
     if by_slabs:
@@ -1227,7 +1269,14 @@
         shard_output = rest_two[:, cut : cut + shard_rows].transpose(1, 0, 2)
         shard_output = shard_output.reshape(shard_rows, width)
         shard_shrink = rest_two[:, cut + shard_rows :].transpose(1, 0, 2).reshape(-1, width)
-        square_total = sum_all(local_squares.reshape(1, 1))[0, 0]
+        square_total = local_squares.reshape(1, 1)
+        for axis, bit in (("seq", 1), ("dp", 1), ("dp", 2)):
+            square_total = square_total + swap(square_total, axis, bit)
+        square_total, tokens_got = stage(square_total, tokens_got)
+        held[0] = held[0] + tokens_got.astype(F32)
+        for axis, bit in (("dp", 4), ("seq", 2)):
+            square_total = square_total + swap(square_total, axis, bit)
+        square_total = square_total[0, 0]
     else:
         rest_other = rest_theirs.astype(F32)
         grads = (
@@ -1247,6 +1296,7 @@
             for g in (shard_joint, shard_output, shard_expand, shard_shrink, shard_vector)
         )
         square_total = lax.psum(local_squares, ("dp", "seq"))
+    token_gradient = held[0].reshape(rows, length, width)
     gradient_norm = jnp.sqrt(square_total)
     clip_scale = CLIP_LEVEL / (gradient_norm + 1e-06)
     joint_master, joint_momentum, joint_variance = adam_step(

time: 476 us -> 475 us (level)
  Pallas kernels: 272 us -> 260 us
  other arithmetic: 33.3 us -> 42.8 us
  starting transfers between devices: 69.8 us -> 61.5 us
  waiting for transfers between devices: 52.7 us -> 57.8 us
    pallas_call x2, Pallas kernels: 44 us -> 34.2 us  [feed_grad(): pl.pallas_call(functools.partial(feed_grad_kernel, added), grid_spec=pltp...]
    ppermute x53, starting transfers between devices: 69.8 us -> 61.5 us  [swap(): lax.ppermute(x, axis, [(i, i ^ bit) for i in range(lax.axis_size(axis))])]
    pallas_call x2, Pallas kernels: 24.2 us -> 16.3 us  [share(): pl.pallas_call(skipping(functools.partial(share_kernel, start), 3, len(de...]
    ppermute x53, waiting for transfers between devices: 52.7 us -> 57.8 us  [swap(): lax.ppermute(x, axis, [(i, i ^ bit) for i in range(lax.axis_size(axis))])]
    unnamed x103 -> x133, local copies, waits for them, and re-layouts: 10.2 us -> 11 us
  transfers between devices with their start and end apart: 53 -> 53, of which waited for: 20 -> 18; matrix products, arithmetic and copies ran while one was open for 9% -> 10% of each run, Pallas kernels for 34% -> 34%
where the time goes in v2:
time: 475 us; the launch traced here: 466 us
  Pallas kernels  260 us (55%)
  starting transfers between devices  61.5 us (13%)
  waiting for transfers between devices  57.8 us (12%)
  other arithmetic  42.8 us (9%)
  local copies, waits for them, and re-layouts  34.9 us (7%)
  between operations  8.46 us (2%)
    pallas_call x4, Pallas kernels, attend_back(): pl.pallas_call(skipping(functools.partial(attend_back_kernel, blocks, sta...  65.2 us
    ppermute x53, starting transfers between devices, swap(): lax.ppermute(x, axis, [(i, i ^ bit) for i in range(lax.axis_size(axis))])  61.5 us
    ppermute x53, waiting for transfers between devices, swap(): lax.ppermute(x, axis, [(i, i ^ bit) for i in range(lax.axis_size(axis))])  57.8 us
    pallas_call x1, Pallas kernels, feed(): pl.pallas_call(feed_kernel, grid_spec=pltpu.PrefetchScalarGridSpec(num_sc...  50.2 us
    pallas_call x2, Pallas kernels, feed_grad(): pl.pallas_call(functools.partial(feed_grad_kernel, added), grid_spec=pltp...  34.2 us
    pallas_call x2, Pallas kernels, attend(): pl.pallas_call(skipping(functools.partial(attend_kernel, blocks, start),...  29.6 us
    pallas_call x2, Pallas kernels, token_grad(): pl.pallas_call(skipping(functools.partial(token_grad_kernel, steps, sent,...  23.9 us
    pallas_call x1, Pallas kernels, project(): pl.pallas_call(skipping(functools.partial(project_kernel, blocks, steps),...  21 us
  transfers between devices with their start and end apart: 53, of which 18 were waited for; matrix products, arithmetic and copies ran while one was open for 10% of the time, Pallas kernels for 34%

profile of v2, /device:TPU:0, one launch (start us, length us, event | category | flops | bytes accessed | tf_op | source)
XLA Modules:
  0.0 465.7 jit_solution(1866560477630159753)
XLA Ops:
  5.2 3.0 collective-permute-start.7
  13.3 2.6 collective-permute-start.1
  20.3 1.7 collective-permute-done.1
  23.1 5.9 %collective-permute-done.2 = bf16[2,48,1280]{2,1,0:T(8,128)(2,1)S(1)} collective-permute-done((bf16[2,48,1280]{2,1,0:T(8,128)(2,1)S(1)}, bf16[2,48,1280]{2,1,0:T(8,128)(2,1)S(1)}, u32[]{:S(2)}, u32[]{:S(2)}) %collective-permute-start.2) | collective-permute-done | bytes 245792 | tf_op jit(solution)/shard_map/ppermute | solution.py:60
  29.9 3.3 collective-permute-start.6
  34.1 1.6 collective-permute-start.5
  37.4 10.4 %collective-permute-done.6 = bf16[432,384]{1,0:T(8,128)(2,1)S(1)} collective-permute-done((bf16[432,384]{1,0:T(8,128)(2,1)S(1)}, bf16[432,384]{1,0:T(8,128)(2,1)S(1)}, u32[]{:S(2)}, u32[]{:S(2)}) %collective-permute-start.6) | collective-permute-done | bytes 331808 | tf_op jit(solution)/shard_map/ppermute | solution.py:60
  50.8 8.2 %share.2.refs_5_.refs_8_ = f32[2,6,256,128]{3,2,1,0:T(8,128)} custom-call(bf16[4,12,256,1024]{3,2,1,0:T(8,128)(2,1)} %refs_9_.7, s32[4,256,128]{2,1,0:T(8,128)} %broadcast_in_dim.62.refs_1_.refs_4_.refs_10_, s32[4,8,1024]{2,1,0:T(8,128)} %broadcast_in_dim.63.refs_2_, bf16[4,48,1280]{2,1,0:T(8,128)(2,1)} %pad_maximum_fusion.4.refs_3_.refs_6_), custom_call_target="tpu_custom_call" | custom-call | flops 25165824 | bytes 12582912 | tf_op jit(solution)/shard_map/share/pallas_call | solution.py:215
  62.6 1.5 collective-permute-start.9
  64.2 1.8 collective-permute-done.13.refs_10_
  67.6 8.2 %share.3.refs_15_.refs_8_ = f32[2,6,256,128]{3,2,1,0:T(8,128)} custom-call(bf16[4,12,256,1024]{3,2,1,0:T(8,128)(2,1)} %refs_9_.7, s32[4,256,128]{2,1,0:T(8,128)} %broadcast_in_dim.62.refs_1_.refs_4_.refs_10_, s32[4,8,1024]{2,1,0:T(8,128)} %broadcast_in_dim.63.refs_2_, bf16[4,48,1280]{2,1,0:T(8,128)(2,1)} %collective-permute-done.5.refs_3_.refs_8_, ...), custom_call_target="tpu_custom_call" | custom-call | flops 25165824 | bytes 12582912 | tf_op jit(solution)/shard_map/share/pallas_call | solution.py:215
  77.4 5.9 %collective-permute-done.10 = bf16[2,432,384]{2,1,0:T(8,128)(2,1)S(1)} collective-permute-done((bf16[2,432,384]{2,1,0:T(8,128)(2,1)S(1)}, bf16[2,432,384]{2,1,0:T(8,128)(2,1)S(1)}, u32[]{:S(2)}, u32[]{:S(2)}) %collective-permute-start.10) | collective-permute-done | bytes 663584 | tf_op jit(solution)/shard_map/ppermute | solution.py:60
  84.2 1.3 pad_maximum_fusion.refs_0_
  85.5 1.6 collective-permute-start.19
  87.1 1.5 collective-permute-start.17
  90.2 21.0 %project.1 = (bf16[1024,768]{1,0:T(8,128)(2,1)}, bf16[4,1024,768]{2,1,0:T(8,128)(2,1)}, bf16[4,1024,768]{2,1,0:T(8,128)(2,1)}, bf16[768,2304]{1,0:T(8,128)(2,1)}) custom-call(s32[23]{0:T(128)} %stack.146.refs_0_.meta, s32[4,4]{1,0:T(4,128)} %copy-done.48, bf16[1024,768]{1,0:T(8,128)(2,1)} %bitcast.267, bf16[1024,768]{1,0:T(8,128)(2,1)} %bitcast.47.refs_3_.refs_2_, ...), custom_call_target="tpu_custom_call" | custom-call | flops 10871635968 | bytes 12582912 | tf_op jit(solution)/shard_map/project/pallas_call | solution.py:166
  111.3 5.8 %collective-permute-done.19.refs_2_ = bf16[4,432,384]{2,1,0:T(8,128)(2,1)S(1)} collective-permute-done((bf16[4,432,384]{2,1,0:T(8,128)(2,1)S(1)}, bf16[4,432,384]{2,1,0:T(8,128)(2,1)S(1)}, u32[]{:S(2)}, u32[]{:S(2)}) %collective-permute-start.19) | collective-permute-done | bytes 1327136 | tf_op jit(solution)/shard_map/ppermute | solution.py:60
  118.4 1.3 slice.232
  120.8 1.5 collective-permute-start.20
  122.4 1.3 collective-permute-start.18
  125.0 13.5 %attend.2 = (bf16[4,256,768]{2,1,0:T(8,128)(2,1)}, f32[4,6,256,128]{3,2,1,0:T(8,128)}) custom-call(s32[4,5]{1,0:T(4,128)} %pad_add_fusion.refs_0_.refs_1_, bf16[4,256,768]{2,1,0:T(8,128)(2,1)} %bitcast.252, bf16[4,4,256,768]{3,2,1,0:T(8,128)(2,1)} %bitcast.237, bf16[4,4,256,768]{3,2,1,0:T(8,128)(2,1)} %bitcast.243, ...), custom_call_target="tpu_custom_call" | custom-call | flops 6442450944 | bytes 3145728 | tf_op jit(solution)/shard_map/attend/pallas_call | solution.py:324
  138.5 2.6 collective-permute-start.22
  144.2 16.1 %attend.3 = (bf16[4,256,768]{2,1,0:T(8,128)(2,1)}, f32[4,6,256,128]{3,2,1,0:T(8,128)}) custom-call(s32[4,5]{1,0:T(4,128)} %pad_add_fusion.refs_0_.refs_1_, bf16[4,256,768]{2,1,0:T(8,128)(2,1)} %bitcast.253, bf16[4,4,256,768]{3,2,1,0:T(8,128)(2,1)} %bitcast.238, bf16[4,4,256,768]{3,2,1,0:T(8,128)(2,1)} %bitcast.244, ...), custom_call_target="tpu_custom_call", output_to_operand_aliasing={{0}: (6, {}), {1}: (7, {})} | custom-call | flops 6442450944 | bytes 3145728 | tf_op jit(solution)/shard_map/attend/pallas_call | solution.py:324
  161.4 50.2 %feed.1 = (bf16[1024,768]{1,0:T(8,128)(2,1)}, f32[1024,768]{1,0:T(8,128)}, bf16[1024,768]{1,0:T(8,128)(2,1)}, bf16[1024,3072]{1,0:T(8,128)(2,1)}, bf16[1024,3072...) custom-call(s32[23]{0:T(128)} %stack.146.refs_0_.meta, ...), custom_call_target="tpu_custom_call" | custom-call | flops 21743271936 | bytes 28311552 | tf_op jit(solution)/shard_map/feed/pallas_call | solution.py:610
  211.6 15.6 %feed_grad.2.refs_12_ = bf16[2,2,4,432,384]{4,3,2,1,0:T(8,128)(2,1)} custom-call(s32[23]{0:T(128)} %copy-done.60, bf16[1024,768]{1,0:T(8,128)(2,1)} %get-tuple-element.150.h1_ref, bf16[1024,3072]{1,0:T(8,128)(2,1)} %get-tuple-element.151.du_ref, bf16[1024,3072]{1,0:T(8,128)(2,1)} %get-tuple-element.152.gl_ref, bf16[1024,768]{1,0:T(8,128)(2,1)} %get-tuple-element.153.dz_ref, ...), custom_call_target="tpu_custom_call" | custom-call | flops 5435817984 | bytes 12582912 | tf_op jit(solution)/shard_map/feed_grad/pallas_call | solution.py:729
  227.2 15.3 %attend_back.4 = (bf16[4,256,768]{2,1,0:T(8,128)(2,1)}, bf16[4,4,256,768]{3,2,1,0:T(8,128)(2,1)}, bf16[4,4,256,768]{3,2,1,0:T(8,128)(2,1)}) custom-call(s32[23]{0:T(128)} %stack.146.refs_0_.meta, s32[4,5]{1,0:T(4,128)} %pad_add_fusion.refs_0_.refs_1_, bf16[4,256,768]{2,1,0:T(8,128)(2,1)} %bitcast.254, bf16[4,4,256,768]{3,2,1,0:T(8,128)(2,1)} %bitcast.239, ...), custom_call_target="tpu_custom_call" | custom-call | flops 8053063680 | bytes 6291456 | tf_op jit(solution)/shard_map/attend_back/pallas_call | solution.py:425
  242.6 18.7 %feed_grad.3 = (f32[4,432,384]{2,1,0:T(8,128)}, f32[2,432,384]{2,1,0:T(8,128)}, f32[2,432,384]{2,1,0:T(8,128)}, bf16[2,2,432,384]{3,2,1,0:T(8,128)(2,1)}, bf16[2,2,432,384]{3,2,1,0:T(8,128)(2,1)}) custom-call(s32[23]{0:T(128)} %stack.146.refs_0_.meta, bf16[1024,768]{1,0:T(8,128)(2,1)} %get-tuple-element.150.h1_ref, ...), custom_call_target="tpu_custom_call" | custom-call | flops 5435817984 | bytes 12582912 | tf_op jit(solution)/shard_map/feed_grad/pallas_call | solution.py:729
  261.3 2.9 collective-permute-start.26
  264.1 2.3 collective-permute-start.27
  266.4 12.7 %attend_back.5 = (bf16[4,256,768]{2,1,0:T(8,128)(2,1)}, bf16[4,4,256,768]{3,2,1,0:T(8,128)(2,1)}, bf16[4,4,256,768]{3,2,1,0:T(8,128)(2,1)}) custom-call(s32[23]{0:T(128)} %stack.146.refs_0_.meta, s32[4,5]{1,0:T(4,128)} %pad_add_fusion.refs_0_.refs_1_, bf16[4,256,768]{2,1,0:T(8,128)(2,1)} %bitcast.255, ...), custom_call_target="tpu_custom_call", output_to_operand_aliasing={{0}: (12, {}), {1}: (13, {}), {2}: (14, {})} | custom-call | flops 8053063680 | bytes 6291456 | tf_op jit(solution)/shard_map/attend_back/pallas_call | solution.py:425
  279.2 18.6 %attend_back.6 = (bf16[4,256,768]{2,1,0:T(8,128)(2,1)}, bf16[4,4,256,768]{3,2,1,0:T(8,128)(2,1)}, bf16[4,4,256,768]{3,2,1,0:T(8,128)(2,1)}) custom-call(s32[23]{0:T(128)} %stack.146.refs_0_.meta, s32[4,5]{1,0:T(4,128)} %pad_add_fusion.refs_0_.refs_1_, bf16[4,256,768]{2,1,0:T(8,128)(2,1)} %bitcast.256, ...), custom_call_target="tpu_custom_call", output_to_operand_aliasing={{0}: (12, {}), {1}: (13, {}), {2}: (14, {})} | custom-call | flops 8053063680 | bytes 6291456 | tf_op jit(solution)/shard_map/attend_back/pallas_call | solution.py:425
  300.4 3.1 collective-permute-start.28
  303.8 1.3 copy-done.2
  305.2 3.0 collective-permute-start.29
  308.2 18.6 %attend_back.7 = (bf16[4,256,768]{2,1,0:T(8,128)(2,1)}, bf16[4,4,256,768]{3,2,1,0:T(8,128)(2,1)}, bf16[4,4,256,768]{3,2,1,0:T(8,128)(2,1)}) custom-call(s32[23]{0:T(128)} %stack.146.refs_0_.meta, s32[4,5]{1,0:T(4,128)} %pad_add_fusion.refs_0_.refs_1_, bf16[4,256,768]{2,1,0:T(8,128)(2,1)} %bitcast.257, ...), custom_call_target="tpu_custom_call", output_to_operand_aliasing={{0}: (12, {}), {1}: (13, {}), {2}: (14, {})} | custom-call | flops 8053063680 | bytes 6291456 | tf_op jit(solution)/shard_map/attend_back/pallas_call | solution.py:425
  326.8 2.8 fusion.4
  332.1 19.7 %joint_grad.1 = (f32[2,2,4,48,1152]{4,3,2,1,0:T(8,128)}, bf16[2,2,4,48,1152]{4,3,2,1,0:T(8,128)(2,1)}, f32[8,768]{1,0:T(8,128)}) custom-call(s32[23]{0:T(128)} %stack.146.refs_0_.meta, bf16[1024,768]{1,0:T(8,128)(2,1)} %bitcast.269, bf16[1024,768]{1,0:T(8,128)(2,1)} %bitcast.47.refs_3_.refs_2_, bf16[1024,768]{1,0:T(8,128)(2,1)} %bitcast.48.refs_4_.refs_3_, ...), custom_call_target="tpu_custom_call" | custom-call | flops 10871635968 | bytes 25165824 | tf_op jit(solution)/shard_map/joint_grad/pallas_call | solution.py:867
  351.8 1.9 collective-permute-start.31
  353.7 14.3 %token_grad.2 = (bf16[2,1024,768]{2,1,0:T(8,128)(2,1)}, bf16[1,1024,768]{2,1,0:T(8,128)(2,1)}) custom-call(s32[23]{0:T(128)} %stack.146.refs_0_.meta, s32[4,4]{1,0:T(4,128)} %copy-done.48, bf16[4,1024,768]{2,1,0:T(8,128)(2,1)} %bitcast.232, bf16[4,1024,768]{2,1,0:T(8,128)(2,1)} %bitcast.235, bf16[768,2304]{1,0:T(8,128)(2,1)} %get-tuple-element.173.refs_4_), custom_call_target="tpu_custom_call" | custom-call | flops 7247757312 | bytes 14155776 | tf_op jit(solution)/shard_map/token_grad/pallas_call | solution.py:800
  370.4 3.4 collective-permute-done.32
  375.2 3.0 fusion.47
  381.8 3.8 collective-permute-start.39
  385.6 9.6 %token_grad.3 = f32[1,1024,768]{2,1,0:T(8,128)} custom-call(s32[23]{0:T(128)} %stack.146.refs_0_.meta, s32[4,4]{1,0:T(4,128)} %copy-done.48, bf16[4,1024,768]{2,1,0:T(8,128)(2,1)} %bitcast.233, bf16[4,1024,768]{2,1,0:T(8,128)(2,1)} %bitcast.236, bf16[768,2304]{1,0:T(8,128)(2,1)} %get-tuple-element.173.refs_4_, bf16[1024,768]{1,0:T(8,128)(2,1)} %bitcast.263, ...), custom_call_target="tpu_custom_call" | custom-call | flops 2415919104 | bytes 4718592 | tf_op jit(solution)/shard_map/token_grad/pallas_call | solution.py:800
  396.4 1.2 convert_element_type.148
  397.7 2.1 collective-permute-start.38
  400.5 3.2 fusion
  404.4 1.5 collective-permute-done.37
  405.9 1.8 multiply_reduce_fusion
  408.0 2.1 collective-permute-start.42
  410.6 3.8 collective-permute-done.42
  414.8 2.6 collective-permute-start.43
  418.2 2.6 collective-permute-done.44
  426.9 1.9 bitcast_select_fusion.1
  429.4 2.0 collective-permute-start.46
  431.4 1.7 collective-permute-done.46
  433.6 1.4 collective-permute-start.47
  435.0 2.3 collective-permute-done.47
  437.9 1.6 bitcast_select_fusion.3
  439.5 4.6 collective-permute-done.48
  444.1 4.0 bitcast_add_fusion
  448.0 1.7 collective-permute-start.49
  449.8 2.7 collective-permute-done.49
  453.1 2.0 collective-permute-start.50
  455.1 1.6 collective-permute-done.50
  (326 shorter events, 67.1 us)
Async XLA Ops:
  3.6 13.8 %copy-start.19 = (f32[24,3072]{1,0:T(8,128)S(1)}, f32[24,3072]{1,0:T(8,128)}, u32[]{:S(2)}) copy-start(f32[24,3072]{1,0:T(8,128)} %param.28) | copy-start | bytes 884740
  3.6 8.4 %collective-permute-start = (bf16[24,1280]{1,0:T(8,128)(2,1)}, bf16[24,1280]{1,0:T(8,128)(2,1)S(1)}, u32[]{:S(2)}, u32[]{:S(2)}) collective-permute-start(bf16[24,1280]{1,0:T(8,128)(2,1)} %get-tuple-element.258), channel_id=1, source_target_pairs={{0,1},{1,0},{2,3},{3,2},{4,5},{5,4},{6,7},{7,6},{8,9},{9,8},{10,11... | collective-permute-start | bytes 184328 | tf_op jit(solution)/shard_map/ppermute | solution.py:60
  4.0 62.1 %collective-permute-start.11 = (bf16[4,256,768]{2,1,0:T(8,128)(2,1)S(1)}, bf16[4,256,768]{2,1,0:T(8,128)(2,1)}, u32[]{:S(2)}, u32[]{:S(2)}) collective-permute-start(bf16[4,256,768]{2,1,0:T(8,128)(2,1)S(1)} %copy-done.12), channel_id=1, source_target_pairs={{0,1},{1,0},{2,3},{3,2},{4,5},{5,4},{6,7},{7,6},{8,9},{9,8},{10,11... | collective-permute-start | bytes 4718600 | tf_op jit(solution)/shard_map/ppermute | solution.py:60
  5.2 13.9 %copy-start.21 = (f32[96,768]{1,0:T(8,128)S(1)}, f32[96,768]{1,0:T(8,128)}, u32[]{:S(2)}) copy-start(f32[96,768]{1,0:T(8,128)} %param.29) | copy-start | bytes 884740
  5.2 53.8 %collective-permute-start.7 = (bf16[3,256,768]{2,1,0:T(8,128)(2,1)}, bf16[3,256,768]{2,1,0:T(8,128)(2,1)S(1)}, u32[]{:S(2)}, u32[]{:S(2)}) collective-permute-start(bf16[3,256,768]{2,1,0:T(8,128)(2,1)} %slice.223), channel_id=1, source_target_pairs={{0,2},{1,3},{2,0},{3,1},{4,6},{5,7},{6,4},{7,5},{8,10},{9,11},{10,... | collective-permute-start | bytes 3538952 | tf_op jit(solution)/shard_map/ppermute | solution.py:60
  13.3 8.8 %collective-permute-start.1 = (bf16[48,1280]{1,0:T(8,128)(2,1)}, bf16[48,1280]{1,0:T(8,128)(2,1)S(1)}, u32[]{:S(2)}, u32[]{:S(2)}) collective-permute-start(bf16[48,1280]{1,0:T(8,128)(2,1)} %maximum_select_fusion.2), channel_id=1, source_target_pairs={{0,16},{4,20},{8,24},{12,28},{16,0},{20,4},{24,8},{28,12},{1,17},{... | collective-permute-start | bytes 368648 | tf_op jit(solution)/shard_map/ppermute | solution.py:60
  19.3 3.6 collective-permute-start.3
  22.1 7.0 %collective-permute-start.2 = (bf16[2,48,1280]{2,1,0:T(8,128)(2,1)S(1)}, bf16[2,48,1280]{2,1,0:T(8,128)(2,1)S(1)}, u32[]{:S(2)}, u32[]{:S(2)}) collective-permute-start(bf16[2,48,1280]{2,1,0:T(8,128)(2,1)S(1)} %pad_maximum_fusion.10), channel_id=1, source_target_pairs={{0,8},{4,12},{8,0},{12,4},{16,24},{20,28},{24,16},{28,20},{1,9},{5... | collective-permute-start | bytes 737288 | tf_op jit(solution)/shard_map/ppermute | solution.py:60
  22.9 13.2 %copy-start.54 = (s32[4,4,1]{1,0,2:T(4,128)S(1)}, s32[4,4,1]{1,0,2:T(4,128)}, u32[]{:S(2)}) copy-start(s32[4,4,1]{1,0,2:T(4,128)} %copy.106) | copy-start | bytes 196
  22.9 13.2 %copy-start.55 = (s32[4,4,1]{1,0,2:T(4,128)S(1)}, s32[4,4,1]{1,0,2:T(4,128)}, u32[]{:S(2)}) copy-start(s32[4,4,1]{1,0,2:T(4,128)} %copy.107) | copy-start | bytes 196
  29.9 17.8 %collective-permute-start.6 = (bf16[432,384]{1,0:T(8,128)(2,1)S(1)}, bf16[432,384]{1,0:T(8,128)(2,1)S(1)}, u32[]{:S(2)}, u32[]{:S(2)}) collective-permute-start(bf16[432,384]{1,0:T(8,128)(2,1)S(1)} %pad_maximum_fusion.8), channel_id=1, source_target_pairs={{0,16},{4,20},{8,24},{12,28},{16,0},{20,4},{24,8},{28,12},{1,17},{... | collective-permute-start | bytes 995336 | tf_op jit(solution)/shard_map/ppermute | solution.py:60
  34.1 24.9 %collective-permute-start.5 = (bf16[4,48,1280]{2,1,0:T(8,128)(2,1)}, bf16[4,48,1280]{2,1,0:T(8,128)(2,1)}, u32[]{:S(2)}, u32[]{:S(2)}) collective-permute-start(bf16[4,48,1280]{2,1,0:T(8,128)(2,1)} %pad_maximum_fusion.4.refs_3_.refs_6_), channel_id=1, source_target_pairs={{0,4},{4,0},{8,12},{12,8},{16,20},{20,16},{24,28},{28,24},{1,5},{5... | collective-permute-start | bytes 1474568 | tf_op jit(solution)/shard_map/ppermute | solution.py:60
  35.6 23.3 %collective-permute-start.4 = (bf16[4,48,1280]{2,1,0:T(8,128)(2,1)}, bf16[4,48,1280]{2,1,0:T(8,128)(2,1)}, u32[]{:S(2)}, u32[]{:S(2)}) collective-permute-start(bf16[4,48,1280]{2,1,0:T(8,128)(2,1)} %pad_maximum_fusion.4.refs_3_.refs_6_), channel_id=1, source_target_pairs={{0,2},{1,3},{2,0},{3,1},{4,6},{5,7},{6,4},{7,5},{8,10},{9,11},{10,... | collective-permute-start | bytes 1474568 | tf_op jit(solution)/shard_map/ppermute | solution.py:60
  36.2 24.7 %copy-start.48 = (s32[4,4]{1,0:T(4,128)}, s32[4,4]{1,0:T(4,128)S(1)}, u32[]{:S(2)}) copy-start(s32[4,4]{1,0:T(4,128)S(1)} %get-tuple-element.230.refs_1_) | copy-start | bytes 196
  47.7 11.2 %collective-permute-start.8 = (bf16[1,256,768]{2,1,0:T(8,128)(2,1)}, bf16[1,256,768]{2,1,0:T(8,128)(2,1)S(1)}, u32[]{:S(2)}, u32[]{:S(2)}) collective-permute-start(bf16[1,256,768]{2,1,0:T(8,128)(2,1)} %slice.224), channel_id=1, source_target_pairs={{0,2},{1,3},{2,0},{3,1},{4,6},{5,7},{6,4},{7,5},{8,10},{9,11},{10,... | collective-permute-start | bytes 1179656 | tf_op jit(solution)/shard_map/ppermute | solution.py:60
  60.8 22.5 %collective-permute-start.12 = (bf16[4,256,768]{2,1,0:T(8,128)(2,1)}, bf16[4,256,768]{2,1,0:T(8,128)(2,1)}, u32[]{:S(2)}, u32[]{:S(2)}) collective-permute-start(bf16[4,256,768]{2,1,0:T(8,128)(2,1)} %constant_dynamic-update-slice_fusion), channel_id=1, source_target_pairs={{0,1},{1,0},{2,3},{3,2},{4,5},{5,4},{6,7},{7,6},{8,9},{9,8},{10,11... | collective-permute-start | bytes 4718600 | tf_op jit(solution)/shard_map/ppermute | solution.py:60
  60.9 5.1 %collective-permute-start.13 = (bf16[4,48,1280]{2,1,0:T(8,128)(2,1)}, bf16[4,48,1280]{2,1,0:T(8,128)(2,1)}, u32[]{:S(2)}, u32[]{:S(2)}) collective-permute-start(bf16[4,48,1280]{2,1,0:T(8,128)(2,1)} %pad_maximum_fusion.4.refs_3_.refs_6_), channel_id=1, source_target_pairs={{0,1},{1,0},{2,3},{3,2},{4,5},{5,4},{6,7},{7,6},{8,9},{9,8},{10,11... | collective-permute-start | bytes 1474568 | tf_op jit(solution)/shard_map/ppermute | solution.py:60
  62.6 14.8 %collective-permute-start.14 = (bf16[4,48,1280]{2,1,0:T(8,128)(2,1)}, bf16[4,48,1280]{2,1,0:T(8,128)(2,1)S(1)}, u32[]{:S(2)}, u32[]{:S(2)}) collective-permute-start(bf16[4,48,1280]{2,1,0:T(8,128)(2,1)} %collective-permute-done.4.refs_4_.refs_7_), channel_id=1, source_target_pairs={{0,1},{1,0},{2,3},{3,2},{4,5},{5,4},{6,7},{7,6},{8,9},{9,8},{10,11... | collective-permute-start | bytes 1474568 | tf_op jit(solution)/shard_map/ppermute | solution.py:60
  62.6 14.8 %collective-permute-start.9 = (bf16[4,48,1280]{2,1,0:T(8,128)(2,1)}, bf16[4,48,1280]{2,1,0:T(8,128)(2,1)}, u32[]{:S(2)}, u32[]{:S(2)}) collective-permute-start(bf16[4,48,1280]{2,1,0:T(8,128)(2,1)} %collective-permute-done.4.refs_4_.refs_7_), channel_id=1, source_target_pairs={{0,4},{4,0},{8,12},{12,8},{16,20},{20,16},{24,28},{28,24},{1,5},{5... | collective-permute-start | bytes 1474568 | tf_op jit(solution)/shard_map/ppermute | solution.py:60
  66.0 11.4 %collective-permute-start.15 = (bf16[4,48,1280]{2,1,0:T(8,128)(2,1)}, bf16[4,48,1280]{2,1,0:T(8,128)(2,1)}, u32[]{:S(2)}, u32[]{:S(2)}) collective-permute-start(bf16[4,48,1280]{2,1,0:T(8,128)(2,1)} %collective-permute-done.5.refs_3_.refs_8_), channel_id=1, source_target_pairs={{0,1},{1,0},{2,3},{3,2},{4,5},{5,4},{6,7},{7,6},{8,9},{9,8},{10,11... | collective-permute-start | bytes 1474568 | tf_op jit(solution)/shard_map/ppermute | solution.py:60
  66.1 17.2 %collective-permute-start.10 = (bf16[2,432,384]{2,1,0:T(8,128)(2,1)S(1)}, bf16[2,432,384]{2,1,0:T(8,128)(2,1)S(1)}, u32[]{:S(2)}, u32[]{:S(2)}) collective-permute-start(bf16[2,432,384]{2,1,0:T(8,128)(2,1)S(1)} %pad_maximum_fusion.1), channel_id=1, source_target_pairs={{0,8},{4,12},{8,0},{12,4},{16,24},{20,28},{24,16},{28,20},{1,9},{5... | collective-permute-start | bytes 1990664 | tf_op jit(solution)/shard_map/ppermute | solution.py:60
  77.4 11.2 %copy-start.64 = (bf16[4,48,1280]{2,1,0:T(8,128)(2,1)}, bf16[4,48,1280]{2,1,0:T(8,128)(2,1)S(1)}, u32[]{:S(2)}) copy-start(bf16[4,48,1280]{2,1,0:T(8,128)(2,1)S(1)} %collective-permute-done.14.refs_11_) | copy-start | bytes 1474564
  84.2 6.1 %collective-permute-start.16 = (bf16[4,48,1280]{2,1,0:T(8,128)(2,1)}, bf16[4,48,1280]{2,1,0:T(8,128)(2,1)}, u32[]{:S(2)}, u32[]{:S(2)}) collective-permute-start(bf16[4,48,1280]{2,1,0:T(8,128)(2,1)} %collective-permute-done.9.refs_9_), channel_id=1, source_target_pairs={{0,1},{1,0},{2,3},{3,2},{4,5},{5,4},{6,7},{7,6},{8,9},{9,8},{10,11... | collective-permute-start | bytes 1474568 | tf_op jit(solution)/shard_map/ppermute | solution.py:60
  85.5 38.8 %copy-start.16 = (bf16[4,432,384]{2,1,0:T(8,128)(2,1)}, bf16[4,432,384]{2,1,0:T(8,128)(2,1)S(1)}, u32[]{:S(2)}) copy-start(bf16[4,432,384]{2,1,0:T(8,128)(2,1)S(1)} %pad_maximum_fusion.refs_0_) | copy-start | bytes 3981316
  85.5 31.6 %collective-permute-start.19 = (bf16[4,432,384]{2,1,0:T(8,128)(2,1)S(1)}, bf16[4,432,384]{2,1,0:T(8,128)(2,1)S(1)}, u32[]{:S(2)}, u32[]{:S(2)}) collective-permute-start(bf16[4,432,384]{2,1,0:T(8,128)(2,1)S(1)} %pad_maximum_fusion.refs_0_), channel_id=1, source_target_pairs={{0,4},{4,0},{8,12},{12,8},{16,20},{20,16},{24,28},{28,24},{1,5},{5... | collective-permute-start | bytes 3981320 | tf_op jit(solution)/shard_map/ppermute | solution.py:60
  87.1 31.4 %collective-permute-start.17 = (bf16[4,432,384]{2,1,0:T(8,128)(2,1)S(1)}, bf16[4,432,384]{2,1,0:T(8,128)(2,1)}, u32[]{:S(2)}, u32[]{:S(2)}) collective-permute-start(bf16[4,432,384]{2,1,0:T(8,128)(2,1)S(1)} %pad_maximum_fusion.refs_0_), channel_id=1, source_target_pairs={{0,2},{1,3},{2,0},{3,1},{4,6},{5,7},{6,4},{7,5},{8,10},{9,11},{10,... | collective-permute-start | bytes 3981320 | tf_op jit(solution)/shard_map/ppermute | solution.py:60
  120.8 20.3 %collective-permute-start.20 = (bf16[2,432,384]{2,1,0:T(8,128)(2,1)}, bf16[2,432,384]{2,1,0:T(8,128)(2,1)S(1)}, u32[]{:S(2)}, u32[]{:S(2)}) collective-permute-start(bf16[2,432,384]{2,1,0:T(8,128)(2,1)} %slice.233), channel_id=1, source_target_pairs={{0,2},{1,3},{2,0},{3,1},{4,6},{5,7},{6,4},{7,5},{8,10},{9,11},{10,... | collective-permute-start | bytes 1990664 | tf_op jit(solution)/shard_map/ppermute | solution.py:60
  122.4 18.8 %collective-permute-start.18 = (bf16[2,432,384]{2,1,0:T(8,128)(2,1)S(1)}, bf16[2,432,384]{2,1,0:T(8,128)(2,1)S(1)}, u32[]{:S(2)}, u32[]{:S(2)}) collective-permute-start(bf16[2,432,384]{2,1,0:T(8,128)(2,1)S(1)} %slice.232), channel_id=1, source_target_pairs={{0,4},{4,0},{8,12},{12,8},{16,20},{20,16},{24,28},{28,24},{1,5},{5... | collective-permute-start | bytes 1990664 | tf_op jit(solution)/shard_map/ppermute | solution.py:60
  124.3 36.0 %collective-permute-start.21 = (bf16[4,432,384]{2,1,0:T(8,128)(2,1)S(1)}, bf16[4,432,384]{2,1,0:T(8,128)(2,1)}, u32[]{:S(2)}, u32[]{:S(2)}) collective-permute-start(bf16[4,432,384]{2,1,0:T(8,128)(2,1)S(1)} %pad_maximum_fusion.refs_0_), channel_id=1, source_target_pairs={{0,1},{1,0},{2,3},{3,2},{4,5},{5,4},{6,7},{7,6},{8,9},{9,8},{10,11... | collective-permute-start | bytes 3981320 | tf_op jit(solution)/shard_map/ppermute | solution.py:60
  138.5 21.8 %collective-permute-start.22 = (bf16[4,432,384]{2,1,0:T(8,128)(2,1)}, bf16[4,432,384]{2,1,0:T(8,128)(2,1)}, u32[]{:S(2)}, u32[]{:S(2)}) collective-permute-start(bf16[4,432,384]{2,1,0:T(8,128)(2,1)} %collective-permute-done.17.refs_1_), channel_id=1, source_target_pairs={{0,1},{1,0},{2,3},{3,2},{4,5},{5,4},{6,7},{7,6},{8,9},{9,8},{10,11... | collective-permute-start | bytes 3981320 | tf_op jit(solution)/shard_map/ppermute | solution.py:60
  141.1 19.2 %collective-permute-start.23 = (bf16[4,432,384]{2,1,0:T(8,128)(2,1)}, bf16[4,432,384]{2,1,0:T(8,128)(2,1)}, u32[]{:S(2)}, u32[]{:S(2)}) collective-permute-start(bf16[4,432,384]{2,1,0:T(8,128)(2,1)} %copy-done.32), channel_id=1, source_target_pairs={{0,1},{1,0},{2,3},{3,2},{4,5},{5,4},{6,7},{7,6},{8,9},{9,8},{10,11... | collective-permute-start | bytes 3981320 | tf_op jit(solution)/shard_map/ppermute | solution.py:60
  143.1 17.2 %collective-permute-start.24 = (bf16[4,432,384]{2,1,0:T(8,128)(2,1)}, bf16[4,432,384]{2,1,0:T(8,128)(2,1)S(1)}, u32[]{:S(2)}, u32[]{:S(2)}) collective-permute-start(bf16[4,432,384]{2,1,0:T(8,128)(2,1)} %constant_dynamic-update-slice_fusion.2.refs_8_.refs_3_), channel_id=1, source_target_pairs={{0,1},{1,0},{2,3},{3,2},{4,5},{5,4},{6,7},{7,6},{8,9},{9,8},{10,11... | collective-permute-start | bytes 3981320 | tf_op jit(solution)/shard_map/ppermute | solution.py:60
  143.5 16.7 %copy-start.60 = (s32[23]{0:T(128)}, s32[23]{0:T(128)S(1)}, u32[]{:S(2)}) copy-start(s32[23]{0:T(128)S(1)} %constant_dynamic-update-slice_fusion.4.meta) | copy-start | bytes 280
  227.1 15.5 %collective-permute-start.25 = (bf16[2,2,4,432,384]{4,3,2,1,0:T(8,128)(2,1)}, bf16[2,2,4,432,384]{4,3,2,1,0:T(8,128)(2,1)}, u32[]{:S(2)}, u32[]{:S(2)}) collective-permute-start(bf16[2,2,4,432,384]{4,3,2,1,0:T(8,128)(2,1)} %feed_grad.2.refs_12_), channel_id=1, source_target_pairs={{0,1},{1,0},{2,3},{3,2},{4,5},{5,4},{6,7},{7,6},{8,9},{9,8},{10,11... | collective-permute-start | bytes 15925256 | tf_op jit(solution)/shard_map/ppermute | solution.py:60
  261.3 36.5 %collective-permute-start.26 = (bf16[2,2,432,384]{3,2,1,0:T(8,128)(2,1)}, bf16[2,2,432,384]{3,2,1,0:T(8,128)(2,1)S(1)}, u32[]{:S(2)}, u32[]{:S(2)}) collective-permute-start(bf16[2,2,432,384]{3,2,1,0:T(8,128)(2,1)} %get-tuple-element.159.refs_15_), channel_id=1, source_target_pairs={{0,4},{4,0},{8,12},{12,8},{16,20},{20,16},{24,28},{28,24},{1,5},{5... | collective-permute-start | bytes 3981320 | tf_op jit(solution)/shard_map/ppermute | solution.py:60
  264.1 33.6 %collective-permute-start.27 = (bf16[2,2,432,384]{3,2,1,0:T(8,128)(2,1)}, bf16[2,2,432,384]{3,2,1,0:T(8,128)(2,1)S(1)}, u32[]{:S(2)}, u32[]{:S(2)}) collective-permute-start(bf16[2,2,432,384]{3,2,1,0:T(8,128)(2,1)} %get-tuple-element.160.refs_16_), channel_id=1, source_target_pairs={{0,2},{1,3},{2,0},{3,1},{4,6},{5,7},{6,4},{7,5},{8,10},{9,11},{10,... | collective-permute-start | bytes 3981320 | tf_op jit(solution)/shard_map/ppermute | solution.py:60
  300.4 26.4 %collective-permute-start.28 = (bf16[2,432,384]{2,1,0:T(8,128)(2,1)S(1)}, bf16[2,432,384]{2,1,0:T(8,128)(2,1)}, u32[]{:S(2)}, u32[]{:S(2)}) collective-permute-start(bf16[2,432,384]{2,1,0:T(8,128)(2,1)S(1)} %fusion.8.refs_15_), channel_id=1, source_target_pairs={{0,4},{4,0},{8,12},{12,8},{16,20},{20,16},{24,28},{28,24},{1,5},{5... | collective-permute-start | bytes 1990664 | tf_op jit(solution)/shard_map/ppermute | solution.py:60
  305.2 21.6 %collective-permute-start.29 = (bf16[2,432,384]{2,1,0:T(8,128)(2,1)S(1)}, bf16[2,432,384]{2,1,0:T(8,128)(2,1)}, u32[]{:S(2)}, u32[]{:S(2)}) collective-permute-start(bf16[2,432,384]{2,1,0:T(8,128)(2,1)S(1)} %fusion.6.refs_16_), channel_id=1, source_target_pairs={{0,2},{1,3},{2,0},{3,1},{4,6},{5,7},{6,4},{7,5},{8,10},{9,11},{10,... | collective-permute-start | bytes 1990664 | tf_op jit(solution)/shard_map/ppermute | solution.py:60
  332.1 21.6 %copy-start.28 = (bf16[2,432,384]{2,1,0:T(8,128)(2,1)S(1)}, bf16[2,432,384]{2,1,0:T(8,128)(2,1)}, u32[]{:S(2)}) copy-start(bf16[2,432,384]{2,1,0:T(8,128)(2,1)} %pad_maximum_fusion.2.refs_8_) | copy-start | bytes 1990660
  351.8 22.0 %collective-permute-start.31 = (bf16[2,2,4,48,1152]{4,3,2,1,0:T(8,128)(2,1)}, bf16[2,2,4,48,1152]{4,3,2,1,0:T(8,128)(2,1)S(1)}, u32[]{:S(2)}, u32[]{:S(2)}) collective-permute-start(bf16[2,2,4,48,1152]{4,3,2,1,0:T(8,128)(2,1)} %get-tuple-element.180), channel_id=1, source_target_pairs={{0,1},{1,0},{2,3},{3,2},{4,5},{5,4},{6,7},{7,6},{8,9},{9,8},{10,11... | collective-permute-start | bytes 5308424 | tf_op jit(solution)/shard_map/ppermute | solution.py:60
  353.7 20.1 %collective-permute-start.30 = (bf16[2,432,384]{2,1,0:T(8,128)(2,1)S(1)}, bf16[2,432,384]{2,1,0:T(8,128)(2,1)S(1)}, u32[]{:S(2)}, u32[]{:S(2)}) collective-permute-start(bf16[2,432,384]{2,1,0:T(8,128)(2,1)S(1)} %copy-done.28), channel_id=1, source_target_pairs={{0,8},{4,12},{8,0},{12,4},{16,24},{20,28},{24,16},{28,20},{1,9},{5... | collective-permute-start | bytes 1990664 | tf_op jit(solution)/shard_map/ppermute | solution.py:60
  353.7 14.3 %copy-start.50 = (f32[8,768]{1,0:T(8,128)S(1)}, f32[8,768]{1,0:T(8,128)}, u32[]{:S(2)}) copy-start(f32[8,768]{1,0:T(8,128)} %get-tuple-element.182) | copy-start | bytes 73732
  368.0 27.2 %collective-permute-start.33 = (bf16[2,1024,768]{2,1,0:T(8,128)(2,1)}, bf16[2,1024,768]{2,1,0:T(8,128)(2,1)}, u32[]{:S(2)}, u32[]{:S(2)}) collective-permute-start(bf16[2,1024,768]{2,1,0:T(8,128)(2,1)} %get-tuple-element.184), channel_id=1, source_target_pairs={{0,1},{1,0},{2,3},{3,2},{4,5},{5,4},{6,7},{7,6},{8,9},{9,8},{10,11... | collective-permute-start | bytes 9437192 | tf_op jit(solution)/shard_map/ppermute | solution.py:60
  369.8 4.0 collective-permute-start.32
  373.8 21.4 %collective-permute-start.36 = (f32[12,768]{1,0:T(8,128)S(1)}, f32[12,768]{1,0:T(8,128)S(1)}, u32[]{:S(2)}, u32[]{:S(2)}) collective-permute-start(f32[12,768]{1,0:T(8,128)S(1)} %fusion.39), channel_id=1, source_target_pairs={{0,4},{4,0},{8,12},{12,8},{16,20},{20,16},{24,28},{28,24},{1,5},{5... | collective-permute-start | bytes 110600 | tf_op jit(solution)/shard_map/ppermute | solution.py:60
  378.4 16.8 %collective-permute-start.34 = (bf16[2,2,48,1152]{3,2,1,0:T(8,128)(2,1)S(1)}, bf16[2,2,48,1152]{3,2,1,0:T(8,128)(2,1)}, u32[]{:S(2)}, u32[]{:S(2)}) collective-permute-start(bf16[2,2,48,1152]{3,2,1,0:T(8,128)(2,1)S(1)} %pad_maximum_fusion.5.refs_7_), channel_id=1, source_target_pairs={{0,4},{4,0},{8,12},{12,8},{16,20},{20,16},{24,28},{28,24},{1,5},{5... | collective-permute-start | bytes 1327112 | tf_op jit(solution)/shard_map/ppermute | solution.py:60
  379.9 15.2 %collective-permute-start.35 = (bf16[2,2,48,1152]{3,2,1,0:T(8,128)(2,1)}, bf16[2,2,48,1152]{3,2,1,0:T(8,128)(2,1)}, u32[]{:S(2)}, u32[]{:S(2)}) collective-permute-start(bf16[2,2,48,1152]{3,2,1,0:T(8,128)(2,1)} %pad_maximum_fusion.6.refs_8_), channel_id=1, source_target_pairs={{0,2},{1,3},{2,0},{3,1},{4,6},{5,7},{6,4},{7,5},{8,10},{9,11},{10,... | collective-permute-start | bytes 1327112 | tf_op jit(solution)/shard_map/ppermute | solution.py:60
  381.8 21.8 %collective-permute-start.39 = (bf16[432,384]{1,0:T(8,128)(2,1)}, bf16[432,384]{1,0:T(8,128)(2,1)}, u32[]{:S(2)}, u32[]{:S(2)}) collective-permute-start(bf16[432,384]{1,0:T(8,128)(2,1)} %fusion.20), channel_id=1, source_target_pairs={{0,16},{4,20},{8,24},{12,28},{16,0},{20,4},{24,8},{28,12},{1,17},{... | collective-permute-start | bytes 995336 | tf_op jit(solution)/shard_map/ppermute | solution.py:60
  395.2 8.4 %collective-permute-start.40 = (f32[12,768]{1,0:T(8,128)S(1)}, f32[12,768]{1,0:T(8,128)S(1)}, u32[]{:S(2)}, u32[]{:S(2)}) collective-permute-start(f32[12,768]{1,0:T(8,128)S(1)} %add.427), channel_id=1, source_target_pairs={{0,2},{1,3},{2,0},{3,1},{4,6},{5,7},{6,4},{7,5},{8,10},{9,11},{10,... | collective-permute-start | bytes 110600 | tf_op jit(solution)/shard_map/ppermute | solution.py:60
  397.7 6.7 %collective-permute-start.38 = (bf16[2,48,1152]{2,1,0:T(8,128)(2,1)S(1)}, bf16[2,48,1152]{2,1,0:T(8,128)(2,1)S(1)}, u32[]{:S(2)}, u32[]{:S(2)}) collective-permute-start(bf16[2,48,1152]{2,1,0:T(8,128)(2,1)S(1)} %get-tuple-element.233), channel_id=1, source_target_pairs={{0,2},{1,3},{2,0},{3,1},{4,6},{5,7},{6,4},{7,5},{8,10},{9,11},{10,... | collective-permute-start | bytes 663560 | tf_op jit(solution)/shard_map/ppermute | solution.py:60
  399.8 6.1 %collective-permute-start.37 = (bf16[2,48,1152]{2,1,0:T(8,128)(2,1)S(1)}, bf16[2,48,1152]{2,1,0:T(8,128)(2,1)S(1)}, u32[]{:S(2)}, u32[]{:S(2)}) collective-permute-start(bf16[2,48,1152]{2,1,0:T(8,128)(2,1)S(1)} %get-tuple-element.234), channel_id=1, source_target_pairs={{0,4},{4,0},{8,12},{12,8},{16,20},{20,16},{24,28},{28,24},{1,5},{5... | collective-permute-start | bytes 663560 | tf_op jit(solution)/shard_map/ppermute | solution.py:60
  407.9 6.5 %collective-permute-start.41 = (bf16[2,48,1152]{2,1,0:T(8,128)(2,1)S(1)}, bf16[2,48,1152]{2,1,0:T(8,128)(2,1)S(1)}, u32[]{:S(2)}, u32[]{:S(2)}) collective-permute-start(bf16[2,48,1152]{2,1,0:T(8,128)(2,1)S(1)} %pad_maximum_fusion.11), channel_id=1, source_target_pairs={{0,8},{4,12},{8,0},{12,4},{16,24},{20,28},{24,16},{28,20},{1,9},{5... | collective-permute-start | bytes 663560 | tf_op jit(solution)/shard_map/ppermute | solution.py:60
  408.0 6.4 %collective-permute-start.42 = (f32[12,768]{1,0:T(8,128)S(1)}, f32[12,768]{1,0:T(8,128)S(1)}, u32[]{:S(2)}, u32[]{:S(2)}) collective-permute-start(f32[12,768]{1,0:T(8,128)S(1)} %add.434), channel_id=1, source_target_pairs={{0,8},{4,12},{8,0},{12,4},{16,24},{20,28},{24,16},{28,20},{1,9},{5... | collective-permute-start | bytes 110600 | tf_op jit(solution)/shard_map/ppermute | solution.py:60
  410.1 34.0 %collective-permute-start.48 = (bf16[1024,768]{1,0:T(8,128)(2,1)}, bf16[1024,768]{1,0:T(8,128)(2,1)}, u32[]{:S(2)}, u32[]{:S(2)}) collective-permute-start(bf16[1024,768]{1,0:T(8,128)(2,1)} %fusion), channel_id=1, source_target_pairs={{0,2},{1,3},{2,0},{3,1},{4,6},{5,7},{6,4},{7,5},{8,10},{9,11},{10,... | collective-permute-start | bytes 4718600 | tf_op jit(solution)/shard_map/ppermute | solution.py:60
  414.5 29.6 %copy-start.1 = (f32[1,1024,768]{2,1,0:T(8,128)S(1)}, f32[1,1024,768]{2,1,0:T(8,128)}, u32[]{:S(2)}) copy-start(f32[1,1024,768]{2,1,0:T(8,128)} %token_grad.3) | copy-start | bytes 9437188
  414.5 6.4 %collective-permute-start.44 = (f32[12,768]{1,0:T(8,128)S(1)}, f32[12,768]{1,0:T(8,128)S(1)}, u32[]{:S(2)}, u32[]{:S(2)}) collective-permute-start(f32[12,768]{1,0:T(8,128)S(1)} %add.438), channel_id=1, source_target_pairs={{0,16},{4,20},{8,24},{12,28},{16,0},{20,4},{24,8},{28,12},{1,17},{... | collective-permute-start | bytes 110600 | tf_op jit(solution)/shard_map/ppermute | solution.py:60
  414.8 7.2 %collective-permute-start.43 = (bf16[48,1152]{1,0:T(8,128)(2,1)S(1)}, bf16[48,1152]{1,0:T(8,128)(2,1)S(1)}, u32[]{:S(2)}, u32[]{:S(2)}) collective-permute-start(bf16[48,1152]{1,0:T(8,128)(2,1)S(1)} %fusion.29), channel_id=1, source_target_pairs={{0,16},{4,20},{8,24},{12,28},{16,0},{20,4},{24,8},{28,12},{1,17},{... | collective-permute-start | bytes 331784 | tf_op jit(solution)/shard_map/ppermute | solution.py:60
  418.2 8.7 %collective-permute-start.52 = (f32[216,384]{1,0:T(8,128)}, f32[216,384]{1,0:T(8,128)}, u32[]{:S(2)}, u32[]{:S(2)}) collective-permute-start(f32[216,384]{1,0:T(8,128)} %dynamic-slice_bitcast_fusion), channel_id=1, source_target_pairs={{0,1},{1,0},{2,3},{3,2},{4,5},{5,4},{6,7},{7,6},{8,9},{9,8},{10,11... | collective-permute-start | bytes 995336 | tf_op jit(solution)/shard_map/ppermute | solution.py:60
  425.3 3.5 collective-permute-start.45
  426.4 11.5 %collective-permute-start.51 = (f32[24,1152]{1,0:T(8,128)S(1)}, f32[24,1152]{1,0:T(8,128)S(1)}, u32[]{:S(2)}, u32[]{:S(2)}) collective-permute-start(f32[24,1152]{1,0:T(8,128)S(1)} %dynamic-slice_bitcast_fusion.2), channel_id=1, source_target_pairs={{0,1},{1,0},{2,3},{3,2},{4,5},{5,4},{6,7},{7,6},{8,9},{9,8},{10,11... | collective-permute-start | bytes 331784 | tf_op jit(solution)/shard_map/ppermute | solution.py:60
  429.4 3.7 collective-permute-start.46
  433.6 3.7 collective-permute-start.47
  448.0 4.4 collective-permute-start.49
  453.1 3.6 collective-permute-start.50
  (54 other events, 161.4 us)
